TPU v7x, 32 devices: a whole 2x2x4 slice. The times are simulated.
32 devices in a mesh: section: 4 (over x, core), dp: 8 (over z, y).
Axes of the slice: x: 2, y: 2, z: 4, core: 2. Of those that a mesh axis runs over, the one named last changes fastest.
Arguments:
- arriving_activations: bfloat16 [4, 16, 12, 12, 256], P('section', 'dp'), may hold values from -6 to 6
- fresh_images: bfloat16 [3, 16, 12, 12, 256], P(None, 'dp'), may hold values from -6 to 6
- saved_inputs: bfloat16 [4, 4, 16, 12, 12, 256], P(None, 'section', 'dp'), may hold values from -6 to 6
- arriving_gradients: bfloat16 [4, 16, 12, 12, 256], P('section', 'dp'), may hold values from -6 to 6
- fresh_gradients: bfloat16 [3, 16, 12, 12, 256], P(None, 'dp'), may hold values from -6 to 6
- feed_order: int32 [3], replicated, may hold values from 0 to 2, each once
- forward_weight: bfloat16 [4, 2304, 256], P('section'), may hold values from -0.125 to 0.125
- forward_gain: float32 [4, 256], P('section'), may hold values from 0.1 to 1.9
- forward_bias: float32 [4, 256], P('section'), may hold values from -3 to 3
- backward_weight: bfloat16 [4, 2304, 256], P('section'), may hold values from -0.125 to 0.125
- backward_gain: float32 [4, 256], P('section'), may hold values from 0.1 to 1.9
- backward_bias: float32 [4, 256], P('section'), may hold values from -3 to 3
Outputs:
- section_outputs: float32 [4, 4, 16, 12, 12, 256], P(None, 'section', 'dp')
- input_gradients: float32 [4, 4, 16, 12, 12, 256], P(None, 'section', 'dp')
- weight_gradient: float32 [4, 2304, 256], P('section', 'dp')
Inputs may be any that keep to these rules, and one draw needn't show every extreme that they name: `feed_order`: each of 0 to 2 appears once.
All inputs are finite; a program needn't handle non-finite values.
Results may differ from a plain program's by a relative error of at most 0.0044.
Values sent between devices are 32-bit elements; how exact they have to be, the bound alone decides.
No kernel may reach another device: no remote copies, remote signals or barrier semaphores. Data moves between devices by JAX's collectives and lax.ppermute only.
A program may use at most 64 MiB of HBM per device.

v0:
```python
import jax
import jax.numpy as jnp
from jax import lax
from jax.sharding import PartitionSpec as P

GROUPS = 32
TICKS = 4


def passed_along(block, axis, distance):
    devices = range(lax.axis_size(axis))
    route = [(i - distance, i) for i in devices if i - distance in devices]
    return lax.ppermute(block, axis, route)


def group_norm_silu(values, gain, bias):
    grouped = values.reshape(values.shape[0], values.shape[1] * values.shape[2], GROUPS, -1)
    average = jnp.mean(grouped, axis=(1, 3), keepdims=True)
    spread = jnp.mean(jnp.square(grouped - average), axis=(1, 3), keepdims=True)
    normed = ((grouped - average) * lax.rsqrt(spread + 1e-05)).reshape(values.shape)
    scaled = normed * gain + bias
    return scaled * jax.nn.sigmoid(scaled)


def patches(images):
    rows = images.shape[1]
    cols = images.shape[2]
    padded = jnp.pad(images, ((0, 0), (1, 1), (1, 1), (0, 0)))
    shifted = [
        padded[:, shift_row : shift_row + rows, shift_col : shift_col + cols, :]
        for shift_row in range(3)
        for shift_col in range(3)
    ]
    return jnp.concatenate(shifted, axis=-1).reshape(-1, 9 * images.shape[3])


def flipped(weight):
    channels = weight.shape[1]
    return (
        weight.reshape(3, 3, channels, channels)[::-1, ::-1]
        .transpose(0, 1, 3, 2)
        .reshape(9 * channels, channels)
    )


def forward_layer(widened, weight, gain, bias):
    hidden = group_norm_silu(widened, gain, bias).astype(jnp.bfloat16)
    convolved = jnp.dot(patches(hidden), weight, preferred_element_type=jnp.float32).reshape(
        widened.shape
    )
    return widened + convolved


def backward_layer(saved, incoming, narrow, weight, gain, bias):
    widened = saved.astype(jnp.float32)
    activated, pullback = jax.vjp(lambda values: group_norm_silu(values, gain, bias), widened)
    hidden = activated.astype(jnp.bfloat16)
    hidden_grad = jnp.dot(
        patches(narrow), flipped(weight), preferred_element_type=jnp.float32
    ).reshape(saved.shape)
    (through_norm,) = pullback(hidden_grad)
    return (incoming + through_norm, patches(hidden))


def shards(
    arriving_activations,
    fresh_images,
    saved_inputs,
    arriving_gradients,
    fresh_gradients,
    feed_order,
    forward_weight,
    forward_gain,
    forward_bias,
    backward_weight,
    backward_gain,
    backward_bias,
):
    section_pos = lax.axis_index("section")
    act_in = arriving_activations[0].astype(jnp.float32)
    grad_in = arriving_gradients[0].astype(jnp.float32)
    act_out = act_in
    grad_out = grad_in
    emitted = []
    returned = []
    column_list = []
    incoming_list = []
    for tick_num in range(TICKS):
        if tick_num > 0:
            index = feed_order[tick_num - 1]
            arrived, arrived_grad = passed_along((act_out, grad_out), "section", 1)
            chosen = lax.dynamic_index_in_dim(fresh_images, index, 0, keepdims=False).astype(
                jnp.float32
            )
            act_in = jnp.where(section_pos == 0, chosen, arrived)
            chosen_grad = lax.dynamic_index_in_dim(
                fresh_gradients, index, 0, keepdims=False
            ).astype(jnp.float32)
            grad_in = jnp.where(section_pos == 0, chosen_grad, arrived_grad)
        narrow = grad_in.astype(jnp.bfloat16)
        act_out = forward_layer(act_in, forward_weight[0], forward_gain[0], forward_bias[0])
        grad_out, columns = backward_layer(
            saved_inputs[tick_num, 0],
            grad_in,
            narrow,
            backward_weight[0],
            backward_gain[0],
            backward_bias[0],
        )
        emitted.append(act_out)
        returned.append(grad_out)
        column_list.append(columns)
        incoming_list.append(narrow.reshape(-1, narrow.shape[3]))
    column_rows = jnp.concatenate(column_list, axis=0)
    incoming_rows = jnp.concatenate(incoming_list, axis=0)
    factor = 1.0 / (lax.axis_size("dp") * act_in.shape[0])
    total = (
        lax.dot_general(
            column_rows, incoming_rows, (((0,), (0,)), ((), ())), preferred_element_type=jnp.float32
        )
        * factor
    )
    shard_sum = lax.psum_scatter(total, "dp", scatter_dimension=0, tiled=True)
    return (jnp.stack(emitted)[:, None], jnp.stack(returned)[:, None], shard_sum[None])


def solution(mesh):
    placed = (
        P("section", "dp", None, None, None),
        P(None, "dp", None, None, None),
        P(None, "section", "dp", None, None, None),
        P("section", "dp", None, None, None),
        P(None, "dp", None, None, None),
        P(),
        P("section", None, None),
        P("section", None),
        P("section", None),
        P("section", None, None),
        P("section", None),
        P("section", None),
    )
    return jax.shard_map(
        shards,
        mesh=mesh,
        in_specs=placed,
        out_specs=(
            P(None, "section", "dp", None, None, None),
            P(None, "section", "dp", None, None, None),
            P("section", "dp", None),
        ),
        check_vma=False,
    )
```

profile of v0, /device:TPU:0, one launch (start us, length us, event | category | flops | bytes accessed | tf_op | source)
XLA Modules:
  0.0 222.0 jit_solution(3800894750607989050)
XLA Ops:
  17.7 1.5 copy.35
  19.3 2.6 %multiply_reduce_fusion.6 = (f32[2,256]{1,0:T(2,128)S(1)}, f32[2,256]{1,0:T(2,128)S(1)}, f32[2,12,12,256]{3,2,1,0:T(8,128)S(1)}) fusion(f32[2,256]{1,0:T(2,128)S(1)} %mul.459, f32[2,256]{1,0:T(2,128)S(1)} %sub.207, bf16[1,1,2,12,12,256]{5,2,4,3,1,0:T(2,128)(2,1)S(1)} %get-tuple-element.20, f32[256]{0:T(256)S(1)} %bitcast.356, f32[256]{0:T(256)S(1)} %bitcast.365, ...), kind=kOutput, calls=%fused_computation.171 | convolution fusion | flops 341138432 | bytes 2959360 | tf_op jit(solution)/shard_map/dot_general | solution.py:58
  23.2 3.1 %collective-permute-start.3 = (f32[2,12,12,256]{3,2,1,0:T(8,128)S(1)}, f32[2,12,12,256]{3,2,1,0:T(8,128)}, u32[]{:S(2)}, u32[]{:S(2)}) collective-permute-start(f32[2,12,12,256]{3,2,1,0:T(8,128)S(1)} %get-tuple-element.28), channel_id=1, source_target_pairs={{0,8},{8,16},{16,24},{1,9},{9,17},{17,25},{2,10},{10,18},{18,26},{... | collective-permute-start | bytes 884744 | tf_op jit(solution)/shard_map/ppermute | solution.py:13
  29.3 3.9 %collective-permute-start = (f32[2,12,12,256]{3,2,1,0:T(8,128)}, f32[2,12,12,256]{3,2,1,0:T(8,128)S(1)}, u32[]{:S(2)}, u32[]{:S(2)}) collective-permute-start(f32[2,12,12,256]{3,2,1,0:T(8,128)} %convolution_add_fusion.3), channel_id=1, source_target_pairs={{0,8},{8,16},{16,24},{1,9},{9,17},{17,25},{2,10},{10,18},{18,26},{... | collective-permute-start | bytes 884744 | tf_op jit(solution)/shard_map/ppermute | solution.py:13
  47.6 2.1 constant_dynamic-slice_fusion
  58.5 2.2 %multiply_reduce_fusion.5 = (f32[2,256]{1,0:T(2,128)S(1)}, f32[2,256]{1,0:T(2,128)S(1)}, f32[2,12,12,256]{3,2,1,0:T(8,128)S(1)}) fusion(f32[2,256]{1,0:T(2,128)S(1)} %copy-done.32, f32[2,256]{1,0:T(2,128)S(1)} %sub.214, bf16[1,1,2,12,12,256]{5,2,4,3,1,0:T(2,128)(2,1)S(1)} %get-tuple-element.19, f32[256]{0:T(256)S(1)} %bitcast.358, f32[256]{0:T(256)S(1)} %bitcast.367, ...), kind=kOutput, calls=%fused_computation.170 | convolution fusion | flops 341138432 | bytes 2959360 | tf_op jit(solution)/shard_map/dot_general | solution.py:58
  62.4 1.7 fusion.92
  64.1 3.9 %collective-permute-start.4 = (f32[2,12,12,256]{3,2,1,0:T(8,128)}, f32[2,12,12,256]{3,2,1,0:T(8,128)}, u32[]{:S(2)}, u32[]{:S(2)}) collective-permute-start(f32[2,12,12,256]{3,2,1,0:T(8,128)} %get-tuple-element.30), channel_id=1, source_target_pairs={{0,8},{8,16},{16,24},{1,9},{9,17},{17,25},{2,10},{10,18},{18,26},{... | collective-permute-start | bytes 884744 | tf_op jit(solution)/shard_map/ppermute | solution.py:13
  71.7 1.5 collective-permute-start.1
  82.9 3.0 %multiply_reduce_fusion.4 = (f32[2,256]{1,0:T(2,128)S(1)}, f32[2,256]{1,0:T(2,128)S(1)}, f32[2,12,12,256]{3,2,1,0:T(8,128)}) fusion(f32[2,256]{1,0:T(2,128)S(1)} %copy-done.33, f32[2,256]{1,0:T(2,128)S(1)} %sub.221, bf16[1,1,2,12,12,256]{5,2,4,3,1,0:T(2,128)(2,1)S(1)} %get-tuple-element.18, f32[256]{0:T(256)S(1)} %bitcast.359, f32[256]{0:T(256)S(1)} %bitcast.368, ...), kind=kOutput, calls=%fused_computation.169 | convolution fusion | flops 341138432 | bytes 2959360 | tf_op jit(solution)/shard_map/dot_general | solution.py:58
  86.9 2.0 fusion.109
  88.9 3.7 %collective-permute-start.5 = (f32[2,12,12,256]{3,2,1,0:T(8,128)}, f32[2,12,12,256]{3,2,1,0:T(8,128)}, u32[]{:S(2)}, u32[]{:S(2)}) collective-permute-start(f32[2,12,12,256]{3,2,1,0:T(8,128)} %get-tuple-element.32), channel_id=1, source_target_pairs={{0,8},{8,16},{16,24},{1,9},{9,17},{17,25},{2,10},{10,18},{18,26},{... | collective-permute-start | bytes 884744 | tf_op jit(solution)/shard_map/ppermute | solution.py:13
  104.5 3.0 %multiply_reduce_fusion.3 = (f32[2,256]{1,0:T(2,128)S(1)}, f32[2,256]{1,0:T(2,128)S(1)}, f32[2,12,12,256]{3,2,1,0:T(8,128)}) fusion(f32[2,256]{1,0:T(2,128)S(1)} %copy-done.34, f32[2,256]{1,0:T(2,128)S(1)} %sub.228, bf16[1,1,2,12,12,256]{5,2,4,3,1,0:T(2,128)(2,1)S(1)} %get-tuple-element.17, f32[256]{0:T(256)S(1)} %bitcast.361, f32[256]{0:T(256)S(1)} %bitcast.370, ...), kind=kOutput, calls=%fused_computation.168 | convolution fusion | flops 341138432 | bytes 2959360 | tf_op jit(solution)/shard_map/dot_general | solution.py:58
  109.1 2.0 fusion.126
  111.4 2.1 constant_dynamic-update-slice_fusion.76
  117.9 3.2 %reshape.405 = bf16[288,2304]{1,0:T(8,128)(2,1)} reshape(bf16[2,12,12,2304]{3,2,1,0:T(8,128)(2,1)} %constant_dynamic-update-slice_fusion.72) | data formatting | bytes 2654208 | tf_op jit(solution)/shard_map/reshape | solution.py:34
  123.4 3.2 %reshape.406 = bf16[288,2304]{1,0:T(8,128)(2,1)} reshape(bf16[2,12,12,2304]{3,2,1,0:T(8,128)(2,1)} %constant_dynamic-update-slice_fusion.81) | data formatting | bytes 2654208 | tf_op jit(solution)/shard_map/reshape | solution.py:34
  129.7 3.2 %reshape.407 = bf16[288,2304]{1,0:T(8,128)(2,1)} reshape(bf16[2,12,12,2304]{3,2,1,0:T(8,128)(2,1)} %constant_dynamic-update-slice_fusion.90) | data formatting | bytes 2654208 | tf_op jit(solution)/shard_map/reshape | solution.py:34
  135.1 3.2 %reshape.408 = bf16[288,2304]{1,0:T(8,128)(2,1)} reshape(bf16[2,12,12,2304]{3,2,1,0:T(8,128)(2,1)} %constant_dynamic-update-slice_fusion.99) | data formatting | bytes 2654208 | tf_op jit(solution)/shard_map/reshape | solution.py:34
  138.3 4.7 %fusion.8 = f32[2304,256]{1,0:T(8,128)} fusion(bf16[288,2304]{1,0:T(8,128)(2,1)} %reshape.408, bf16[288,2304]{1,0:T(8,128)(2,1)} %reshape.407, bf16[288,2304]{1,0:T(8,128)(2,1)} %reshape.406, bf16[288,2304]{1,0:T(8,128)(2,1)} %reshape.405, bf16[288,256]{1,0:T(8,128)(2,1)S(1)} %reshape.412, bf16[288,256]{1,0:T(8,128)(2,1)S(1)} %copy-done.18, ...), kind=kOutput, calls=%fused_computation.8 | convolution fusion | flops 1383137280 | bytes 8257536 | tf_op jit(solution)/shard_map/dot_general | solution.py:118
  145.5 2.6 %collective-permute-start.2 = (f32[2,12,12,256]{3,2,1,0:T(8,128)S(1)}, f32[2,12,12,256]{3,2,1,0:T(8,128)S(1)}, u32[]{:S(2)}, u32[]{:S(2)}) collective-permute-start(f32[2,12,12,256]{3,2,1,0:T(8,128)S(1)} %convolution_add_fusion.1), channel_id=1, source_target_pairs={{0,8},{8,16},{16,24},{1,9},{9,17},{17,25},{2,10},{10,18},{18,26},{... | collective-permute-start | bytes 884744 | tf_op jit(solution)/shard_map/ppermute | solution.py:13
  149.4 2.0 copy.45
  155.1 2.0 copy.44
  157.1 58.1 %reduce-scatter.2.cloned.1.call-done = f32[288,256]{1,0:T(8,128)} async-done(((f32[2304,256]{1,0:T(8,128)}), f32[288,256]{1,0:T(8,128)}) %reduce-scatter.2.cloned.1.call-update) | async-done | bytes 294928 | tf_op jit(solution)/shard_map/reduce_scatter | solution.py:123
  (371 shorter events, 80.8 us)
Async XLA Ops:
  7.2 20.8 %copy-start = (bf16[1,2304,256]{2,1,0:T(8,128)(2,1)S(1)}, bf16[1,2304,256]{2,1,0:T(8,128)(2,1)}, u32[]{:S(2)}) copy-start(bf16[1,2304,256]{2,1,0:T(8,128)(2,1)} %param.18) | copy-start | bytes 3538948
  7.2 208.0 %reduce-scatter.2.cloned.1.call-start = ((), (), s32[]{:S(2)}) async-start(), calls=%async_computation.1 | async-start | bytes 2654208 | tf_op jit(solution)/shard_map/reduce_scatter | solution.py:123
  8.3 6.8 %copy-start.15 = (bf16[4,1,2,12,12,256]{5,2,4,3,1,0:T(2,128)(2,1)S(1)}, bf16[4,1,2,12,12,256]{5,2,4,3,1,0:T(2,128)(2,1)}, u32[]{:S(2)}) copy-start(bf16[4,1,2,12,12,256]{5,2,4,3,1,0:T(2,128)(2,1)} %param.14) | copy-start | bytes 1769476
  16.3 6.6 %copy-start.31 = (f32[2,256]{1,0:T(2,128)}, f32[2,256]{1,0:T(2,128)S(1)}, u32[]{:S(2)}) copy-start(f32[2,256]{1,0:T(2,128)S(1)} %mul.459) | copy-start | bytes 6148
  23.2 27.8 %collective-permute-start.3 = (f32[2,12,12,256]{3,2,1,0:T(8,128)S(1)}, f32[2,12,12,256]{3,2,1,0:T(8,128)}, u32[]{:S(2)}, u32[]{:S(2)}) collective-permute-start(f32[2,12,12,256]{3,2,1,0:T(8,128)S(1)} %get-tuple-element.28), channel_id=1, source_target_pairs={{0,8},{8,16},{16,24},{1,9},{9,17},{17,25},{2,10},{10,18},{18,26},{... | collective-permute-start | bytes 884744 | tf_op jit(solution)/shard_map/ppermute | solution.py:13
  29.3 9.2 %copy-start.44 = (s32[3]{0:T(128)S(1)}, s32[3]{0:T(128)}, u32[]{:S(2)}) copy-start(s32[3]{0:T(128)} %param.17) | copy-start | bytes 40
  29.3 39.5 %collective-permute-start = (f32[2,12,12,256]{3,2,1,0:T(8,128)}, f32[2,12,12,256]{3,2,1,0:T(8,128)S(1)}, u32[]{:S(2)}, u32[]{:S(2)}) collective-permute-start(f32[2,12,12,256]{3,2,1,0:T(8,128)} %convolution_add_fusion.3), channel_id=1, source_target_pairs={{0,8},{8,16},{16,24},{1,9},{9,17},{17,25},{2,10},{10,18},{18,26},{... | collective-permute-start | bytes 884744 | tf_op jit(solution)/shard_map/ppermute | solution.py:13
  35.5 12.1 %copy-start.38 = (f32[2,32]{1,0:T(2,128)}, f32[2,32]{1,0:T(2,128)S(1)}, u32[]{:S(2)}) copy-start(f32[2,32]{1,0:T(2,128)S(1)} %reduce_sum.554) | copy-start | bytes 772
  52.5 6.0 %copy-start.24 = (f32[1,256]{1,0:T(1,128)S(1)}, f32[1,256]{1,0:T(1,128)}, u32[]{:S(2)}) copy-start(f32[1,256]{1,0:T(1,128)} %param.23) | copy-start | bytes 3076
  52.5 6.0 %copy-start.28 = (f32[1,256]{1,0:T(1,128)S(1)}, f32[1,256]{1,0:T(1,128)}, u32[]{:S(2)}) copy-start(f32[1,256]{1,0:T(1,128)} %param.22) | copy-start | bytes 3076
  52.5 6.0 %copy-start.32 = (f32[2,256]{1,0:T(2,128)S(1)}, f32[2,256]{1,0:T(2,128)}, u32[]{:S(2)}) copy-start(f32[2,256]{1,0:T(2,128)} %mul.483) | copy-start | bytes 6148
  64.1 11.3 %collective-permute-start.4 = (f32[2,12,12,256]{3,2,1,0:T(8,128)}, f32[2,12,12,256]{3,2,1,0:T(8,128)}, u32[]{:S(2)}, u32[]{:S(2)}) collective-permute-start(f32[2,12,12,256]{3,2,1,0:T(8,128)} %get-tuple-element.30), channel_id=1, source_target_pairs={{0,8},{8,16},{16,24},{1,9},{9,17},{17,25},{2,10},{10,18},{18,26},{... | collective-permute-start | bytes 884744 | tf_op jit(solution)/shard_map/ppermute | solution.py:13
  71.7 7.5 %copy-start.3 = (f32[2,12,12,256]{3,2,1,0:T(8,128)}, f32[2,12,12,256]{3,2,1,0:T(8,128)S(1)}, u32[]{:S(2)}) copy-start(f32[2,12,12,256]{3,2,1,0:T(8,128)S(1)} %convolution_add_fusion.2) | copy-start | bytes 884740
  71.7 21.7 %collective-permute-start.1 = (f32[2,12,12,256]{3,2,1,0:T(8,128)S(1)}, f32[2,12,12,256]{3,2,1,0:T(8,128)S(1)}, u32[]{:S(2)}, u32[]{:S(2)}) collective-permute-start(f32[2,12,12,256]{3,2,1,0:T(8,128)S(1)} %convolution_add_fusion.2), channel_id=1, source_target_pairs={{0,8},{8,16},{16,24},{1,9},{9,17},{17,25},{2,10},{10,18},{18,26},{... | collective-permute-start | bytes 884744 | tf_op jit(solution)/shard_map/ppermute | solution.py:13
  76.2 6.7 %copy-start.25 = (f32[1,256]{1,0:T(1,128)S(1)}, f32[1,256]{1,0:T(1,128)}, u32[]{:S(2)}) copy-start(f32[1,256]{1,0:T(1,128)} %param.23) | copy-start | bytes 3076
  76.2 6.7 %copy-start.29 = (f32[1,256]{1,0:T(1,128)S(1)}, f32[1,256]{1,0:T(1,128)}, u32[]{:S(2)}) copy-start(f32[1,256]{1,0:T(1,128)} %param.22) | copy-start | bytes 3076
  76.2 6.7 %copy-start.33 = (f32[2,256]{1,0:T(2,128)S(1)}, f32[2,256]{1,0:T(2,128)}, u32[]{:S(2)}) copy-start(f32[2,256]{1,0:T(2,128)} %mul.504) | copy-start | bytes 6148
  76.9 6.0 %copy-start.13 = (bf16[3,3,256,256]{3,2,1,0:T(8,128)(2,1)S(1)}, bf16[3,3,256,256]{3,2,1,0:T(8,128)(2,1)}, u32[]{:S(2)}) copy-start(bf16[3,3,256,256]{3,2,1,0:T(8,128)(2,1)} %copy.35) | copy-start | bytes 3538948
  88.9 7.7 %collective-permute-start.5 = (f32[2,12,12,256]{3,2,1,0:T(8,128)}, f32[2,12,12,256]{3,2,1,0:T(8,128)}, u32[]{:S(2)}, u32[]{:S(2)}) collective-permute-start(f32[2,12,12,256]{3,2,1,0:T(8,128)} %get-tuple-element.32), channel_id=1, source_target_pairs={{0,8},{8,16},{16,24},{1,9},{9,17},{17,25},{2,10},{10,18},{18,26},{... | collective-permute-start | bytes 884744 | tf_op jit(solution)/shard_map/ppermute | solution.py:13
  98.4 6.0 %copy-start.14 = (bf16[3,3,256,256]{3,2,1,0:T(8,128)(2,1)S(1)}, bf16[3,3,256,256]{3,2,1,0:T(8,128)(2,1)}, u32[]{:S(2)}) copy-start(bf16[3,3,256,256]{3,2,1,0:T(8,128)(2,1)} %copy.35) | copy-start | bytes 3538948
  98.5 6.0 %copy-start.26 = (f32[1,256]{1,0:T(1,128)S(1)}, f32[1,256]{1,0:T(1,128)}, u32[]{:S(2)}) copy-start(f32[1,256]{1,0:T(1,128)} %param.23) | copy-start | bytes 3076
  98.5 6.0 %copy-start.30 = (f32[1,256]{1,0:T(1,128)S(1)}, f32[1,256]{1,0:T(1,128)}, u32[]{:S(2)}) copy-start(f32[1,256]{1,0:T(1,128)} %param.22) | copy-start | bytes 3076
  98.5 6.0 %copy-start.34 = (f32[2,256]{1,0:T(2,128)S(1)}, f32[2,256]{1,0:T(2,128)}, u32[]{:S(2)}) copy-start(f32[2,256]{1,0:T(2,128)} %mul.525) | copy-start | bytes 6148
  145.5 5.9 %collective-permute-start.2 = (f32[2,12,12,256]{3,2,1,0:T(8,128)S(1)}, f32[2,12,12,256]{3,2,1,0:T(8,128)S(1)}, u32[]{:S(2)}, u32[]{:S(2)}) collective-permute-start(f32[2,12,12,256]{3,2,1,0:T(8,128)S(1)} %convolution_add_fusion.1), channel_id=1, source_target_pairs={{0,8},{8,16},{16,24},{1,9},{9,17},{17,25},{2,10},{10,18},{18,26},{... | collective-permute-start | bytes 884744 | tf_op jit(solution)/shard_map/ppermute | solution.py:13
  (28 other events, 81.7 us)
Sparse Core Ops, SparseCore 0:
  143.2 71.9 reduce-scatter.1
where the time goes:
time: 223 us; the launch traced here: 222 us
  local copies, waits for them, and re-layouts  88.6 us (40%)
  waiting for transfers between devices  58.1 us (26%)
  between operations  20.7 us (9%)
  starting transfers between devices  18.8 us (8%)
  matrix products  18.8 us (8%)
  other arithmetic  17.1 us (8%)
    reduce_scatter x1, waiting for transfers between devices, shards(): shard_sum = lax.psum_scatter(total, 'dp', scatter_dimension=0, tiled=True)  58.1 us
    unnamed x182, local copies, waits for them, and re-layouts  50 us
    ppermute x6, starting transfers between devices, passed_along(): return lax.ppermute(block, axis, route)  18.7 us
    reshape x4, local copies, waits for them, and re-layouts, patches(): return jnp.concatenate(shifted, axis=-1).reshape(-1, 9 * images.shape[3])  12.8 us
    dot_general x4, matrix products, backward_layer(): jnp.dot(patches(narrow), flipped(weight), preferred_element_type=jnp.floa...  10.8 us
    concatenate x12, local copies, waits for them, and re-layouts, patches(): return jnp.concatenate(shifted, axis=-1).reshape(-1, 9 * images.shape[3])  6.27 us
    convert_element_type x4, other arithmetic, backward_layer(): hidden = activated.astype(jnp.bfloat16)  5.93 us
    dot_general x1, matrix products, shards(): lax.dot_general(column_rows, incoming_rows, (((0,), (0,)), ((), ())), pre...  4.72 us
  transfers between devices with their start and end apart: 7, of which 1 were waited for; matrix products, arithmetic and copies ran while one was open for 28% of the time, Pallas kernels for 0%

commit v1 on v0

v1 whole, which is shorter than its diff:
```python
import functools
import math

import jax
import jax.numpy as jnp
from jax import lax
from jax.experimental import pallas as pl
from jax.experimental.pallas import tpu as pltpu
from jax.sharding import PartitionSpec as P

GROUPS = 32
F32 = jnp.float32
BF16 = jnp.bfloat16
LANES = 128
VMEM_LIMIT = 24 * 1024 * 1024


class Dims:
    def __init__(self, images, rows, cols, channels):
        self.n, self.h, self.w, self.c = images, rows, cols, channels
        self.cts = channels // LANES
        self.unit = self.cts * images
        self.pix = rows * cols
        self.flat = self.pix * self.unit
        per = 8 // math.gcd(8, self.unit)
        self.pad = -(-(cols + 1) // per) * per
        self.padded = (self.pix + 2 * self.pad) * self.unit
        self.count = self.pix * (channels // GROUPS)


def interleaved(x, d):
    lead = x.shape[:-4]
    k = len(lead)
    x = x.reshape(*lead, d.n, d.pix, d.cts, LANES)
    x = x.transpose(*range(k), k + 1, k + 2, k, k + 3)
    return x.reshape(*lead, d.flat, LANES)


def standard(x, d):
    lead = x.shape[:-2]
    k = len(lead)
    x = x.reshape(*lead, d.pix, d.cts, d.n, LANES)
    x = x.transpose(*range(k), k + 2, k, k + 1, k + 3)
    return x.reshape(*lead, d.n, d.h, d.w, d.c)


def group_sum(v, width):
    lane = lax.broadcasted_iota(jnp.int32, v.shape, 1)
    k = 1
    while k < width:
        v = v + jnp.where((lane & k) == 0, pltpu.roll(v, LANES - k, 1), pltpu.roll(v, k, 1))
        k *= 2
    return v


def pattern(ref, d):
    row = lax.broadcasted_iota(jnp.int32, (8, LANES), 0)
    ct = (row // d.n) % d.cts
    out = jnp.broadcast_to(ref[0:1, :], (8, LANES))
    for i in range(1, d.cts):
        out = jnp.where(ct == i, jnp.broadcast_to(ref[i : i + 1, :], (8, LANES)), out)
    return out


def unit_sum(v, d):
    s = jnp.sum(v, axis=0)
    k = d.unit
    while k < 8:
        s = s + pltpu.roll(s, k, 0)
        k *= 2
    return group_sum(s, d.c // GROUPS)


def normalized(x, d):
    tiles = x.reshape(-1, 8, LANES)
    scale = 1.0 / d.count
    mean = unit_sum(tiles, d) * scale
    centred = tiles - mean
    var = unit_sum(centred * centred, d) * scale
    rstd = lax.rsqrt(var + 1e-05)
    return centred * rstd, rstd


def sigmoid(a):
    return 0.5 * jnp.tanh(0.5 * a) + 0.5


def spread(value, refs, d):
    zeros = jnp.zeros((d.pad * d.unit, LANES), F32)
    for ref in refs:
        ref[0 : d.pad * d.unit, :] = zeros
        ref[d.padded - d.pad * d.unit : d.padded, :] = zeros
        ref[d.pad * d.unit : d.pad * d.unit + d.flat, :] = value
    edge = jnp.zeros((d.unit, LANES), F32)
    for i in range(d.h):
        last = (d.pad + i * d.w + d.w - 1) * d.unit
        first = (d.pad + i * d.w) * d.unit
        refs[0][last : last + d.unit, :] = edge
        refs[2][first : first + d.unit, :] = edge


def plane(ref, d, shift, n):
    parts = [
        ref[pl.ds((d.pad + shift) * d.unit + ct * d.n + n, d.pix, stride=d.unit), :] for ct in range(d.cts)
    ]
    return jnp.concatenate(parts, axis=1)


def gather_patches(refs, out_ref, d):
    for kr in range(3):
        for kc in range(3):
            tap = kr * 3 + kc
            for n in range(d.n):
                block = plane(refs[kc], d, (kr - 1) * d.w + kc - 1, n)
                out_ref[n * d.pix : (n + 1) * d.pix, tap * d.c : (tap + 1) * d.c] = block.astype(BF16)


def from_interleaved(ref, d, base=0):
    rows = [
        jnp.concatenate(
            [ref[pl.ds(base + ct * d.n + n, d.pix, stride=d.unit), :] for ct in range(d.cts)], axis=1
        )
        for n in range(d.n)
    ]
    return jnp.concatenate(rows, axis=0)


def to_interleaved(ref, n, value, d):
    for ct in range(d.cts):
        ref[pl.ds(ct * d.n + n, d.pix, stride=d.unit), :] = value[:, ct * LANES : (ct + 1) * LANES]


def prep_kernel(d, saved_ref, gain_ref, bias_ref, slope_ref, normed_ref, rstd_ref, hidden_ref, tmp):
    x = saved_ref[...].astype(F32)
    normed, rstd = normalized(x, d)
    gain = pattern(gain_ref, d)
    a = normed * gain + pattern(bias_ref, d)
    s = sigmoid(a)
    rstd_ref[...] = rstd
    for ref, value in (
        (normed_ref, normed),
        (slope_ref, s * (1.0 + a * (1.0 - s)) * gain),
        (hidden_ref, a * s),
    ):
        tmp[...] = value.reshape(d.flat, LANES)
        ref[...] = from_interleaved(tmp, d).astype(ref.dtype)


def entering(first, sec_ref, fresh_ref, arrived_ref):
    fresh = fresh_ref[0].astype(F32)
    if first:
        return fresh
    return jnp.where(sec_ref[1] == 0, fresh, arrived_ref[...])


def backward_kernel(
    d, first, sec_ref, fresh_ref, arrived_ref, slope_ref, normed_ref, rstd_ref, weight_ref, out_ref, e_ref, left, mid, right, cols
):
    e = entering(first, sec_ref, fresh_ref, arrived_ref)
    e_ref[...] = e
    spread(e, (left, mid, right), d)
    gather_patches((left, mid, right), cols, d)
    grad = None
    for tap in range(9):
        part = lax.dot_general(
            cols[:, tap * d.c : (tap + 1) * d.c],
            weight_ref[(8 - tap) * d.c : (9 - tap) * d.c, :],
            (((1,), (1,)), ((), ())),
            preferred_element_type=F32,
        )
        grad = part if grad is None else grad + part
    through = grad * slope_ref[...]
    weighted = through * normed_ref[...]
    rows = []
    for ct in range(d.cts):
        for n in range(d.n):
            for v in (through, weighted):
                rows.append(
                    jnp.sum(v[n * d.pix : (n + 1) * d.pix, ct * LANES : (ct + 1) * LANES], axis=0, keepdims=True)
                )
    sums = group_sum(jnp.concatenate(rows, axis=0), d.c // GROUPS) * (1.0 / d.count)
    for n in range(d.n):
        for ct in range(d.cts):
            k = (ct * d.n + n) * 2
            here = (slice(n * d.pix, (n + 1) * d.pix), slice(ct * LANES, (ct + 1) * LANES))
            rstd = rstd_ref[ct * d.n + n : ct * d.n + n + 1, :]
            value = (through[here] - sums[k : k + 1] - normed_ref[here] * sums[k + 1 : k + 2]) * rstd
            where = ct * d.n + n
            e_here = mid[pl.ds(d.pad * d.unit + where, d.pix, stride=d.unit), :]
            out_ref[pl.ds(where, d.pix, stride=d.unit), :] = value + e_here


def forward_kernel(
    d, first, sec_ref, fresh_ref, arrived_ref, gain_ref, bias_ref, weight_ref, out_ref, left, mid, right, cols, kept
):
    x = entering(first, sec_ref, fresh_ref, arrived_ref)
    kept[...] = x
    normed, _ = normalized(x, d)
    a = normed * pattern(gain_ref, d) + pattern(bias_ref, d)
    hidden = (a * sigmoid(a)).reshape(d.flat, LANES)
    spread(hidden, (left, mid, right), d)
    gather_patches((left, mid, right), cols, d)
    conv = jnp.dot(cols[...], weight_ref[...], preferred_element_type=F32)
    for n in range(d.n):
        for ct in range(d.cts):
            where = pl.ds(ct * d.n + n, d.pix, stride=d.unit)
            out_ref[where, :] = (
                kept[where, :] + conv[n * d.pix : (n + 1) * d.pix, ct * LANES : (ct + 1) * LANES]
            )


def weight_kernel(d, ticks, chunk, factor, slot_ref, *refs):
    e_refs, h_refs = refs[:ticks], refs[ticks : 2 * ticks]
    up_ref, down_ref, left, mid, right, cols, hid = refs[2 * ticks :]
    rows = d.n * d.pix
    for t in range(ticks):
        spread(e_refs[t][...], (left, mid, right), d)
        gather_patches((left, mid, right), cols.at[t * rows : (t + 1) * rows], d)
        hid[t * rows : (t + 1) * rows, :] = h_refs[t][...]
    h = hid[...]
    size = math.gcd(d.c, chunk)
    for tap in range(9):
        block = lax.dot_general(
            h, cols[:, (8 - tap) * d.c : (9 - tap) * d.c], (((0,), (0,)), ((), ())), preferred_element_type=F32
        ) * factor
        at = tap * d.c
        while at < (tap + 1) * d.c:
            owner = at // chunk
            stop = min((owner + 1) * chunk, (tap + 1) * d.c)
            piece = block[at - tap * d.c : stop - tap * d.c]
            where = pl.ds(at - owner * chunk, stop - at)
            up_ref[slot_ref[owner], where, :] = piece[:, :LANES]
            down_ref[slot_ref[owner + 9 * d.c // chunk], where, :] = piece[:, LANES:]
            at = stop


def call(body, out_shape, scratch, cost, *operands):
    smem = pl.BlockSpec(memory_space=pltpu.SMEM)
    vmem = pl.BlockSpec(memory_space=pltpu.VMEM)
    specs = [smem if o.dtype == jnp.int32 else vmem for o in operands]
    return pl.pallas_call(
        body,
        out_shape=out_shape,
        in_specs=specs,
        out_specs=jax.tree.map(lambda _: vmem, out_shape),
        scratch_shapes=scratch,
        compiler_params=pltpu.CompilerParams(vmem_limit_bytes=VMEM_LIMIT),
        cost_estimate=cost,
    )(*operands)


def fed_call(body, out_shape, scratch, cost, sec, fresh, *operands):
    vmem = pl.BlockSpec(memory_space=pltpu.VMEM)
    grid_spec = pltpu.PrefetchScalarGridSpec(
        num_scalar_prefetch=1,
        grid=(1,),
        in_specs=[pl.BlockSpec((1,) + fresh.shape[1:], lambda i, sec: (sec[0], 0, 0))] + [vmem] * len(operands),
        out_specs=jax.tree.map(lambda _: vmem, out_shape),
        scratch_shapes=scratch,
    )
    return pl.pallas_call(
        body,
        out_shape=out_shape,
        grid_spec=grid_spec,
        compiler_params=pltpu.CompilerParams(vmem_limit_bytes=VMEM_LIMIT),
        cost_estimate=cost,
    )(sec, fresh, *operands)


def cost(us):
    return pl.CostEstimate(flops=0, bytes_accessed=int(us * 3.0e6), transcendentals=0)


def shards(
    arriving_activations,
    fresh_images,
    saved_inputs,
    arriving_gradients,
    fresh_gradients,
    feed_order,
    forward_weight,
    forward_gain,
    forward_bias,
    backward_weight,
    backward_gain,
    backward_bias,
):
    ticks = saved_inputs.shape[0]
    d = Dims(*saved_inputs.shape[2:])
    section = lax.axis_index("section").astype(jnp.int32)
    sections = lax.axis_size("section")
    ring = [(i, (i + 1) % sections) for i in range(sections)]

    act0 = interleaved(arriving_activations, d)
    grad0 = interleaved(arriving_gradients, d)
    fresh_act = interleaved(fresh_images, d)
    fresh_grad = interleaved(fresh_gradients, d)
    saved = interleaved(saved_inputs[:, 0], d)
    vectors = [
        v[0].reshape(d.cts, LANES) for v in (forward_gain, forward_bias, backward_gain, backward_bias)
    ]
    fgain, fbias, bgain, bbias = vectors

    msg = jax.ShapeDtypeStruct((d.flat, LANES), F32)
    rows = d.n * d.pix
    wide = jax.ShapeDtypeStruct((rows, d.c), F32)
    padded = pltpu.VMEM((d.padded, LANES), F32)
    cols = pltpu.VMEM((rows, 9 * d.c), BF16)

    def prep(t):
        return call(
            functools.partial(prep_kernel, d),
            (wide, wide, jax.ShapeDtypeStruct((8, LANES), F32), jax.ShapeDtypeStruct((rows, d.c), BF16)),
            [pltpu.VMEM((d.flat, LANES), F32)],
            cost(1.5),
            saved[t],
            bgain,
            bbias,
        )

    def source(t, first_block, fresh):
        if t == 0:
            return jnp.zeros((2,), jnp.int32), first_block
        return jnp.stack([feed_order[t - 1], section]), fresh

    def backward(t, arrived, prepared):
        sec, fresh = source(t, grad0, fresh_grad)
        slope, normed, rstd, _ = prepared
        return fed_call(
            functools.partial(backward_kernel, d, t == 0),
            (msg, msg),
            [padded] * 3 + [cols],
            cost(2.0),
            sec,
            fresh,
            arrived,
            slope,
            normed,
            rstd,
            backward_weight[0],
        )

    def forward(t, arrived):
        sec, fresh = source(t, act0, fresh_act)
        return fed_call(
            functools.partial(forward_kernel, d, t == 0),
            msg,
            [padded] * 3 + [cols, pltpu.VMEM((d.flat, LANES), F32)],
            cost(2.0),
            sec,
            fresh,
            arrived,
            fgain,
            fbias,
            forward_weight[0],
        )

    nothing = jnp.zeros((8, LANES), F32)
    arrived, arrived_grad = nothing, nothing
    emitted, returned, entered, hidden = [], [], [], []
    for t in range(ticks):
        prepared = prep(t)
        hidden.append(prepared[3])
        grad_out, e = backward(t, arrived_grad, prepared)
        returned.append(grad_out)
        entered.append(e)
        if t < ticks - 1:
            arrived_grad = lax.ppermute(grad_out, "section", ring)
        act_out = forward(t, arrived)
        emitted.append(act_out)
        if t < ticks - 1:
            arrived = lax.ppermute(act_out, "section", ring)

    n = lax.axis_size("dp")
    order = list(range(0, n, 2)) + list(range(n - 1 - n % 2, 0, -2))
    place = [order.index(i) for i in range(n)]
    chunk = 9 * d.c // n
    places = jnp.array(place, jnp.int32)
    me = places[lax.axis_index("dp")]
    slots = jnp.concatenate([(me - 1 - places) % n, (places - me - 1) % n])
    factor = 1.0 / (n * d.n)
    half = jax.ShapeDtypeStruct((n, chunk, LANES), F32)
    up, down = call(
        functools.partial(weight_kernel, d, ticks, chunk, factor),
        (half, half),
        [padded] * 3 + [pltpu.VMEM((ticks * rows, 9 * d.c), BF16), pltpu.VMEM((ticks * rows, d.c), BF16)],
        cost(4.0),
        slots,
        *entered,
        *hidden,
    )
    onward = [(order[i], order[(i + 1) % n]) for i in range(n)]
    back = [(b, a) for a, b in onward]
    a, b = up[0], down[0]
    for s in range(1, n):
        a, b = lax.ppermute(a, "dp", onward), lax.ppermute(b, "dp", back)
        a, b = a + up[s], b + down[s]
    shard_sum = jnp.concatenate([a, b], axis=1)
    return (
        jnp.stack([standard(v, d) for v in emitted])[:, None],
        jnp.stack([standard(v, d) for v in returned])[:, None],
        shard_sum[None],
    )


def solution(mesh):
    placed = (
        P("section", "dp", None, None, None),
        P(None, "dp", None, None, None),
        P(None, "section", "dp", None, None, None),
        P("section", "dp", None, None, None),
        P(None, "dp", None, None, None),
        P(),
        P("section", None, None),
        P("section", None),
        P("section", None),
        P("section", None, None),
        P("section", None),
        P("section", None),
    )
    return jax.shard_map(
        shards,
        mesh=mesh,
        in_specs=placed,
        out_specs=(
            P(None, "section", "dp", None, None, None),
            P(None, "section", "dp", None, None, None),
            P("section", "dp", None),
        ),
        check_vma=False,
    )
```

time: 223 us -> 96.6 us (0.43)
  local copies, waits for them, and re-layouts: 88.6 us -> 18.6 us
  waiting for transfers between devices: 58.1 us -> 26.8 us
  Pallas kernels: 0 us -> 22.3 us
  between operations: 20.7 us -> 1.8 us
  matrix products: 18.8 us -> 0 us
  other arithmetic: 17.1 us -> 8.06 us
    reduce_scatter x1 -> x0, waiting for transfers between devices: 58.1 us -> none  [shards(): shard_sum = lax.psum_scatter(total, 'dp', scatter_dimension=0, tiled=True)]
    unnamed x182 -> x96, local copies, waits for them, and re-layouts: 50 us -> 13.5 us
    ppermute x6 -> x20, waiting for transfers between devices: 0.02 us -> 26.8 us  [the longest x14 22.7 us: shards(): a, b = (lax.ppermute(a, 'dp', onward), lax.ppermute(b, 'dp', back))]
    pallas_call x0 -> x13, Pallas kernels: none -> 22.3 us  [the longest x8 16.2 us: fed_call(): pl.pallas_call(body, out_shape=out_shape, grid_spec=grid_spec, compiler_p...]
    dot_general x9 -> x0, matrix products: 18.8 us -> none  [the longest x4 10.8 us: backward_layer(): jnp.dot(patches(narrow), flipped(weight), preferred_element_type=jnp.floa...]
    reshape x8 -> x0, local copies, waits for them, and re-layouts: 14.9 us -> none  [the longest x4 12.8 us: patches(): return jnp.concatenate(shifted, axis=-1).reshape(-1, 9 * images.shape[3])]
    convert_element_type x11 -> x0, other arithmetic: 8.34 us -> none  [the longest x4 5.93 us: backward_layer(): hidden = activated.astype(jnp.bfloat16)]
    concatenate x12 -> x0, local copies, waits for them, and re-layouts: 6.27 us -> none  [patches(): return jnp.concatenate(shifted, axis=-1).reshape(-1, 9 * images.shape[3])]
  transfers between devices with their start and end apart: 7 -> 20, of which waited for: 1 -> 10; matrix products, arithmetic and copies ran while one was open for 28% -> 10% of each run, Pallas kernels for 0% -> 21%
where the time goes in v1:
time: 96.6 us; the launch traced here: 96.1 us
  waiting for transfers between devices  26.8 us (28%)
  Pallas kernels  22.3 us (23%)
  local copies, waits for them, and re-layouts  18.6 us (19%)
  starting transfers between devices  18.6 us (19%)
  other arithmetic  8.06 us (8%)
  between operations  1.8 us (2%)
    ppermute x14, waiting for transfers between devices, shards(): a, b = (lax.ppermute(a, 'dp', onward), lax.ppermute(b, 'dp', back))  22.7 us
    pallas_call x8, Pallas kernels, fed_call(): pl.pallas_call(body, out_shape=out_shape, grid_spec=grid_spec, compiler_p...  16.2 us
    ppermute x14, starting transfers between devices, shards(): a, b = (lax.ppermute(a, 'dp', onward), lax.ppermute(b, 'dp', back))  15.3 us
    unnamed x96, local copies, waits for them, and re-layouts  13.5 us
    pallas_call x5, Pallas kernels, call(): pl.pallas_call(body, out_shape=out_shape, in_specs=specs, out_specs=jax.t...  6.12 us
    ppermute x3, waiting for transfers between devices, shards(): arrived = lax.ppermute(act_out, 'section', ring)  2.79 us
    ppermute x3, starting transfers between devices, shards(): arrived = lax.ppermute(act_out, 'section', ring)  2.78 us
    broadcast_in_dim x1, other arithmetic, shards(): jnp.stack([standard(v, d) for v in returned])[:, None]  2.51 us
  transfers between devices with their start and end apart: 20, of which 10 were waited for; matrix products, arithmetic and copies ran while one was open for 10% of the time, Pallas kernels for 21%

profile of v1, /device:TPU:0, one launch (start us, length us, event | category | flops | bytes accessed | tf_op | source)
XLA Modules:
  0.0 96.1 jit_solution(1165911629187564802)
XLA Ops:
  0.7 2.3 %fusion.2 = (bf16[1,144,2,2,128]{4,3,2,1,0:T(2,128)(2,1)}, bf16[1,144,2,2,128]{4,3,2,1,0:T(2,128)(2,1)}, bf16[1,144,2,2,128]{4,3,2,1,0:T(2,128)(2,1)S(1)}, bf16[1,144,2,2,128]{4,3,2,1,0:T(2,128)(2,1)S(1)}) fusion(bf16[4,144,2,2,128]{4,3,2,1,0:T(2,128)(2,1)} %bitcast.156), kind=kLoop, calls=%fused_computation.31 | loop fusion | bytes 1179648 | tf_op jit(solution)/shard_map/slice | solution.py:316
  7.2 1.7 %shard_map.148 = f32[576,128]{1,0:T(8,128)S(1)} custom-call(s32[2]{0:T(128)S(1)} %broadcast_5_sec_ref.2.sec_ref, bf16[1,576,128]{2,1,0:T(8,128)(2,1)S(1)} %bitcast.139, f32[8,128]{1,0:T(8,128)S(1)} %broadcast_in_dim.12.arrived_ref, f32[2,128]{1,0:T(2,128)S(1)} %bitcast.148, f32[2,128]{1,0:T(2,128)S(1)} %bitcast.152, bf16[2304,256]{1,0:T(8,128)(2,1)S(1)} %bitcast.117), custom_call_target="tpu_custom_call" | custom-call | bytes 6000000 | tf_op jit(solution)/shard_map/pallas_call | solution.py:261
  8.9 2.7 %collective-permute-start = (f32[576,128]{1,0:T(8,128)S(1)}, f32[576,128]{1,0:T(8,128)}, u32[]{:S(2)}, u32[]{:S(2)}) collective-permute-start(f32[576,128]{1,0:T(8,128)S(1)} %shard_map.148), channel_id=1, source_target_pairs={{0,8},{8,16},{16,24},{24,0},{1,9},{9,17},{17,25},{25,1},{2,10},{10... | collective-permute-start | bytes 884744 | tf_op jit(solution)/shard_map/ppermute | solution.py:372
  19.9 3.1 %shard_map.155 = (f32[576,128]{1,0:T(8,128)}, f32[576,128]{1,0:T(8,128)S(1)}) custom-call(s32[2]{0:T(128)S(1)} %pad_add_fusion.sec_ref, bf16[3,576,128]{2,1,0:T(8,128)(2,1)S(1)} %bitcast.121, f32[576,128]{1,0:T(8,128)} %collective-permute-done.3.arrived_ref, f32[288,256]{1,0:T(8,128)S(1)} %copy-done.21, f32[288,256]{1,0:T(8,128)S(1)} %copy-done.23, ...), custom_call_target="tpu_custom_call" | custom-call | bytes 6000000 | tf_op jit(solution)/shard_map/pallas_call | solution.py:261
  34.9 2.7 %shard_map.149 = f32[576,128]{1,0:T(8,128)S(1)} custom-call(s32[2]{0:T(128)S(1)} %copy-done.45, bf16[3,576,128]{2,1,0:T(8,128)(2,1)S(1)} %bitcast.124, f32[576,128]{1,0:T(8,128)} %collective-permute-done.arrived_ref, f32[2,128]{1,0:T(2,128)S(1)} %bitcast.149, f32[2,128]{1,0:T(2,128)S(1)} %bitcast.153, bf16[2304,256]{1,0:T(8,128)(2,1)S(1)} %bitcast.118), custom_call_target="tpu_custom_call" | custom-call | bytes 6000000 | tf_op jit(solution)/shard_map/pallas_call | solution.py:261
  37.8 2.4 %shard_map.157 = (f32[576,128]{1,0:T(8,128)S(1)}, f32[576,128]{1,0:T(8,128)S(1)}) custom-call(s32[2]{0:T(128)S(1)} %pad_add_fusion.1.sec_ref, bf16[3,576,128]{2,1,0:T(8,128)(2,1)S(1)} %bitcast.122, f32[576,128]{1,0:T(8,128)} %collective-permute-done.4.arrived_ref, f32[288,256]{1,0:T(8,128)S(1)} %copy-done.17, f32[288,256]{1,0:T(8,128)S(1)} %copy-done.19, ...), custom_call_target="tpu_custom_call" | custom-call | bytes 6000000 | tf_op jit(solution)/shard_map/pallas_call | solution.py:261
  41.0 2.8 %collective-permute-done.1.arrived_ref = f32[576,128]{1,0:T(8,128)S(1)} collective-permute-done((f32[576,128]{1,0:T(8,128)S(1)}, f32[576,128]{1,0:T(8,128)S(1)}, u32[]{:S(2)}, u32[]{:S(2)}) %collective-permute-start.1) | collective-permute-done | bytes 294944 | tf_op jit(solution)/shard_map/ppermute | solution.py:372
  43.8 1.7 %shard_map.150 = f32[576,128]{1,0:T(8,128)S(1)} custom-call(s32[2]{0:T(128)S(1)} %pad_add_fusion.1.sec_ref, bf16[3,576,128]{2,1,0:T(8,128)(2,1)S(1)} %bitcast.125, f32[576,128]{1,0:T(8,128)S(1)} %collective-permute-done.1.arrived_ref, f32[2,128]{1,0:T(2,128)S(1)} %bitcast.150, f32[2,128]{1,0:T(2,128)S(1)} %bitcast.154, bf16[2304,256]{1,0:T(8,128)(2,1)S(1)} %bitcast.119), custom_call_target="tpu_custom_call" | custom-call | bytes 6000000 | tf_op jit(solution)/shard_map/pallas_call | solution.py:261
  48.6 2.8 %shard_map.160 = (f32[8,288,128]{2,1,0:T(8,128)S(1)}, f32[8,288,128]{2,1,0:T(8,128)S(1)}) custom-call(s32[16]{0:T(128)S(1)} %pad_add_fusion.3.slot_ref, f32[576,128]{1,0:T(8,128)S(1)} %copy-done.9, f32[576,128]{1,0:T(8,128)S(1)} %copy-done.11, f32[576,128]{1,0:T(8,128)S(1)} %get-tuple-element.47.refs_2_, f32[576,128]{1,0:T(8,128)S(1)} %get-tuple-element.48.refs_3_, ...), custom_call_target="tpu_custom_call" | custom-call | bytes 12000000 | tf_op jit(solution)/shard_map/pallas_call | solution.py:241
  51.4 1.6 %collective-permute-start.6 = (f32[288,128]{1,0:T(8,128)S(1)}, f32[288,128]{1,0:T(8,128)S(1)}, u32[]{:S(2)}, u32[]{:S(2)}) collective-permute-start(f32[288,128]{1,0:T(8,128)S(1)} %slice_bitcast_fusion.1), channel_id=1, source_target_pairs={{0,2},{2,4},{4,6},{6,7},{7,5},{5,3},{3,1},{1,0},{8,10},{10,12},{12... | collective-permute-start | bytes 442376 | tf_op jit(solution)/shard_map/ppermute | solution.py:396
  53.7 2.5 %maximum_bitcast_fusion.1 = f32[4,1,2,12,12,256]{5,2,4,3,1,0:T(2,128)} fusion(f32[1,2,12,12,256]{4,1,3,2,0:T(2,128)S(1)} %bitcast.137, f32[1,2,12,12,256]{4,1,3,2,0:T(2,128)S(1)} %bitcast.136, f32[1,2,12,12,256]{4,1,3,2,0:T(2,128)} %bitcast.44, f32[1,2,12,12,256]{4,1,3,2,0:T(2,128)S(1)} %bitcast.135), kind=kLoop, calls=%fused_computation.1 | loop fusion | flops 884736 | bytes 2359296 | tf_op jit(solution)/shard_map/broadcast_in_dim | solution.py:401
  56.2 1.7 %shard_map.151 = f32[576,128]{1,0:T(8,128)S(1)} custom-call(s32[2]{0:T(128)S(1)} %pad_add_fusion.2.sec_ref, bf16[3,576,128]{2,1,0:T(8,128)(2,1)S(1)} %bitcast.126, f32[576,128]{1,0:T(8,128)S(1)} %collective-permute-done.2.arrived_ref, f32[2,128]{1,0:T(2,128)S(1)} %bitcast.151, f32[2,128]{1,0:T(2,128)S(1)} %bitcast.155, bf16[2304,256]{1,0:T(8,128)(2,1)S(1)} %bitcast.120), custom_call_target="tpu_custom_call" | custom-call | bytes 6000000 | tf_op jit(solution)/shard_map/pallas_call | solution.py:261
  59.5 1.6 %collective-permute-start.7 = (f32[288,128]{1,0:T(8,128)S(1)}, f32[288,128]{1,0:T(8,128)S(1)}, u32[]{:S(2)}, u32[]{:S(2)}) collective-permute-start(f32[288,128]{1,0:T(8,128)S(1)} %bitcast_add_fusion.13), channel_id=1, source_target_pairs={{0,2},{2,4},{4,6},{6,7},{7,5},{5,3},{3,1},{1,0},{8,10},{10,12},{12... | collective-permute-start | bytes 442376 | tf_op jit(solution)/shard_map/ppermute | solution.py:396
  61.7 3.0 %collective-permute-done.7 = f32[288,128]{1,0:T(8,128)S(1)} collective-permute-done((f32[288,128]{1,0:T(8,128)S(1)}, f32[288,128]{1,0:T(8,128)S(1)}, u32[]{:S(2)}, u32[]{:S(2)}) %collective-permute-start.7) | collective-permute-done | bytes 147488 | tf_op jit(solution)/shard_map/ppermute | solution.py:396
  64.7 1.6 %collective-permute-start.8 = (f32[288,128]{1,0:T(8,128)S(1)}, f32[288,128]{1,0:T(8,128)S(1)}, u32[]{:S(2)}, u32[]{:S(2)}) collective-permute-start(f32[288,128]{1,0:T(8,128)S(1)} %bitcast_add_fusion.12), channel_id=1, source_target_pairs={{0,2},{2,4},{4,6},{6,7},{7,5},{5,3},{3,1},{1,0},{8,10},{10,12},{12... | collective-permute-start | bytes 442376 | tf_op jit(solution)/shard_map/ppermute | solution.py:396
  66.9 3.8 %collective-permute-done.8 = f32[288,128]{1,0:T(8,128)S(1)} collective-permute-done((f32[288,128]{1,0:T(8,128)S(1)}, f32[288,128]{1,0:T(8,128)S(1)}, u32[]{:S(2)}, u32[]{:S(2)}) %collective-permute-start.8) | collective-permute-done | bytes 147488 | tf_op jit(solution)/shard_map/ppermute | solution.py:396
  70.7 1.6 %collective-permute-start.9 = (f32[288,128]{1,0:T(8,128)S(1)}, f32[288,128]{1,0:T(8,128)S(1)}, u32[]{:S(2)}, u32[]{:S(2)}) collective-permute-start(f32[288,128]{1,0:T(8,128)S(1)} %bitcast_add_fusion.11), channel_id=1, source_target_pairs={{0,2},{2,4},{4,6},{6,7},{7,5},{5,3},{3,1},{1,0},{8,10},{10,12},{12... | collective-permute-start | bytes 442376 | tf_op jit(solution)/shard_map/ppermute | solution.py:396
  73.2 4.2 %collective-permute-done.9 = f32[288,128]{1,0:T(8,128)S(1)} collective-permute-done((f32[288,128]{1,0:T(8,128)S(1)}, f32[288,128]{1,0:T(8,128)S(1)}, u32[]{:S(2)}, u32[]{:S(2)}) %collective-permute-start.9) | collective-permute-done | bytes 147488 | tf_op jit(solution)/shard_map/ppermute | solution.py:396
  77.5 1.6 %collective-permute-start.10 = (f32[288,128]{1,0:T(8,128)S(1)}, f32[288,128]{1,0:T(8,128)S(1)}, u32[]{:S(2)}, u32[]{:S(2)}) collective-permute-start(f32[288,128]{1,0:T(8,128)S(1)} %bitcast_add_fusion.10), channel_id=1, source_target_pairs={{0,2},{2,4},{4,6},{6,7},{7,5},{5,3},{3,1},{1,0},{8,10},{10,12},{12... | collective-permute-start | bytes 442376 | tf_op jit(solution)/shard_map/ppermute | solution.py:396
  79.6 3.7 %collective-permute-done.10 = f32[288,128]{1,0:T(8,128)S(1)} collective-permute-done((f32[288,128]{1,0:T(8,128)S(1)}, f32[288,128]{1,0:T(8,128)S(1)}, u32[]{:S(2)}, u32[]{:S(2)}) %collective-permute-start.10) | collective-permute-done | bytes 147488 | tf_op jit(solution)/shard_map/ppermute | solution.py:396
  85.5 3.0 %collective-permute-done.11 = f32[288,128]{1,0:T(8,128)S(1)} collective-permute-done((f32[288,128]{1,0:T(8,128)S(1)}, f32[288,128]{1,0:T(8,128)S(1)}, u32[]{:S(2)}, u32[]{:S(2)}) %collective-permute-start.11) | collective-permute-done | bytes 147488 | tf_op jit(solution)/shard_map/ppermute | solution.py:396
  88.5 1.6 %collective-permute-start.12 = (f32[288,128]{1,0:T(8,128)S(1)}, f32[288,128]{1,0:T(8,128)S(1)}, u32[]{:S(2)}, u32[]{:S(2)}) collective-permute-start(f32[288,128]{1,0:T(8,128)S(1)} %bitcast_add_fusion.8), channel_id=1, source_target_pairs={{0,2},{2,4},{4,6},{6,7},{7,5},{5,3},{3,1},{1,0},{8,10},{10,12},{12... | collective-permute-start | bytes 442376 | tf_op jit(solution)/shard_map/ppermute | solution.py:396
  90.7 3.0 %collective-permute-done.12 = f32[288,128]{1,0:T(8,128)S(1)} collective-permute-done((f32[288,128]{1,0:T(8,128)S(1)}, f32[288,128]{1,0:T(8,128)S(1)}, u32[]{:S(2)}, u32[]{:S(2)}) %collective-permute-start.12) | collective-permute-done | bytes 147488 | tf_op jit(solution)/shard_map/ppermute | solution.py:396
  93.8 1.6 %collective-permute-done.19 = f32[288,128]{1,0:T(8,128)S(1)} collective-permute-done((f32[288,128]{1,0:T(8,128)S(1)}, f32[288,128]{1,0:T(8,128)S(1)}, u32[]{:S(2)}, u32[]{:S(2)}) %collective-permute-start.19) | collective-permute-done | bytes 147488 | tf_op jit(solution)/shard_map/ppermute | solution.py:396
  (154 shorter events, 35.7 us)
Async XLA Ops:
  6.8 10.5 %copy-start.6 = (f32[576,128]{1,0:T(8,128)}, f32[576,128]{1,0:T(8,128)S(1)}, u32[]{:S(2)}) copy-start(f32[576,128]{1,0:T(8,128)S(1)} %get-tuple-element.32) | copy-start | bytes 884740
  6.8 10.5 %copy-start.2 = (bf16[3,2,12,12,256]{4,1,3,2,0:T(2,128)(2,1)S(1)}, bf16[3,2,12,12,256]{4,1,3,2,0:T(2,128)(2,1)}, u32[]{:S(2)}) copy-start(bf16[3,2,12,12,256]{4,1,3,2,0:T(2,128)(2,1)} %param.17) | copy-start | bytes 1327108
  6.8 10.5 %collective-permute-start.3 = (f32[576,128]{1,0:T(8,128)S(1)}, f32[576,128]{1,0:T(8,128)}, u32[]{:S(2)}, u32[]{:S(2)}) collective-permute-start(f32[576,128]{1,0:T(8,128)S(1)} %get-tuple-element.32), channel_id=1, source_target_pairs={{0,8},{8,16},{16,24},{24,0},{1,9},{9,17},{17,25},{25,1},{2,10},{10... | collective-permute-start | bytes 884744 | tf_op jit(solution)/shard_map/ppermute | solution.py:368
  8.9 25.3 %collective-permute-start = (f32[576,128]{1,0:T(8,128)S(1)}, f32[576,128]{1,0:T(8,128)}, u32[]{:S(2)}, u32[]{:S(2)}) collective-permute-start(f32[576,128]{1,0:T(8,128)S(1)} %shard_map.148), channel_id=1, source_target_pairs={{0,8},{8,16},{16,24},{24,0},{1,9},{9,17},{17,25},{25,1},{2,10},{10... | collective-permute-start | bytes 884744 | tf_op jit(solution)/shard_map/ppermute | solution.py:372
  19.9 7.4 %copy-start.4 = (bf16[1,144,2,2,128]{4,3,2,1,0:T(2,128)(2,1)S(1)}, bf16[1,144,2,2,128]{4,3,2,1,0:T(2,128)(2,1)}, u32[]{:S(2)}) copy-start(bf16[1,144,2,2,128]{4,3,2,1,0:T(2,128)(2,1)} %get-tuple-element.55) | copy-start | bytes 442372
  19.9 14.4 %copy-start.3 = (bf16[3,2,12,12,256]{4,1,3,2,0:T(2,128)(2,1)S(1)}, bf16[3,2,12,12,256]{4,1,3,2,0:T(2,128)(2,1)}, u32[]{:S(2)}) copy-start(bf16[3,2,12,12,256]{4,1,3,2,0:T(2,128)(2,1)} %param.14) | copy-start | bytes 1327108
  23.7 14.0 %collective-permute-start.4 = (f32[576,128]{1,0:T(8,128)}, f32[576,128]{1,0:T(8,128)}, u32[]{:S(2)}, u32[]{:S(2)}) collective-permute-start(f32[576,128]{1,0:T(8,128)} %get-tuple-element.36), channel_id=1, source_target_pairs={{0,8},{8,16},{16,24},{24,0},{1,9},{9,17},{17,25},{25,1},{2,10},{10... | collective-permute-start | bytes 884744 | tf_op jit(solution)/shard_map/ppermute | solution.py:368
  37.6 6.2 %collective-permute-start.1 = (f32[576,128]{1,0:T(8,128)S(1)}, f32[576,128]{1,0:T(8,128)S(1)}, u32[]{:S(2)}, u32[]{:S(2)}) collective-permute-start(f32[576,128]{1,0:T(8,128)S(1)} %shard_map.149), channel_id=1, source_target_pairs={{0,8},{8,16},{16,24},{24,0},{1,9},{9,17},{17,25},{25,1},{2,10},{10... | collective-permute-start | bytes 884744 | tf_op jit(solution)/shard_map/ppermute | solution.py:372
  40.2 6.8 %collective-permute-start.5 = (f32[576,128]{1,0:T(8,128)S(1)}, f32[576,128]{1,0:T(8,128)S(1)}, u32[]{:S(2)}, u32[]{:S(2)}) collective-permute-start(f32[576,128]{1,0:T(8,128)S(1)} %get-tuple-element.40), channel_id=1, source_target_pairs={{0,8},{8,16},{16,24},{24,0},{1,9},{9,17},{17,25},{25,1},{2,10},{10... | collective-permute-start | bytes 884744 | tf_op jit(solution)/shard_map/ppermute | solution.py:368
  45.6 10.7 %collective-permute-start.2 = (f32[576,128]{1,0:T(8,128)S(1)}, f32[576,128]{1,0:T(8,128)S(1)}, u32[]{:S(2)}, u32[]{:S(2)}) collective-permute-start(f32[576,128]{1,0:T(8,128)S(1)} %shard_map.150), channel_id=1, source_target_pairs={{0,8},{8,16},{16,24},{24,0},{1,9},{9,17},{17,25},{25,1},{2,10},{10... | collective-permute-start | bytes 884744 | tf_op jit(solution)/shard_map/ppermute | solution.py:372
  51.4 8.1 %collective-permute-start.6 = (f32[288,128]{1,0:T(8,128)S(1)}, f32[288,128]{1,0:T(8,128)S(1)}, u32[]{:S(2)}, u32[]{:S(2)}) collective-permute-start(f32[288,128]{1,0:T(8,128)S(1)} %slice_bitcast_fusion.1), channel_id=1, source_target_pairs={{0,2},{2,4},{4,6},{6,7},{7,5},{5,3},{3,1},{1,0},{8,10},{10,12},{12... | collective-permute-start | bytes 442376 | tf_op jit(solution)/shard_map/ppermute | solution.py:396
  53.0 8.1 %collective-permute-start.13 = (f32[288,128]{1,0:T(8,128)S(1)}, f32[288,128]{1,0:T(8,128)S(1)}, u32[]{:S(2)}, u32[]{:S(2)}) collective-permute-start(f32[288,128]{1,0:T(8,128)S(1)} %slice_bitcast_fusion), channel_id=1, source_target_pairs={{2,0},{4,2},{6,4},{7,6},{5,7},{3,5},{1,3},{0,1},{10,8},{12,10},{14... | collective-permute-start | bytes 442376 | tf_op jit(solution)/shard_map/ppermute | solution.py:396
  59.5 5.2 %collective-permute-start.7 = (f32[288,128]{1,0:T(8,128)S(1)}, f32[288,128]{1,0:T(8,128)S(1)}, u32[]{:S(2)}, u32[]{:S(2)}) collective-permute-start(f32[288,128]{1,0:T(8,128)S(1)} %bitcast_add_fusion.13), channel_id=1, source_target_pairs={{0,2},{2,4},{4,6},{6,7},{7,5},{5,3},{3,1},{1,0},{8,10},{10,12},{12... | collective-permute-start | bytes 442376 | tf_op jit(solution)/shard_map/ppermute | solution.py:396
  61.2 5.2 %collective-permute-start.14 = (f32[288,128]{1,0:T(8,128)S(1)}, f32[288,128]{1,0:T(8,128)S(1)}, u32[]{:S(2)}, u32[]{:S(2)}) collective-permute-start(f32[288,128]{1,0:T(8,128)S(1)} %bitcast_add_fusion.6), channel_id=1, source_target_pairs={{2,0},{4,2},{6,4},{7,6},{5,7},{3,5},{1,3},{0,1},{10,8},{12,10},{14... | collective-permute-start | bytes 442376 | tf_op jit(solution)/shard_map/ppermute | solution.py:396
  64.7 6.0 %collective-permute-start.8 = (f32[288,128]{1,0:T(8,128)S(1)}, f32[288,128]{1,0:T(8,128)S(1)}, u32[]{:S(2)}, u32[]{:S(2)}) collective-permute-start(f32[288,128]{1,0:T(8,128)S(1)} %bitcast_add_fusion.12), channel_id=1, source_target_pairs={{0,2},{2,4},{4,6},{6,7},{7,5},{5,3},{3,1},{1,0},{8,10},{10,12},{12... | collective-permute-start | bytes 442376 | tf_op jit(solution)/shard_map/ppermute | solution.py:396
  66.4 6.2 %collective-permute-start.15 = (f32[288,128]{1,0:T(8,128)S(1)}, f32[288,128]{1,0:T(8,128)S(1)}, u32[]{:S(2)}, u32[]{:S(2)}) collective-permute-start(f32[288,128]{1,0:T(8,128)S(1)} %bitcast_add_fusion.5), channel_id=1, source_target_pairs={{2,0},{4,2},{6,4},{7,6},{5,7},{3,5},{1,3},{0,1},{10,8},{12,10},{14... | collective-permute-start | bytes 442376 | tf_op jit(solution)/shard_map/ppermute | solution.py:396
  70.7 6.7 %collective-permute-start.9 = (f32[288,128]{1,0:T(8,128)S(1)}, f32[288,128]{1,0:T(8,128)S(1)}, u32[]{:S(2)}, u32[]{:S(2)}) collective-permute-start(f32[288,128]{1,0:T(8,128)S(1)} %bitcast_add_fusion.11), channel_id=1, source_target_pairs={{0,2},{2,4},{4,6},{6,7},{7,5},{5,3},{3,1},{1,0},{8,10},{10,12},{12... | collective-permute-start | bytes 442376 | tf_op jit(solution)/shard_map/ppermute | solution.py:396
  72.6 6.5 %collective-permute-start.16 = (f32[288,128]{1,0:T(8,128)S(1)}, f32[288,128]{1,0:T(8,128)S(1)}, u32[]{:S(2)}, u32[]{:S(2)}) collective-permute-start(f32[288,128]{1,0:T(8,128)S(1)} %bitcast_add_fusion.4), channel_id=1, source_target_pairs={{2,0},{4,2},{6,4},{7,6},{5,7},{3,5},{1,3},{0,1},{10,8},{12,10},{14... | collective-permute-start | bytes 442376 | tf_op jit(solution)/shard_map/ppermute | solution.py:396
  77.5 5.8 %collective-permute-start.10 = (f32[288,128]{1,0:T(8,128)S(1)}, f32[288,128]{1,0:T(8,128)S(1)}, u32[]{:S(2)}, u32[]{:S(2)}) collective-permute-start(f32[288,128]{1,0:T(8,128)S(1)} %bitcast_add_fusion.10), channel_id=1, source_target_pairs={{0,2},{2,4},{4,6},{6,7},{7,5},{5,3},{3,1},{1,0},{8,10},{10,12},{12... | collective-permute-start | bytes 442376 | tf_op jit(solution)/shard_map/ppermute | solution.py:396
  79.1 5.8 %collective-permute-start.17 = (f32[288,128]{1,0:T(8,128)S(1)}, f32[288,128]{1,0:T(8,128)S(1)}, u32[]{:S(2)}, u32[]{:S(2)}) collective-permute-start(f32[288,128]{1,0:T(8,128)S(1)} %bitcast_add_fusion.3), channel_id=1, source_target_pairs={{2,0},{4,2},{6,4},{7,6},{5,7},{3,5},{1,3},{0,1},{10,8},{12,10},{14... | collective-permute-start | bytes 442376 | tf_op jit(solution)/shard_map/ppermute | solution.py:396
  83.3 5.2 %collective-permute-start.11 = (f32[288,128]{1,0:T(8,128)S(1)}, f32[288,128]{1,0:T(8,128)S(1)}, u32[]{:S(2)}, u32[]{:S(2)}) collective-permute-start(f32[288,128]{1,0:T(8,128)S(1)} %bitcast_add_fusion.9), channel_id=1, source_target_pairs={{0,2},{2,4},{4,6},{6,7},{7,5},{5,3},{3,1},{1,0},{8,10},{10,12},{12... | collective-permute-start | bytes 442376 | tf_op jit(solution)/shard_map/ppermute | solution.py:396
  85.0 5.2 %collective-permute-start.18 = (f32[288,128]{1,0:T(8,128)S(1)}, f32[288,128]{1,0:T(8,128)S(1)}, u32[]{:S(2)}, u32[]{:S(2)}) collective-permute-start(f32[288,128]{1,0:T(8,128)S(1)} %bitcast_add_fusion.2), channel_id=1, source_target_pairs={{2,0},{4,2},{6,4},{7,6},{5,7},{3,5},{1,3},{0,1},{10,8},{12,10},{14... | collective-permute-start | bytes 442376 | tf_op jit(solution)/shard_map/ppermute | solution.py:396
  88.5 5.2 %collective-permute-start.12 = (f32[288,128]{1,0:T(8,128)S(1)}, f32[288,128]{1,0:T(8,128)S(1)}, u32[]{:S(2)}, u32[]{:S(2)}) collective-permute-start(f32[288,128]{1,0:T(8,128)S(1)} %bitcast_add_fusion.8), channel_id=1, source_target_pairs={{0,2},{2,4},{4,6},{6,7},{7,5},{5,3},{3,1},{1,0},{8,10},{10,12},{12... | collective-permute-start | bytes 442376 | tf_op jit(solution)/shard_map/ppermute | solution.py:396
  90.2 5.2 %collective-permute-start.19 = (f32[288,128]{1,0:T(8,128)S(1)}, f32[288,128]{1,0:T(8,128)S(1)}, u32[]{:S(2)}, u32[]{:S(2)}) collective-permute-start(f32[288,128]{1,0:T(8,128)S(1)} %bitcast_add_fusion.1), channel_id=1, source_target_pairs={{2,0},{4,2},{6,4},{7,6},{5,7},{3,5},{1,3},{0,1},{10,8},{12,10},{14... | collective-permute-start | bytes 442376 | tf_op jit(solution)/shard_map/ppermute | solution.py:396
  (44 other events, 108.8 us)

commit v2 on v1

--- a/solution.py
+++ b/solution.py
@@ -131,7 +131,7 @@
 
 
 def prep_kernel(d, saved_ref, gain_ref, bias_ref, slope_ref, normed_ref, rstd_ref, hidden_ref, tmp):
-    x = saved_ref[...].astype(F32)
+    x = saved_ref[0].astype(F32)
     normed, rstd = normalized(x, d)
     gain = pattern(gain_ref, d)
     a = normed * gain + pattern(bias_ref, d)
@@ -146,17 +146,40 @@
         ref[...] = from_interleaved(tmp, d).astype(ref.dtype)
 
 
-def entering(first, sec_ref, fresh_ref, arrived_ref):
+def entering(first, fresh_ref, arrived_ref):
     fresh = fresh_ref[0].astype(F32)
     if first:
         return fresh
-    return jnp.where(sec_ref[1] == 0, fresh, arrived_ref[...])
+    return jnp.where(lax.axis_index("section") == 0, fresh, arrived_ref[...])
+
+
+def keep(out_ref, all_ref, tick, sem):
+    copy = pltpu.make_async_copy(out_ref, all_ref.at[tick], sem)
+    copy.start()
+    copy.wait()
 
 
 def backward_kernel(
-    d, first, sec_ref, fresh_ref, arrived_ref, slope_ref, normed_ref, rstd_ref, weight_ref, out_ref, e_ref, left, mid, right, cols
+    d,
+    tick,
+    feed_ref,
+    fresh_ref,
+    arrived_ref,
+    slope_ref,
+    normed_ref,
+    rstd_ref,
+    weight_ref,
+    kept_ref,
+    out_ref,
+    e_ref,
+    all_ref,
+    left,
+    mid,
+    right,
+    cols,
+    sem,
 ):
-    e = entering(first, sec_ref, fresh_ref, arrived_ref)
+    e = entering(tick == 0, fresh_ref, arrived_ref)
     e_ref[...] = e
     spread(e, (left, mid, right), d)
     gather_patches((left, mid, right), cols, d)
@@ -188,12 +211,29 @@
             where = ct * d.n + n
             e_here = mid[pl.ds(d.pad * d.unit + where, d.pix, stride=d.unit), :]
             out_ref[pl.ds(where, d.pix, stride=d.unit), :] = value + e_here
+    keep(out_ref, all_ref, tick, sem)
 
 
 def forward_kernel(
-    d, first, sec_ref, fresh_ref, arrived_ref, gain_ref, bias_ref, weight_ref, out_ref, left, mid, right, cols, kept
+    d,
+    tick,
+    feed_ref,
+    fresh_ref,
+    arrived_ref,
+    gain_ref,
+    bias_ref,
+    weight_ref,
+    kept_ref,
+    out_ref,
+    all_ref,
+    left,
+    mid,
+    right,
+    cols,
+    kept,
+    sem,
 ):
-    x = entering(first, sec_ref, fresh_ref, arrived_ref)
+    x = entering(tick == 0, fresh_ref, arrived_ref)
     kept[...] = x
     normed, _ = normalized(x, d)
     a = normed * pattern(gain_ref, d) + pattern(bias_ref, d)
@@ -207,18 +247,22 @@
             out_ref[where, :] = (
                 kept[where, :] + conv[n * d.pix : (n + 1) * d.pix, ct * LANES : (ct + 1) * LANES]
             )
-
-
-def weight_kernel(d, ticks, chunk, factor, slot_ref, *refs):
+    keep(out_ref, all_ref, tick, sem)
+
+
+def weight_kernel(d, ticks, n, place, factor, *refs):
     e_refs, h_refs = refs[:ticks], refs[ticks : 2 * ticks]
-    up_ref, down_ref, left, mid, right, cols, hid = refs[2 * ticks :]
+    streams = refs[2 * ticks : 2 * ticks + 4]
+    left, mid, right, cols, hid = refs[2 * ticks + 4 :]
+    me = lax.axis_index("dp")
+    me = jnp.where(me % 2 == 0, me // 2, n - 1 - me // 2)
     rows = d.n * d.pix
+    chunk = 9 * d.c // n
     for t in range(ticks):
         spread(e_refs[t][...], (left, mid, right), d)
         gather_patches((left, mid, right), cols.at[t * rows : (t + 1) * rows], d)
         hid[t * rows : (t + 1) * rows, :] = h_refs[t][...]
     h = hid[...]
-    size = math.gcd(d.c, chunk)
     for tap in range(9):
         block = lax.dot_general(
             h, cols[:, (8 - tap) * d.c : (9 - tap) * d.c], (((0,), (0,)), ((), ())), preferred_element_type=F32
@@ -226,49 +270,40 @@
         at = tap * d.c
         while at < (tap + 1) * d.c:
             owner = at // chunk
-            stop = min((owner + 1) * chunk, (tap + 1) * d.c)
+            part = (at % chunk) // (chunk // 2)
+            start = owner * chunk + part * (chunk // 2)
+            stop = min(start + chunk // 2, (tap + 1) * d.c)
             piece = block[at - tap * d.c : stop - tap * d.c]
-            where = pl.ds(at - owner * chunk, stop - at)
-            up_ref[slot_ref[owner], where, :] = piece[:, :LANES]
-            down_ref[slot_ref[owner + 9 * d.c // chunk], where, :] = piece[:, LANES:]
+            where = pl.ds(at - start, stop - at)
+            up = (me - 1 - place[owner] + n) % n
+            down = (place[owner] - me - 1 + n) % n
+            streams[2 * part][up, where, :] = piece[:, :LANES]
+            streams[2 * part + 1][down, where, :] = piece[:, LANES:]
             at = stop
 
 
-def call(body, out_shape, scratch, cost, *operands):
-    smem = pl.BlockSpec(memory_space=pltpu.SMEM)
-    vmem = pl.BlockSpec(memory_space=pltpu.VMEM)
-    specs = [smem if o.dtype == jnp.int32 else vmem for o in operands]
+def cost(us):
+    return pl.CostEstimate(flops=0, bytes_accessed=int(us * 3.0e6), transcendentals=0)
+
+
+VMEM = pl.BlockSpec(memory_space=pltpu.VMEM)
+ANY = pl.BlockSpec(memory_space=pl.ANY)
+
+
+def call(body, out_shape, scratch, us, *operands, in_specs=None, out_specs=None, feed=None, alias=None):
+    in_specs = in_specs or [VMEM] * len(operands)
+    out_specs = out_specs or jax.tree.map(lambda _: VMEM, out_shape)
+    scalars = [] if feed is None else [feed]
     return pl.pallas_call(
         body,
         out_shape=out_shape,
-        in_specs=specs,
-        out_specs=jax.tree.map(lambda _: vmem, out_shape),
-        scratch_shapes=scratch,
+        grid_spec=pltpu.PrefetchScalarGridSpec(
+            num_scalar_prefetch=len(scalars), grid=(1,), in_specs=in_specs, out_specs=out_specs, scratch_shapes=scratch
+        ),
         compiler_params=pltpu.CompilerParams(vmem_limit_bytes=VMEM_LIMIT),
-        cost_estimate=cost,
-    )(*operands)
-
-
-def fed_call(body, out_shape, scratch, cost, sec, fresh, *operands):
-    vmem = pl.BlockSpec(memory_space=pltpu.VMEM)
-    grid_spec = pltpu.PrefetchScalarGridSpec(
-        num_scalar_prefetch=1,
-        grid=(1,),
-        in_specs=[pl.BlockSpec((1,) + fresh.shape[1:], lambda i, sec: (sec[0], 0, 0))] + [vmem] * len(operands),
-        out_specs=jax.tree.map(lambda _: vmem, out_shape),
-        scratch_shapes=scratch,
-    )
-    return pl.pallas_call(
-        body,
-        out_shape=out_shape,
-        grid_spec=grid_spec,
-        compiler_params=pltpu.CompilerParams(vmem_limit_bytes=VMEM_LIMIT),
-        cost_estimate=cost,
-    )(sec, fresh, *operands)
-
-
-def cost(us):
-    return pl.CostEstimate(flops=0, bytes_accessed=int(us * 3.0e6), transcendentals=0)
+        cost_estimate=cost(us),
+        input_output_aliases=alias or {},
+    )(*scalars, *operands)
 
 
 def shards(
@@ -287,7 +322,6 @@
 ):
     ticks = saved_inputs.shape[0]
     d = Dims(*saved_inputs.shape[2:])
-    section = lax.axis_index("section").astype(jnp.int32)
     sections = lax.axis_size("section")
     ring = [(i, (i + 1) % sections) for i in range(sections)]
 
@@ -296,78 +330,87 @@
     fresh_act = interleaved(fresh_images, d)
     fresh_grad = interleaved(fresh_gradients, d)
     saved = interleaved(saved_inputs[:, 0], d)
-    vectors = [
+    fgain, fbias, bgain, bbias = [
         v[0].reshape(d.cts, LANES) for v in (forward_gain, forward_bias, backward_gain, backward_bias)
     ]
-    fgain, fbias, bgain, bbias = vectors
 
     msg = jax.ShapeDtypeStruct((d.flat, LANES), F32)
+    every = jax.ShapeDtypeStruct((ticks, d.flat, LANES), F32)
     rows = d.n * d.pix
     wide = jax.ShapeDtypeStruct((rows, d.c), F32)
     padded = pltpu.VMEM((d.padded, LANES), F32)
     cols = pltpu.VMEM((rows, 9 * d.c), BF16)
+    flat = pltpu.VMEM((d.flat, LANES), F32)
+    sem = pltpu.SemaphoreType.DMA
+
+    def block(index):
+        return pl.BlockSpec((1, d.flat, LANES), index)
 
     def prep(t):
         return call(
             functools.partial(prep_kernel, d),
             (wide, wide, jax.ShapeDtypeStruct((8, LANES), F32), jax.ShapeDtypeStruct((rows, d.c), BF16)),
-            [pltpu.VMEM((d.flat, LANES), F32)],
-            cost(1.5),
-            saved[t],
+            [flat],
+            0.8,
+            saved,
             bgain,
             bbias,
-        )
-
-    def source(t, first_block, fresh):
-        if t == 0:
-            return jnp.zeros((2,), jnp.int32), first_block
-        return jnp.stack([feed_order[t - 1], section]), fresh
-
-    def backward(t, arrived, prepared):
-        sec, fresh = source(t, grad0, fresh_grad)
-        slope, normed, rstd, _ = prepared
-        return fed_call(
-            functools.partial(backward_kernel, d, t == 0),
+            in_specs=[block(lambda i: (t, 0, 0)), VMEM, VMEM],
+        )
+
+    def fed(t, body, outs, scratch, us, first, fresh, arrived, kept, *more):
+        index = (lambda i, feed: (0, 0, 0)) if t == 0 else (lambda i, feed: (feed[t - 1], 0, 0))
+        operands = [first if t == 0 else fresh, arrived, *more, kept]
+        return call(
+            functools.partial(body, d, t),
+            (*outs, every),
+            scratch,
+            us,
+            *operands,
+            in_specs=[block(index)] + [VMEM] * (len(operands) - 2) + [ANY],
+            out_specs=tuple([VMEM] * len(outs) + [ANY]),
+            feed=feed_order,
+            alias={} if t == 0 else {len(operands): len(outs)},
+        )
+
+    nothing = jnp.zeros((8, LANES), F32)
+    arrived, arrived_grad, emitted, returned = [nothing] * 4
+    entered, hidden = [], []
+    for t in range(ticks):
+        slope, normed, rstd, h = prep(t)
+        hidden.append(h)
+        grad_out, e, returned = fed(
+            t,
+            backward_kernel,
             (msg, msg),
-            [padded] * 3 + [cols],
-            cost(2.0),
-            sec,
-            fresh,
-            arrived,
+            [padded] * 3 + [cols, sem],
+            1.5,
+            grad0,
+            fresh_grad,
+            arrived_grad,
+            returned,
             slope,
             normed,
             rstd,
             backward_weight[0],
         )
-
-    def forward(t, arrived):
-        sec, fresh = source(t, act0, fresh_act)
-        return fed_call(
-            functools.partial(forward_kernel, d, t == 0),
-            msg,
-            [padded] * 3 + [cols, pltpu.VMEM((d.flat, LANES), F32)],
-            cost(2.0),
-            sec,
-            fresh,
+        entered.append(e)
+        if t < ticks - 1:
+            arrived_grad = lax.ppermute(grad_out, "section", ring)
+        act_out, emitted = fed(
+            t,
+            forward_kernel,
+            (msg,),
+            [padded] * 3 + [cols, flat, sem],
+            1.7,
+            act0,
+            fresh_act,
             arrived,
+            emitted,
             fgain,
             fbias,
             forward_weight[0],
         )
-
-    nothing = jnp.zeros((8, LANES), F32)
-    arrived, arrived_grad = nothing, nothing
-    emitted, returned, entered, hidden = [], [], [], []
-    for t in range(ticks):
-        prepared = prep(t)
-        hidden.append(prepared[3])
-        grad_out, e = backward(t, arrived_grad, prepared)
-        returned.append(grad_out)
-        entered.append(e)
-        if t < ticks - 1:
-            arrived_grad = lax.ppermute(grad_out, "section", ring)
-        act_out = forward(t, arrived)
-        emitted.append(act_out)
         if t < ticks - 1:
             arrived = lax.ppermute(act_out, "section", ring)
 
@@ -375,32 +418,25 @@
     order = list(range(0, n, 2)) + list(range(n - 1 - n % 2, 0, -2))
     place = [order.index(i) for i in range(n)]
     chunk = 9 * d.c // n
-    places = jnp.array(place, jnp.int32)
-    me = places[lax.axis_index("dp")]
-    slots = jnp.concatenate([(me - 1 - places) % n, (places - me - 1) % n])
-    factor = 1.0 / (n * d.n)
-    half = jax.ShapeDtypeStruct((n, chunk, LANES), F32)
-    up, down = call(
-        functools.partial(weight_kernel, d, ticks, chunk, factor),
-        (half, half),
+    half = jax.ShapeDtypeStruct((n, chunk // 2, LANES), F32)
+    streams = call(
+        functools.partial(weight_kernel, d, ticks, n, place, 1.0 / (n * d.n)),
+        (half,) * 4,
         [padded] * 3 + [pltpu.VMEM((ticks * rows, 9 * d.c), BF16), pltpu.VMEM((ticks * rows, d.c), BF16)],
-        cost(4.0),
-        slots,
+        2.7,
         *entered,
         *hidden,
     )
     onward = [(order[i], order[(i + 1) % n]) for i in range(n)]
     back = [(b, a) for a, b in onward]
-    a, b = up[0], down[0]
+    sums = [v[0] for v in streams]
     for s in range(1, n):
-        a, b = lax.ppermute(a, "dp", onward), lax.ppermute(b, "dp", back)
-        a, b = a + up[s], b + down[s]
-    shard_sum = jnp.concatenate([a, b], axis=1)
-    return (
-        jnp.stack([standard(v, d) for v in emitted])[:, None],
-        jnp.stack([standard(v, d) for v in returned])[:, None],
-        shard_sum[None],
+        for i in range(4):
+            sums[i] = lax.ppermute(sums[i], "dp", back if i % 2 else onward) + streams[i][s]
+    shard_sum = jnp.concatenate(
+        [jnp.concatenate(sums[:2], axis=1), jnp.concatenate(sums[2:], axis=1)], axis=0
     )
+    return standard(emitted, d)[:, None], standard(returned, d)[:, None], shard_sum[None]
 
 
 def solution(mesh):

time: 96.6 us -> 78.9 us (0.82)
  starting transfers between devices: 18.6 us -> 38.3 us
  waiting for transfers between devices: 26.8 us -> 7.64 us
  local copies, waits for them, and re-layouts: 18.6 us -> 5.31 us
  other arithmetic: 8.06 us -> 1.06 us
  Pallas kernels: 22.3 us -> 25.4 us
    ppermute x14 -> x28, waiting for transfers between devices: 22.7 us -> 6.04 us  [shards(): lax.ppermute(sums[i], 'dp', back if i % 2 else onward) + streams[i][s]]
    ppermute x14 -> x28, starting transfers between devices: 15.3 us -> 30.5 us  [shards(): lax.ppermute(sums[i], 'dp', back if i % 2 else onward) + streams[i][s]]
    unnamed x96 -> x28, local copies, waits for them, and re-layouts: 13.5 us -> 5.28 us
    ppermute x3, starting transfers between devices: 2.78 us -> 7.11 us  [shards(): arrived = lax.ppermute(act_out, 'section', ring)]
    broadcast_in_dim x2 -> x0, other arithmetic: 4.05 us -> none  [the longest x1 2.51 us: shards(): jnp.stack([standard(v, d) for v in returned])[:, None]]
    slice x2 -> x0, local copies, waits for them, and re-layouts: 3.76 us -> none  [the longest x1 2.34 us: prep(): saved[t]]
    pallas_call x13, Pallas kernels: 22.3 us -> 25.4 us  [call(): pl.pallas_call(body, out_shape=out_shape, grid_spec=pltpu.PrefetchScalarG...]
    ppermute x3, waiting for transfers between devices: 2.79 us -> 0.49 us  [shards(): arrived = lax.ppermute(act_out, 'section', ring)]
  transfers between devices with their start and end apart: 20 -> 34, of which waited for: 10 -> 17; matrix products, arithmetic and copies ran while one was open for 10% -> 0% of each run, Pallas kernels for 21% -> 28%
where the time goes in v2:
time: 78.9 us; the launch traced here: 78.7 us
  starting transfers between devices  38.3 us (49%)
  Pallas kernels  25.4 us (32%)
  waiting for transfers between devices  7.64 us (10%)
  local copies, waits for them, and re-layouts  5.31 us (7%)
  other arithmetic  1.06 us (1%)
  between operations  1 us (1%)
    ppermute x28, starting transfers between devices, shards(): lax.ppermute(sums[i], 'dp', back if i % 2 else onward) + streams[i][s]  30.5 us
    pallas_call x13, Pallas kernels, call(): pl.pallas_call(body, out_shape=out_shape, grid_spec=pltpu.PrefetchScalarG...  25.4 us
    ppermute x3, starting transfers between devices, shards(): arrived = lax.ppermute(act_out, 'section', ring)  7.11 us
    ppermute x28, waiting for transfers between devices, shards(): lax.ppermute(sums[i], 'dp', back if i % 2 else onward) + streams[i][s]  6.04 us
    unnamed x28, local copies, waits for them, and re-layouts  5.28 us
  transfers between devices with their start and end apart: 34, of which 17 were waited for; matrix products, arithmetic and copies ran while one was open for 0% of the time, Pallas kernels for 28%

profile of v2, /device:TPU:0, one launch (start us, length us, event | category | flops | bytes accessed | tf_op | source)
XLA Modules:
  0.0 78.7 jit_solution(9182986302849086301)
XLA Ops:
  6.8 2.2 %shard_map.144 = (f32[576,128]{1,0:T(8,128)S(1)}, f32[576,128]{1,0:T(8,128)S(1)}, f32[4,576,128]{2,1,0:T(8,128)}) custom-call(s32[3]{0:T(128)S(1)} %copy-done.9, bf16[1,576,128]{2,1,0:T(8,128)(2,1)S(1)} %bitcast.125, f32[8,128]{1,0:T(8,128)S(1)} %broadcast_in_dim.6.arrived_ref.kept_ref, f32[288,256]{1,0:T(8,128)S(1)} %get-tuple-element.48.slope_ref, ...), custom_call_target="tpu_custom_call" | custom-call | bytes 4500000 | tf_op jit(solution)/shard_map/pallas_call | solution.py:297
  9.5 2.4 %shard_map.139 = (f32[576,128]{1,0:T(8,128)S(1)}, f32[4,576,128]{2,1,0:T(8,128)}) custom-call(s32[3]{0:T(128)S(1)} %copy-done.9, bf16[1,576,128]{2,1,0:T(8,128)(2,1)S(1)} %bitcast.126, f32[8,128]{1,0:T(8,128)S(1)} %broadcast_in_dim.6.arrived_ref.kept_ref, f32[2,128]{1,0:T(2,128)S(1)} %bitcast.135, f32[2,128]{1,0:T(2,128)S(1)} %bitcast.139, ...), custom_call_target="tpu_custom_call" | custom-call | bytes 5100000 | tf_op jit(solution)/shard_map/pallas_call | solution.py:297
  11.9 2.6 %collective-permute-start = (f32[576,128]{1,0:T(8,128)S(1)}, f32[576,128]{1,0:T(8,128)S(1)}, u32[]{:S(2)}, u32[]{:S(2)}) collective-permute-start(f32[576,128]{1,0:T(8,128)S(1)} %get-tuple-element.41), channel_id=1, source_target_pairs={{0,8},{8,16},{16,24},{24,0},{1,9},{9,17},{17,25},{25,1},{2,10},{10... | collective-permute-start | bytes 884744 | tf_op jit(solution)/shard_map/ppermute | solution.py:415
  15.8 2.1 %shard_map.146 = (f32[576,128]{1,0:T(8,128)S(1)}, f32[576,128]{1,0:T(8,128)S(1)}, f32[4,576,128]{2,1,0:T(8,128)}) custom-call(s32[3]{0:T(128)S(1)} %copy-done.9, bf16[3,576,128]{2,1,0:T(8,128)(2,1)S(1)} %bitcast.119, f32[576,128]{1,0:T(8,128)S(1)} %collective-permute-done.3.arrived_ref, ...), custom_call_target="tpu_custom_call", output_to_operand_aliasing={{2}: (7, {})} | custom-call | bytes 4500000 | tf_op jit(solution)/shard_map/pallas_call | solution.py:297
  19.0 2.4 %shard_map.140 = (f32[576,128]{1,0:T(8,128)S(1)}, f32[4,576,128]{2,1,0:T(8,128)}) custom-call(s32[3]{0:T(128)S(1)} %copy-done.9, bf16[3,576,128]{2,1,0:T(8,128)(2,1)S(1)} %bitcast.122, f32[576,128]{1,0:T(8,128)S(1)} %collective-permute-done.arrived_ref, f32[2,128]{1,0:T(2,128)S(1)} %bitcast.136, ...), custom_call_target="tpu_custom_call", output_to_operand_aliasing={{1}: (6, {})} | custom-call | bytes 5100000 | tf_op jit(solution)/shard_map/pallas_call | solution.py:297
  21.4 2.4 %collective-permute-start.1 = (f32[576,128]{1,0:T(8,128)S(1)}, f32[576,128]{1,0:T(8,128)S(1)}, u32[]{:S(2)}, u32[]{:S(2)}) collective-permute-start(f32[576,128]{1,0:T(8,128)S(1)} %get-tuple-element.43), channel_id=1, source_target_pairs={{0,8},{8,16},{16,24},{24,0},{1,9},{9,17},{17,25},{25,1},{2,10},{10... | collective-permute-start | bytes 884744 | tf_op jit(solution)/shard_map/ppermute | solution.py:415
  24.2 2.1 %shard_map.148 = (f32[576,128]{1,0:T(8,128)S(1)}, f32[576,128]{1,0:T(8,128)S(1)}, f32[4,576,128]{2,1,0:T(8,128)}) custom-call(s32[3]{0:T(128)S(1)} %copy-done.9, bf16[3,576,128]{2,1,0:T(8,128)(2,1)S(1)} %bitcast.120, f32[576,128]{1,0:T(8,128)S(1)} %collective-permute-done.4.arrived_ref, ...), custom_call_target="tpu_custom_call", output_to_operand_aliasing={{2}: (7, {})} | custom-call | bytes 4500000 | tf_op jit(solution)/shard_map/pallas_call | solution.py:297
  27.6 2.4 %shard_map.141 = (f32[576,128]{1,0:T(8,128)S(1)}, f32[4,576,128]{2,1,0:T(8,128)}) custom-call(s32[3]{0:T(128)S(1)} %copy-done.9, bf16[3,576,128]{2,1,0:T(8,128)(2,1)S(1)} %bitcast.123, f32[576,128]{1,0:T(8,128)S(1)} %collective-permute-done.1.arrived_ref, f32[2,128]{1,0:T(2,128)S(1)} %bitcast.137, ...), custom_call_target="tpu_custom_call", output_to_operand_aliasing={{1}: (6, {})} | custom-call | bytes 5100000 | tf_op jit(solution)/shard_map/pallas_call | solution.py:297
  30.1 2.1 %collective-permute-start.2 = (f32[576,128]{1,0:T(8,128)S(1)}, f32[576,128]{1,0:T(8,128)S(1)}, u32[]{:S(2)}, u32[]{:S(2)}) collective-permute-start(f32[576,128]{1,0:T(8,128)S(1)} %get-tuple-element.45), channel_id=1, source_target_pairs={{0,8},{8,16},{16,24},{24,0},{1,9},{9,17},{17,25},{25,1},{2,10},{10... | collective-permute-start | bytes 884744 | tf_op jit(solution)/shard_map/ppermute | solution.py:415
  32.5 2.9 %shard_map.150 = (f32[576,128]{1,0:T(8,128)}, f32[576,128]{1,0:T(8,128)S(1)}, f32[4,576,128]{2,1,0:T(8,128)}) custom-call(s32[3]{0:T(128)S(1)} %copy-done.9, bf16[3,576,128]{2,1,0:T(8,128)(2,1)S(1)} %bitcast.121, f32[576,128]{1,0:T(8,128)S(1)} %collective-permute-done.5.arrived_ref, ...), custom_call_target="tpu_custom_call", output_to_operand_aliasing={{2}: (7, {})} | custom-call | bytes 4500000 | tf_op jit(solution)/shard_map/pallas_call | solution.py:297
  35.4 2.2 %shard_map.151 = (f32[8,144,128]{2,1,0:T(8,128)S(1)}, f32[8,144,128]{2,1,0:T(8,128)S(1)}, f32[8,144,128]{2,1,0:T(8,128)S(1)}, f32[8,144,128]{2,1,0:T(8,128)S(1)}) custom-call(f32[576,128]{1,0:T(8,128)S(1)} %get-tuple-element.67.refs_0_, f32[576,128]{1,0:T(8,128)S(1)} %get-tuple-element.68.refs_1_, f32[576,128]{1,0:T(8,128)S(1)} %get-tuple-element.69.refs_2_, ...), custom_call_target="tpu_custom_call" | custom-call | bytes 8100000 | tf_op jit(solution)/shard_map/pallas_call | solution.py:297
  37.7 2.4 %collective-permute-start.6 = (f32[144,128]{1,0:T(8,128)S(1)}, f32[144,128]{1,0:T(8,128)S(1)}, u32[]{:S(2)}, u32[]{:S(2)}) collective-permute-start(f32[144,128]{1,0:T(8,128)S(1)} %slice_bitcast_fusion.3), channel_id=1, source_target_pairs={{0,2},{2,4},{4,6},{6,7},{7,5},{5,3},{3,1},{1,0},{8,10},{10,12},{12... | collective-permute-start | bytes 221192 | tf_op jit(solution)/shard_map/ppermute | solution.py:435
  40.1 2.0 %collective-permute-start.20 = (f32[144,128]{1,0:T(8,128)S(1)}, f32[144,128]{1,0:T(8,128)S(1)}, u32[]{:S(2)}, u32[]{:S(2)}) collective-permute-start(f32[144,128]{1,0:T(8,128)S(1)} %slice_bitcast_fusion.1), channel_id=1, source_target_pairs={{0,2},{2,4},{4,6},{6,7},{7,5},{5,3},{3,1},{1,0},{8,10},{10,12},{12... | collective-permute-start | bytes 221192 | tf_op jit(solution)/shard_map/ppermute | solution.py:435
  42.2 3.2 %shard_map.142 = (f32[576,128]{1,0:T(8,128)}, f32[4,576,128]{2,1,0:T(8,128)}) custom-call(s32[3]{0:T(128)S(1)} %copy-done.9, bf16[3,576,128]{2,1,0:T(8,128)(2,1)S(1)} %bitcast.124, f32[576,128]{1,0:T(8,128)S(1)} %collective-permute-done.2.arrived_ref, f32[2,128]{1,0:T(2,128)S(1)} %bitcast.138, ...), custom_call_target="tpu_custom_call", output_to_operand_aliasing={{1}: (6, {})} | custom-call | bytes 5100000 | tf_op jit(solution)/shard_map/pallas_call | solution.py:297
  45.4 2.0 %collective-permute-start.7 = (f32[144,128]{1,0:T(8,128)S(1)}, f32[144,128]{1,0:T(8,128)S(1)}, u32[]{:S(2)}, u32[]{:S(2)}) collective-permute-start(f32[144,128]{1,0:T(8,128)S(1)} %bitcast_add_fusion.27), channel_id=1, source_target_pairs={{0,2},{2,4},{4,6},{6,7},{7,5},{5,3},{3,1},{1,0},{8,10},{10,12},{12... | collective-permute-start | bytes 221192 | tf_op jit(solution)/shard_map/ppermute | solution.py:435
  47.6 2.0 %collective-permute-start.21 = (f32[144,128]{1,0:T(8,128)S(1)}, f32[144,128]{1,0:T(8,128)S(1)}, u32[]{:S(2)}, u32[]{:S(2)}) collective-permute-start(f32[144,128]{1,0:T(8,128)S(1)} %bitcast_add_fusion.13), channel_id=1, source_target_pairs={{0,2},{2,4},{4,6},{6,7},{7,5},{5,3},{3,1},{1,0},{8,10},{10,12},{12... | collective-permute-start | bytes 221192 | tf_op jit(solution)/shard_map/ppermute | solution.py:435
  49.9 2.4 %collective-permute-start.8 = (f32[144,128]{1,0:T(8,128)S(1)}, f32[144,128]{1,0:T(8,128)S(1)}, u32[]{:S(2)}, u32[]{:S(2)}) collective-permute-start(f32[144,128]{1,0:T(8,128)S(1)} %bitcast_add_fusion.26), channel_id=1, source_target_pairs={{0,2},{2,4},{4,6},{6,7},{7,5},{5,3},{3,1},{1,0},{8,10},{10,12},{12... | collective-permute-start | bytes 221192 | tf_op jit(solution)/shard_map/ppermute | solution.py:435
  52.6 2.1 %collective-permute-start.22 = (f32[144,128]{1,0:T(8,128)S(1)}, f32[144,128]{1,0:T(8,128)S(1)}, u32[]{:S(2)}, u32[]{:S(2)}) collective-permute-start(f32[144,128]{1,0:T(8,128)S(1)} %bitcast_add_fusion.12), channel_id=1, source_target_pairs={{0,2},{2,4},{4,6},{6,7},{7,5},{5,3},{3,1},{1,0},{8,10},{10,12},{12... | collective-permute-start | bytes 221192 | tf_op jit(solution)/shard_map/ppermute | solution.py:435
  59.4 2.3 %collective-permute-start.10 = (f32[144,128]{1,0:T(8,128)S(1)}, f32[144,128]{1,0:T(8,128)S(1)}, u32[]{:S(2)}, u32[]{:S(2)}) collective-permute-start(f32[144,128]{1,0:T(8,128)S(1)} %bitcast_add_fusion.24), channel_id=1, source_target_pairs={{0,2},{2,4},{4,6},{6,7},{7,5},{5,3},{3,1},{1,0},{8,10},{10,12},{12... | collective-permute-start | bytes 221192 | tf_op jit(solution)/shard_map/ppermute | solution.py:435
  66.9 2.0 %collective-permute-start.25 = (f32[144,128]{1,0:T(8,128)S(1)}, f32[144,128]{1,0:T(8,128)S(1)}, u32[]{:S(2)}, u32[]{:S(2)}) collective-permute-start(f32[144,128]{1,0:T(8,128)S(1)} %bitcast_add_fusion.9), channel_id=1, source_target_pairs={{0,2},{2,4},{4,6},{6,7},{7,5},{5,3},{3,1},{1,0},{8,10},{10,12},{12... | collective-permute-start | bytes 221192 | tf_op jit(solution)/shard_map/ppermute | solution.py:435
  69.2 2.1 %collective-permute-start.12 = (f32[144,128]{1,0:T(8,128)S(1)}, f32[144,128]{1,0:T(8,128)S(1)}, u32[]{:S(2)}, u32[]{:S(2)}) collective-permute-start(f32[144,128]{1,0:T(8,128)S(1)} %bitcast_add_fusion.22), channel_id=1, source_target_pairs={{0,2},{2,4},{4,6},{6,7},{7,5},{5,3},{3,1},{1,0},{8,10},{10,12},{12... | collective-permute-start | bytes 221192 | tf_op jit(solution)/shard_map/ppermute | solution.py:435
  71.4 2.1 %collective-permute-start.26 = (f32[144,128]{1,0:T(8,128)S(1)}, f32[144,128]{1,0:T(8,128)S(1)}, u32[]{:S(2)}, u32[]{:S(2)}) collective-permute-start(f32[144,128]{1,0:T(8,128)S(1)} %bitcast_add_fusion.8), channel_id=1, source_target_pairs={{0,2},{2,4},{4,6},{6,7},{7,5},{5,3},{3,1},{1,0},{8,10},{10,12},{12... | collective-permute-start | bytes 221192 | tf_op jit(solution)/shard_map/ppermute | solution.py:435
  73.6 2.1 %collective-permute-done.19 = f32[144,128]{1,0:T(8,128)S(1)} collective-permute-done((f32[144,128]{1,0:T(8,128)S(1)}, f32[144,128]{1,0:T(8,128)S(1)}, u32[]{:S(2)}, u32[]{:S(2)}) %collective-permute-start.19) | collective-permute-done | bytes 73760 | tf_op jit(solution)/shard_map/ppermute | solution.py:435
  75.8 2.1 %collective-permute-done.33 = f32[144,128]{1,0:T(8,128)S(1)} collective-permute-done((f32[144,128]{1,0:T(8,128)S(1)}, f32[144,128]{1,0:T(8,128)S(1)}, u32[]{:S(2)}, u32[]{:S(2)}) %collective-permute-start.33) | collective-permute-done | bytes 73760 | tf_op jit(solution)/shard_map/ppermute | solution.py:435
  (119 shorter events, 23.0 us)
Async XLA Ops:
  9.0 6.8 %collective-permute-start.3 = (f32[576,128]{1,0:T(8,128)S(1)}, f32[576,128]{1,0:T(8,128)S(1)}, u32[]{:S(2)}, u32[]{:S(2)}) collective-permute-start(f32[576,128]{1,0:T(8,128)S(1)} %get-tuple-element.51), channel_id=1, source_target_pairs={{0,8},{8,16},{16,24},{24,0},{1,9},{9,17},{17,25},{25,1},{2,10},{10... | collective-permute-start | bytes 884744 | tf_op jit(solution)/shard_map/ppermute | solution.py:399
  11.9 7.0 %collective-permute-start = (f32[576,128]{1,0:T(8,128)S(1)}, f32[576,128]{1,0:T(8,128)S(1)}, u32[]{:S(2)}, u32[]{:S(2)}) collective-permute-start(f32[576,128]{1,0:T(8,128)S(1)} %get-tuple-element.41), channel_id=1, source_target_pairs={{0,8},{8,16},{16,24},{24,0},{1,9},{9,17},{17,25},{25,1},{2,10},{10... | collective-permute-start | bytes 884744 | tf_op jit(solution)/shard_map/ppermute | solution.py:415
  18.0 6.2 %collective-permute-start.4 = (f32[576,128]{1,0:T(8,128)S(1)}, f32[576,128]{1,0:T(8,128)S(1)}, u32[]{:S(2)}, u32[]{:S(2)}) collective-permute-start(f32[576,128]{1,0:T(8,128)S(1)} %get-tuple-element.56), channel_id=1, source_target_pairs={{0,8},{8,16},{16,24},{24,0},{1,9},{9,17},{17,25},{25,1},{2,10},{10... | collective-permute-start | bytes 884744 | tf_op jit(solution)/shard_map/ppermute | solution.py:399
  21.4 6.2 %collective-permute-start.1 = (f32[576,128]{1,0:T(8,128)S(1)}, f32[576,128]{1,0:T(8,128)S(1)}, u32[]{:S(2)}, u32[]{:S(2)}) collective-permute-start(f32[576,128]{1,0:T(8,128)S(1)} %get-tuple-element.43), channel_id=1, source_target_pairs={{0,8},{8,16},{16,24},{24,0},{1,9},{9,17},{17,25},{25,1},{2,10},{10... | collective-permute-start | bytes 884744 | tf_op jit(solution)/shard_map/ppermute | solution.py:415
  26.3 6.2 %collective-permute-start.5 = (f32[576,128]{1,0:T(8,128)S(1)}, f32[576,128]{1,0:T(8,128)S(1)}, u32[]{:S(2)}, u32[]{:S(2)}) collective-permute-start(f32[576,128]{1,0:T(8,128)S(1)} %get-tuple-element.61), channel_id=1, source_target_pairs={{0,8},{8,16},{16,24},{24,0},{1,9},{9,17},{17,25},{25,1},{2,10},{10... | collective-permute-start | bytes 884744 | tf_op jit(solution)/shard_map/ppermute | solution.py:399
  30.1 12.1 %collective-permute-start.2 = (f32[576,128]{1,0:T(8,128)S(1)}, f32[576,128]{1,0:T(8,128)S(1)}, u32[]{:S(2)}, u32[]{:S(2)}) collective-permute-start(f32[576,128]{1,0:T(8,128)S(1)} %get-tuple-element.45), channel_id=1, source_target_pairs={{0,8},{8,16},{16,24},{24,0},{1,9},{9,17},{17,25},{25,1},{2,10},{10... | collective-permute-start | bytes 884744 | tf_op jit(solution)/shard_map/ppermute | solution.py:415
  37.7 7.7 %collective-permute-start.6 = (f32[144,128]{1,0:T(8,128)S(1)}, f32[144,128]{1,0:T(8,128)S(1)}, u32[]{:S(2)}, u32[]{:S(2)}) collective-permute-start(f32[144,128]{1,0:T(8,128)S(1)} %slice_bitcast_fusion.3), channel_id=1, source_target_pairs={{0,2},{2,4},{4,6},{6,7},{7,5},{5,3},{3,1},{1,0},{8,10},{10,12},{12... | collective-permute-start | bytes 221192 | tf_op jit(solution)/shard_map/ppermute | solution.py:435
  40.1 7.3 %collective-permute-start.13 = (f32[144,128]{1,0:T(8,128)S(1)}, f32[144,128]{1,0:T(8,128)S(1)}, u32[]{:S(2)}, u32[]{:S(2)}) collective-permute-start(f32[144,128]{1,0:T(8,128)S(1)} %slice_bitcast_fusion.2), channel_id=1, source_target_pairs={{2,0},{4,2},{6,4},{7,6},{5,7},{3,5},{1,3},{0,1},{10,8},{12,10},{14... | collective-permute-start | bytes 221192 | tf_op jit(solution)/shard_map/ppermute | solution.py:435
  40.1 7.4 %collective-permute-start.20 = (f32[144,128]{1,0:T(8,128)S(1)}, f32[144,128]{1,0:T(8,128)S(1)}, u32[]{:S(2)}, u32[]{:S(2)}) collective-permute-start(f32[144,128]{1,0:T(8,128)S(1)} %slice_bitcast_fusion.1), channel_id=1, source_target_pairs={{0,2},{2,4},{4,6},{6,7},{7,5},{5,3},{3,1},{1,0},{8,10},{10,12},{12... | collective-permute-start | bytes 221192 | tf_op jit(solution)/shard_map/ppermute | solution.py:435
  42.1 7.4 %collective-permute-start.27 = (f32[144,128]{1,0:T(8,128)S(1)}, f32[144,128]{1,0:T(8,128)S(1)}, u32[]{:S(2)}, u32[]{:S(2)}) collective-permute-start(f32[144,128]{1,0:T(8,128)S(1)} %slice_bitcast_fusion), channel_id=1, source_target_pairs={{2,0},{4,2},{6,4},{7,6},{5,7},{3,5},{1,3},{0,1},{10,8},{12,10},{14... | collective-permute-start | bytes 221192 | tf_op jit(solution)/shard_map/ppermute | solution.py:435
  47.4 5.1 %collective-permute-start.14 = (f32[144,128]{1,0:T(8,128)S(1)}, f32[144,128]{1,0:T(8,128)S(1)}, u32[]{:S(2)}, u32[]{:S(2)}) collective-permute-start(f32[144,128]{1,0:T(8,128)S(1)} %bitcast_add_fusion.20), channel_id=1, source_target_pairs={{2,0},{4,2},{6,4},{7,6},{5,7},{3,5},{1,3},{0,1},{10,8},{12,10},{14... | collective-permute-start | bytes 221192 | tf_op jit(solution)/shard_map/ppermute | solution.py:435
  47.6 5.0 %collective-permute-start.21 = (f32[144,128]{1,0:T(8,128)S(1)}, f32[144,128]{1,0:T(8,128)S(1)}, u32[]{:S(2)}, u32[]{:S(2)}) collective-permute-start(f32[144,128]{1,0:T(8,128)S(1)} %bitcast_add_fusion.13), channel_id=1, source_target_pairs={{0,2},{2,4},{4,6},{6,7},{7,5},{5,3},{3,1},{1,0},{8,10},{10,12},{12... | collective-permute-start | bytes 221192 | tf_op jit(solution)/shard_map/ppermute | solution.py:435
  49.6 5.1 %collective-permute-start.28 = (f32[144,128]{1,0:T(8,128)S(1)}, f32[144,128]{1,0:T(8,128)S(1)}, u32[]{:S(2)}, u32[]{:S(2)}) collective-permute-start(f32[144,128]{1,0:T(8,128)S(1)} %bitcast_add_fusion.6), channel_id=1, source_target_pairs={{2,0},{4,2},{6,4},{7,6},{5,7},{3,5},{1,3},{0,1},{10,8},{12,10},{14... | collective-permute-start | bytes 221192 | tf_op jit(solution)/shard_map/ppermute | solution.py:435
  49.9 5.0 %collective-permute-start.8 = (f32[144,128]{1,0:T(8,128)S(1)}, f32[144,128]{1,0:T(8,128)S(1)}, u32[]{:S(2)}, u32[]{:S(2)}) collective-permute-start(f32[144,128]{1,0:T(8,128)S(1)} %bitcast_add_fusion.26), channel_id=1, source_target_pairs={{0,2},{2,4},{4,6},{6,7},{7,5},{5,3},{3,1},{1,0},{8,10},{10,12},{12... | collective-permute-start | bytes 221192 | tf_op jit(solution)/shard_map/ppermute | solution.py:435
  52.6 4.7 %collective-permute-start.22 = (f32[144,128]{1,0:T(8,128)S(1)}, f32[144,128]{1,0:T(8,128)S(1)}, u32[]{:S(2)}, u32[]{:S(2)}) collective-permute-start(f32[144,128]{1,0:T(8,128)S(1)} %bitcast_add_fusion.12), channel_id=1, source_target_pairs={{0,2},{2,4},{4,6},{6,7},{7,5},{5,3},{3,1},{1,0},{8,10},{10,12},{12... | collective-permute-start | bytes 221192 | tf_op jit(solution)/shard_map/ppermute | solution.py:435
  54.7 4.6 %collective-permute-start.29 = (f32[144,128]{1,0:T(8,128)S(1)}, f32[144,128]{1,0:T(8,128)S(1)}, u32[]{:S(2)}, u32[]{:S(2)}) collective-permute-start(f32[144,128]{1,0:T(8,128)S(1)} %bitcast_add_fusion.5), channel_id=1, source_target_pairs={{2,0},{4,2},{6,4},{7,6},{5,7},{3,5},{1,3},{0,1},{10,8},{12,10},{14... | collective-permute-start | bytes 221192 | tf_op jit(solution)/shard_map/ppermute | solution.py:435
  54.9 4.5 %collective-permute-start.9 = (f32[144,128]{1,0:T(8,128)S(1)}, f32[144,128]{1,0:T(8,128)S(1)}, u32[]{:S(2)}, u32[]{:S(2)}) collective-permute-start(f32[144,128]{1,0:T(8,128)S(1)} %bitcast_add_fusion.25), channel_id=1, source_target_pairs={{0,2},{2,4},{4,6},{6,7},{7,5},{5,3},{3,1},{1,0},{8,10},{10,12},{12... | collective-permute-start | bytes 221192 | tf_op jit(solution)/shard_map/ppermute | solution.py:435
  56.9 5.2 %collective-permute-start.16 = (f32[144,128]{1,0:T(8,128)S(1)}, f32[144,128]{1,0:T(8,128)S(1)}, u32[]{:S(2)}, u32[]{:S(2)}) collective-permute-start(f32[144,128]{1,0:T(8,128)S(1)} %bitcast_add_fusion.18), channel_id=1, source_target_pairs={{2,0},{4,2},{6,4},{7,6},{5,7},{3,5},{1,3},{0,1},{10,8},{12,10},{14... | collective-permute-start | bytes 221192 | tf_op jit(solution)/shard_map/ppermute | solution.py:435
  57.3 5.2 %collective-permute-start.23 = (f32[144,128]{1,0:T(8,128)S(1)}, f32[144,128]{1,0:T(8,128)S(1)}, u32[]{:S(2)}, u32[]{:S(2)}) collective-permute-start(f32[144,128]{1,0:T(8,128)S(1)} %bitcast_add_fusion.11), channel_id=1, source_target_pairs={{0,2},{2,4},{4,6},{6,7},{7,5},{5,3},{3,1},{1,0},{8,10},{10,12},{12... | collective-permute-start | bytes 221192 | tf_op jit(solution)/shard_map/ppermute | solution.py:435
  59.3 5.0 %collective-permute-start.30 = (f32[144,128]{1,0:T(8,128)S(1)}, f32[144,128]{1,0:T(8,128)S(1)}, u32[]{:S(2)}, u32[]{:S(2)}) collective-permute-start(f32[144,128]{1,0:T(8,128)S(1)} %bitcast_add_fusion.4), channel_id=1, source_target_pairs={{2,0},{4,2},{6,4},{7,6},{5,7},{3,5},{1,3},{0,1},{10,8},{12,10},{14... | collective-permute-start | bytes 221192 | tf_op jit(solution)/shard_map/ppermute | solution.py:435
  59.4 5.2 %collective-permute-start.10 = (f32[144,128]{1,0:T(8,128)S(1)}, f32[144,128]{1,0:T(8,128)S(1)}, u32[]{:S(2)}, u32[]{:S(2)}) collective-permute-start(f32[144,128]{1,0:T(8,128)S(1)} %bitcast_add_fusion.24), channel_id=1, source_target_pairs={{0,2},{2,4},{4,6},{6,7},{7,5},{5,3},{3,1},{1,0},{8,10},{10,12},{12... | collective-permute-start | bytes 221192 | tf_op jit(solution)/shard_map/ppermute | solution.py:435
  64.3 4.8 %collective-permute-start.31 = (f32[144,128]{1,0:T(8,128)S(1)}, f32[144,128]{1,0:T(8,128)S(1)}, u32[]{:S(2)}, u32[]{:S(2)}) collective-permute-start(f32[144,128]{1,0:T(8,128)S(1)} %bitcast_add_fusion.3), channel_id=1, source_target_pairs={{2,0},{4,2},{6,4},{7,6},{5,7},{3,5},{1,3},{0,1},{10,8},{12,10},{14... | collective-permute-start | bytes 221192 | tf_op jit(solution)/shard_map/ppermute | solution.py:435
  64.6 4.5 %collective-permute-start.11 = (f32[144,128]{1,0:T(8,128)S(1)}, f32[144,128]{1,0:T(8,128)S(1)}, u32[]{:S(2)}, u32[]{:S(2)}) collective-permute-start(f32[144,128]{1,0:T(8,128)S(1)} %bitcast_add_fusion.23), channel_id=1, source_target_pairs={{0,2},{2,4},{4,6},{6,7},{7,5},{5,3},{3,1},{1,0},{8,10},{10,12},{12... | collective-permute-start | bytes 221192 | tf_op jit(solution)/shard_map/ppermute | solution.py:435
  66.6 4.7 %collective-permute-start.18 = (f32[144,128]{1,0:T(8,128)S(1)}, f32[144,128]{1,0:T(8,128)S(1)}, u32[]{:S(2)}, u32[]{:S(2)}) collective-permute-start(f32[144,128]{1,0:T(8,128)S(1)} %bitcast_add_fusion.16), channel_id=1, source_target_pairs={{2,0},{4,2},{6,4},{7,6},{5,7},{3,5},{1,3},{0,1},{10,8},{12,10},{14... | collective-permute-start | bytes 221192 | tf_op jit(solution)/shard_map/ppermute | solution.py:435
  (24 other events, 96.1 us)

commit v3 on v2

--- a/solution.py
+++ b/solution.py
@@ -13,6 +13,7 @@
 BF16 = jnp.bfloat16
 LANES = 128
 VMEM_LIMIT = 24 * 1024 * 1024
+WHOLE_VMEM = 60 * 1024 * 1024
 
 
 class Dims:
@@ -130,13 +131,11 @@
         ref[pl.ds(ct * d.n + n, d.pix, stride=d.unit), :] = value[:, ct * LANES : (ct + 1) * LANES]
 
 
-def prep_kernel(d, saved_ref, gain_ref, bias_ref, slope_ref, normed_ref, rstd_ref, hidden_ref, tmp):
-    x = saved_ref[0].astype(F32)
+def prepare(d, x, gain_ref, bias_ref, slope_ref, normed_ref, hidden_ref, tmp):
     normed, rstd = normalized(x, d)
     gain = pattern(gain_ref, d)
     a = normed * gain + pattern(bias_ref, d)
     s = sigmoid(a)
-    rstd_ref[...] = rstd
     for ref, value in (
         (normed_ref, normed),
         (slope_ref, s * (1.0 + a * (1.0 - s)) * gain),
@@ -144,45 +143,17 @@
     ):
         tmp[...] = value.reshape(d.flat, LANES)
         ref[...] = from_interleaved(tmp, d).astype(ref.dtype)
-
-
-def entering(first, fresh_ref, arrived_ref):
-    fresh = fresh_ref[0].astype(F32)
-    if first:
-        return fresh
-    return jnp.where(lax.axis_index("section") == 0, fresh, arrived_ref[...])
-
-
-def keep(out_ref, all_ref, tick, sem):
-    copy = pltpu.make_async_copy(out_ref, all_ref.at[tick], sem)
-    copy.start()
-    copy.wait()
-
-
-def backward_kernel(
-    d,
-    tick,
-    feed_ref,
-    fresh_ref,
-    arrived_ref,
-    slope_ref,
-    normed_ref,
-    rstd_ref,
-    weight_ref,
-    kept_ref,
-    out_ref,
-    e_ref,
-    all_ref,
-    left,
-    mid,
-    right,
-    cols,
-    sem,
-):
-    e = entering(tick == 0, fresh_ref, arrived_ref)
-    e_ref[...] = e
-    spread(e, (left, mid, right), d)
-    gather_patches((left, mid, right), cols, d)
+    return rstd
+
+
+def prep_kernel(d, saved_ref, gain_ref, bias_ref, after_ref, slope_ref, normed_ref, rstd_ref, hidden_ref, tmp):
+    for k in range(slope_ref.shape[0]):
+        x = saved_ref[k + 1].astype(F32)
+        refs = [r.at[k] for r in (slope_ref, normed_ref, hidden_ref)]
+        rstd_ref[k] = prepare(d, x, gain_ref, bias_ref, *refs, tmp)
+
+
+def through_layer(d, cols, weight_ref, slope_ref, normed_ref, rstd_at, mid, out_ref):
     grad = None
     for tap in range(9):
         part = lax.dot_general(
@@ -204,36 +175,61 @@
     sums = group_sum(jnp.concatenate(rows, axis=0), d.c // GROUPS) * (1.0 / d.count)
     for n in range(d.n):
         for ct in range(d.cts):
-            k = (ct * d.n + n) * 2
+            where = ct * d.n + n
+            k = where * 2
             here = (slice(n * d.pix, (n + 1) * d.pix), slice(ct * LANES, (ct + 1) * LANES))
-            rstd = rstd_ref[ct * d.n + n : ct * d.n + n + 1, :]
-            value = (through[here] - sums[k : k + 1] - normed_ref[here] * sums[k + 1 : k + 2]) * rstd
-            where = ct * d.n + n
+            value = (through[here] - sums[k : k + 1] - normed_ref[here] * sums[k + 1 : k + 2]) * rstd_at(where)
             e_here = mid[pl.ds(d.pad * d.unit + where, d.pix, stride=d.unit), :]
             out_ref[pl.ds(where, d.pix, stride=d.unit), :] = value + e_here
-    keep(out_ref, all_ref, tick, sem)
-
-
-def forward_kernel(
-    d,
-    tick,
-    feed_ref,
-    fresh_ref,
-    arrived_ref,
-    gain_ref,
-    bias_ref,
-    weight_ref,
-    kept_ref,
-    out_ref,
-    all_ref,
-    left,
-    mid,
-    right,
-    cols,
-    kept,
-    sem,
+
+
+def first_kernel(d, feed_ref, saved_hbm, grad_hbm, gain_hbm, bias_hbm, weight_hbm, fresh_act_hbm, fresh_grad_hbm, *refs):
+    out_ref, e_ref, hidden_ref, acts_ref, grads_ref = refs[:5]
+    saved, grad, gain, bias, weight, slope, normed, tmp, left, mid, right, cols, sems = refs[5:]
+    pairs = [(grad_hbm.at[0], grad), (saved_hbm.at[0], saved), (gain_hbm, gain), (bias_hbm, bias), (weight_hbm, weight)]
+    for src, dst in ((fresh_act_hbm, acts_ref), (fresh_grad_hbm, grads_ref)):
+        for k in range(feed_ref.shape[0]):
+            pairs.append((src.at[feed_ref[k]], dst.at[k]))
+    copies = [pltpu.make_async_copy(src, dst, sems.at[i]) for i, (src, dst) in enumerate(pairs)]
+    for copy in copies:
+        copy.start()
+    copies[0].wait()
+    e = grad[...].astype(F32)
+    e_ref[...] = e
+    spread(e, (left, mid, right), d)
+    gather_patches((left, mid, right), cols, d)
+    for copy in copies[1:4]:
+        copy.wait()
+    rstd = prepare(d, saved[...].astype(F32), gain, bias, slope, normed, hidden_ref, tmp)
+    copies[4].wait()
+    through_layer(d, cols, weight, slope, normed, lambda i: rstd[i : i + 1, :], mid, out_ref)
+    for copy in copies[5:]:
+        copy.wait()
+
+
+def backward_kernel(
+    d, tick, grads_ref, arrived_ref, slope_ref, normed_ref, rstd_ref, weight_ref, after_ref, out_ref, e_ref, left, mid, right, cols
 ):
-    x = entering(tick == 0, fresh_ref, arrived_ref)
+    k = tick - 1
+    e = jnp.where(lax.axis_index("section") == 0, grads_ref[k].astype(F32), arrived_ref[...])
+    e_ref[...] = e
+    spread(e, (left, mid, right), d)
+    gather_patches((left, mid, right), cols, d)
+    through_layer(
+        d, cols, weight_ref, slope_ref.at[k], normed_ref.at[k], lambda i: rstd_ref[k, i : i + 1, :], mid, out_ref
+    )
+
+
+def forward_kernel(d, tick, last, fresh_ref, arrived_ref, grad_ref, act_ref, gain_ref, bias_ref, weight_ref, *refs):
+    out_ref, emitted_ref, returned_ref, left, mid, right, cols, kept, sems = refs[3:]
+    stores = [pltpu.make_async_copy(grad_ref, returned_ref.at[tick], sems.at[0])]
+    if tick > 0:
+        stores.append(pltpu.make_async_copy(act_ref, emitted_ref.at[tick - 1], sems.at[1]))
+    for store in stores:
+        store.start()
+    x = fresh_ref[max(tick - 1, 0)].astype(F32)
+    if tick > 0:
+        x = jnp.where(lax.axis_index("section") == 0, x, arrived_ref[...])
     kept[...] = x
     normed, _ = normalized(x, d)
     a = normed * pattern(gain_ref, d) + pattern(bias_ref, d)
@@ -247,21 +243,41 @@
             out_ref[where, :] = (
                 kept[where, :] + conv[n * d.pix : (n + 1) * d.pix, ct * LANES : (ct + 1) * LANES]
             )
-    keep(out_ref, all_ref, tick, sem)
-
-
-def weight_kernel(d, ticks, n, place, factor, *refs):
-    e_refs, h_refs = refs[:ticks], refs[ticks : 2 * ticks]
-    streams = refs[2 * ticks : 2 * ticks + 4]
-    left, mid, right, cols, hid = refs[2 * ticks + 4 :]
+    if last:
+        stores.append(pltpu.make_async_copy(out_ref, emitted_ref.at[tick], sems.at[2]))
+        stores[-1].start()
+    for store in stores:
+        store.wait()
+
+
+def slot(owner, me, order):
+    differ = jnp.bitwise_xor(me, owner)
+    out = 0
+    for bit in order:
+        out = out * 2 + jnp.bitwise_and(lax.shift_right_logical(differ, bit), 1)
+    return out
+
+
+def weight_kernel(d, ticks, n, orders, factor, *refs):
+    added = ticks == 0
+    if added:
+        grads_ref, arrived_ref, hid = refs[0], refs[1], refs[2].at[refs[2].shape[0] - 1]
+        before, streams = refs[3:7], refs[7:11]
+        left, mid, right, cols = refs[11:]
+        section = lax.axis_index("section")
+        entered = [jnp.where(section == 0, grads_ref[grads_ref.shape[0] - 1].astype(F32), arrived_ref[...])]
+    else:
+        entered = [ref[...] for ref in refs[:ticks]]
+        streams = refs[ticks + 2 : ticks + 6]
+        left, mid, right, cols, hid = refs[ticks + 6 :]
     me = lax.axis_index("dp")
-    me = jnp.where(me % 2 == 0, me // 2, n - 1 - me // 2)
     rows = d.n * d.pix
     chunk = 9 * d.c // n
-    for t in range(ticks):
-        spread(e_refs[t][...], (left, mid, right), d)
+    for t, e in enumerate(entered):
+        spread(e, (left, mid, right), d)
         gather_patches((left, mid, right), cols.at[t * rows : (t + 1) * rows], d)
-        hid[t * rows : (t + 1) * rows, :] = h_refs[t][...]
+        if not added:
+            hid[t * rows : (t + 1) * rows, :] = refs[ticks][...] if t == 0 else refs[ticks + 1][t - 1]
     h = hid[...]
     for tap in range(9):
         block = lax.dot_general(
@@ -273,12 +289,13 @@
             part = (at % chunk) // (chunk // 2)
             start = owner * chunk + part * (chunk // 2)
             stop = min(start + chunk // 2, (tap + 1) * d.c)
-            piece = block[at - tap * d.c : stop - tap * d.c]
             where = pl.ds(at - start, stop - at)
-            up = (me - 1 - place[owner] + n) % n
-            down = (place[owner] - me - 1 + n) % n
-            streams[2 * part][up, where, :] = piece[:, :LANES]
-            streams[2 * part + 1][down, where, :] = piece[:, LANES:]
+            slots = [slot(owner, me, order) for order in orders]
+            for way in range(2):
+                piece = block[at - tap * d.c : stop - tap * d.c, way * LANES : (way + 1) * LANES]
+                if added:
+                    piece = piece + before[2 * part + way][slots[way], where, :]
+                streams[2 * part + way][slots[way], where, :] = piece
             at = stop
 
 
@@ -287,23 +304,22 @@
 
 
 VMEM = pl.BlockSpec(memory_space=pltpu.VMEM)
+HBM = pl.BlockSpec(memory_space=pltpu.HBM)
+SMEM = pl.BlockSpec(memory_space=pltpu.SMEM)
 ANY = pl.BlockSpec(memory_space=pl.ANY)
 
 
-def call(body, out_shape, scratch, us, *operands, in_specs=None, out_specs=None, feed=None, alias=None):
-    in_specs = in_specs or [VMEM] * len(operands)
-    out_specs = out_specs or jax.tree.map(lambda _: VMEM, out_shape)
-    scalars = [] if feed is None else [feed]
+def call(body, out_shape, scratch, us, *operands, in_specs=None, out_specs=None, alias=None, vmem=VMEM_LIMIT):
     return pl.pallas_call(
         body,
         out_shape=out_shape,
-        grid_spec=pltpu.PrefetchScalarGridSpec(
-            num_scalar_prefetch=len(scalars), grid=(1,), in_specs=in_specs, out_specs=out_specs, scratch_shapes=scratch
-        ),
-        compiler_params=pltpu.CompilerParams(vmem_limit_bytes=VMEM_LIMIT),
+        in_specs=in_specs or [VMEM] * len(operands),
+        out_specs=out_specs or jax.tree.map(lambda _: VMEM, out_shape),
+        scratch_shapes=scratch,
+        compiler_params=pltpu.CompilerParams(vmem_limit_bytes=vmem),
         cost_estimate=cost(us),
         input_output_aliases=alias or {},
-    )(*scalars, *operands)
+    )(*operands)
 
 
 def shards(
@@ -343,99 +359,140 @@
     flat = pltpu.VMEM((d.flat, LANES), F32)
     sem = pltpu.SemaphoreType.DMA
 
-    def block(index):
-        return pl.BlockSpec((1, d.flat, LANES), index)
-
-    def prep(t):
+    whole = pltpu.VMEM((rows, d.c), F32)
+    vector = pltpu.VMEM((d.cts, LANES), F32)
+    narrow = jax.ShapeDtypeStruct((rows, d.c), BF16)
+    raw = pltpu.VMEM((d.flat, LANES), BF16)
+
+    last = ticks - 1
+
+    def later(shape, dtype):
+        return jax.ShapeDtypeStruct((last, *shape), dtype)
+
+    def first():
+        entering = later((d.flat, LANES), BF16)
+        return call(
+            functools.partial(first_kernel, d),
+            (msg, msg, narrow, entering, entering),
+            [raw, raw, vector, vector, pltpu.VMEM(backward_weight.shape[1:], BF16), whole, whole, flat]
+            + [padded] * 3
+            + [cols, sem((5 + 2 * last,))],
+            2.5,
+            feed_order,
+            saved,
+            grad0,
+            bgain,
+            bbias,
+            backward_weight[0],
+            fresh_act,
+            fresh_grad,
+            in_specs=[SMEM] + [HBM] * 7,
+            vmem=WHOLE_VMEM,
+        )
+
+    def prep(after):
         return call(
             functools.partial(prep_kernel, d),
-            (wide, wide, jax.ShapeDtypeStruct((8, LANES), F32), jax.ShapeDtypeStruct((rows, d.c), BF16)),
+            (later((rows, d.c), F32), later((rows, d.c), F32), later((8, LANES), F32), later((rows, d.c), BF16)),
             [flat],
-            0.8,
+            0.7 * last,
             saved,
             bgain,
             bbias,
-            in_specs=[block(lambda i: (t, 0, 0)), VMEM, VMEM],
-        )
-
-    def fed(t, body, outs, scratch, us, first, fresh, arrived, kept, *more):
-        index = (lambda i, feed: (0, 0, 0)) if t == 0 else (lambda i, feed: (feed[t - 1], 0, 0))
-        operands = [first if t == 0 else fresh, arrived, *more, kept]
+            after,
+            in_specs=[VMEM] * 3 + [ANY],
+        )
+
+    def backward(t, arrived, after):
+        slope, normed, rstd, _ = prepared
         return call(
-            functools.partial(body, d, t),
-            (*outs, every),
-            scratch,
-            us,
-            *operands,
-            in_specs=[block(index)] + [VMEM] * (len(operands) - 2) + [ANY],
-            out_specs=tuple([VMEM] * len(outs) + [ANY]),
-            feed=feed_order,
-            alias={} if t == 0 else {len(operands): len(outs)},
-        )
-
-    nothing = jnp.zeros((8, LANES), F32)
-    arrived, arrived_grad, emitted, returned = [nothing] * 4
-    entered, hidden = [], []
-    for t in range(ticks):
-        slope, normed, rstd, h = prep(t)
-        hidden.append(h)
-        grad_out, e, returned = fed(
-            t,
-            backward_kernel,
+            functools.partial(backward_kernel, d, t),
             (msg, msg),
-            [padded] * 3 + [cols, sem],
-            1.5,
-            grad0,
-            fresh_grad,
-            arrived_grad,
-            returned,
+            [padded] * 3 + [cols],
+            0.9,
+            grads,
+            arrived,
             slope,
             normed,
             rstd,
             backward_weight[0],
-        )
-        entered.append(e)
-        if t < ticks - 1:
-            arrived_grad = lax.ppermute(grad_out, "section", ring)
-        act_out, emitted = fed(
-            t,
-            forward_kernel,
-            (msg,),
-            [padded] * 3 + [cols, flat, sem],
-            1.7,
-            act0,
-            fresh_act,
+            after,
+            in_specs=[VMEM] * 6 + [ANY],
+        )
+
+    def forward(t, arrived, grad_out, act_out, after, emitted, returned):
+        return call(
+            functools.partial(forward_kernel, d, t, t == last),
+            (msg, every, every),
+            [padded] * 3 + [cols, flat, sem((3,))],
+            1.3,
+            acts if t else act0,
             arrived,
-            emitted,
+            grad_out,
+            act_out,
             fgain,
             fbias,
             forward_weight[0],
-        )
-        if t < ticks - 1:
-            arrived = lax.ppermute(act_out, "section", ring)
+            after,
+            emitted,
+            returned,
+            in_specs=[VMEM] * 7 + [ANY] * 3,
+            out_specs=(VMEM, ANY, ANY),
+            alias={8: 1, 9: 2} if t else {},
+        )
 
     n = lax.axis_size("dp")
-    order = list(range(0, n, 2)) + list(range(n - 1 - n % 2, 0, -2))
-    place = [order.index(i) for i in range(n)]
+    bits = n.bit_length() - 1
+    orders = (tuple(range(bits)), (1, 0, *range(2, bits)))
     chunk = 9 * d.c // n
     half = jax.ShapeDtypeStruct((n, chunk // 2, LANES), F32)
-    streams = call(
-        functools.partial(weight_kernel, d, ticks, n, place, 1.0 / (n * d.n)),
-        (half,) * 4,
-        [padded] * 3 + [pltpu.VMEM((ticks * rows, 9 * d.c), BF16), pltpu.VMEM((ticks * rows, d.c), BF16)],
-        2.7,
-        *entered,
-        *hidden,
-    )
-    onward = [(order[i], order[(i + 1) % n]) for i in range(n)]
-    back = [(b, a) for a, b in onward]
-    sums = [v[0] for v in streams]
-    for s in range(1, n):
-        for i in range(4):
-            sums[i] = lax.ppermute(sums[i], "dp", back if i % 2 else onward) + streams[i][s]
-    shard_sum = jnp.concatenate(
-        [jnp.concatenate(sums[:2], axis=1), jnp.concatenate(sums[2:], axis=1)], axis=0
-    )
+
+    def weight_terms(ticks, *operands):
+        count = max(ticks, 1)
+        return call(
+            functools.partial(weight_kernel, d, ticks, n, orders, 1.0 / (n * d.n)),
+            (half,) * 4,
+            [padded] * 3
+            + [pltpu.VMEM((count * rows, 9 * d.c), BF16)]
+            + ([pltpu.VMEM((ticks * rows, d.c), BF16)] if ticks else []),
+            0.6 * count,
+            *operands,
+            alias={} if ticks else {3 + i: i for i in range(4)},
+        )
+
+    nothing = jnp.zeros((8, LANES), F32)
+    grad_out, e, h, acts, grads = first()
+    arrived, act_out, emitted, returned = [nothing] * 4
+    entered = [e]
+    prepared = prep(grad_out)
+    for t in range(last):
+        if t > 0:
+            grad_out, e = backward(t, arrived_grad, nothing)
+            entered.append(e)
+        arrived_grad = lax.ppermute(grad_out, "section", ring)
+        after = prepared[2] if t == 0 else nothing
+        act_out, emitted, returned = forward(t, arrived, grad_out, act_out, after, emitted, returned)
+        arrived = lax.ppermute(act_out, "section", ring)
+    before = weight_terms(last, *entered, h, prepared[3])
+    streams = weight_terms(0, grads, arrived_grad, prepared[3], *before)
+
+    def exchange(held, bit):
+        half = held.shape[0] // 2
+        return held[:half] + lax.ppermute(held[half:], "dp", [(i, i ^ (1 << bit)) for i in range(n)])
+
+    done = []
+    for part in range(2):
+        held = [streams[2 * part], streams[2 * part + 1]]
+        for i in range(2):
+            held = [exchange(v, order[i]) for v, order in zip(held, orders)]
+        both = jnp.concatenate(held, axis=2)
+        for bit in range(2, bits):
+            both = exchange(both, bit)
+        done.append(both[0])
+        if part == 0:
+            grad_out, _ = backward(last, arrived_grad, held[0])
+            act_out, emitted, returned = forward(last, arrived, grad_out, act_out, nothing, emitted, returned)
+    shard_sum = jnp.concatenate(done, axis=0)
     return standard(emitted, d)[:, None], standard(returned, d)[:, None], shard_sum[None]
 
 

time: 78.9 us -> 66.4 us (0.84)
  starting transfers between devices: 38.3 us -> 23.9 us
  waiting for transfers between devices: 7.64 us -> 20.7 us
  Pallas kernels: 25.4 us -> 18.3 us
  local copies, waits for them, and re-layouts: 5.31 us -> 1.39 us
    ppermute x28 -> x10, starting transfers between devices: 30.5 us -> 20.4 us  [exchange(): lax.ppermute(held[half:], 'dp', [(i, i ^ 1 << bit) for i in range(n)])]
    pallas_call x13 -> x11, Pallas kernels: 25.4 us -> 18.3 us  [call(): pl.pallas_call(body, out_shape=out_shape, in_specs=in_specs or [VMEM] * l...]
    ppermute x3, waiting for transfers between devices: 1.12 us -> 7.13 us  [shards(): arrived_grad = lax.ppermute(grad_out, 'section', ring)]
    ppermute x28 -> x10, waiting for transfers between devices: 6.04 us -> 11.3 us  [exchange(): lax.ppermute(held[half:], 'dp', [(i, i ^ 1 << bit) for i in range(n)])]
    ppermute x3, starting transfers between devices: 7.11 us -> 2.87 us  [shards(): arrived = lax.ppermute(act_out, 'section', ring)]
    unnamed x28 -> x26, local copies, waits for them, and re-layouts: 5.28 us -> 1.26 us
    ppermute x3, waiting for transfers between devices: 0.49 us -> 2.21 us  [shards(): arrived = lax.ppermute(act_out, 'section', ring)]
  transfers between devices with their start and end apart: 34 -> 16, of which waited for: 17 -> 10; matrix products, arithmetic and copies ran while one was open for 0% -> 1% of each run, Pallas kernels for 28% -> 19%
where the time goes in v3:
time: 66.4 us; the launch traced here: 66.2 us
  starting transfers between devices  23.9 us (36%)
  waiting for transfers between devices  20.7 us (31%)
  Pallas kernels  18.3 us (28%)
  local copies, waits for them, and re-layouts  1.39 us (2%)
  other arithmetic  1.05 us (2%)
  between operations  0.93 us (1%)
    ppermute x10, starting transfers between devices, exchange(): lax.ppermute(held[half:], 'dp', [(i, i ^ 1 << bit) for i in range(n)])  20.4 us
    pallas_call x11, Pallas kernels, call(): pl.pallas_call(body, out_shape=out_shape, in_specs=in_specs or [VMEM] * l...  18.3 us
    ppermute x10, waiting for transfers between devices, exchange(): lax.ppermute(held[half:], 'dp', [(i, i ^ 1 << bit) for i in range(n)])  11.3 us
    ppermute x3, waiting for transfers between devices, shards(): arrived_grad = lax.ppermute(grad_out, 'section', ring)  7.13 us
    ppermute x3, starting transfers between devices, shards(): arrived = lax.ppermute(act_out, 'section', ring)  2.87 us
    ppermute x3, waiting for transfers between devices, shards(): arrived = lax.ppermute(act_out, 'section', ring)  2.21 us
  transfers between devices with their start and end apart: 16, of which 10 were waited for; matrix products, arithmetic and copies ran while one was open for 1% of the time, Pallas kernels for 19%

profile of v3, /device:TPU:0, one launch (start us, length us, event | category | flops | bytes accessed | tf_op | source)
XLA Modules:
  0.0 66.2 jit_solution(11127080413862668222)
XLA Ops:
  0.7 4.9 %shard_map.139 = (f32[576,128]{1,0:T(8,128)}, f32[576,128]{1,0:T(8,128)}, bf16[288,256]{1,0:T(8,128)(2,1)}, bf16[3,576,128]{2,1,0:T(8,128)(2,1)}, bf16[3,576,128]{2,1,0:T(8,128)(2,1)}) custom-call(s32[3]{0:T(128)} %feed_ref.1, bf16[4,576,128]{2,1,0:T(8,128)(2,1)} %bitcast.55, bf16[1,576,128]{2,1,0:T(8,128)(2,1)} %bitcast.74, f32[2,128]{1,0:T(2,128)} %bitcast.66, ...), custom_call_target="tpu_custom_call" | custom-call | bytes 7500000 | tf_op jit(solution)/shard_map/pallas_call | solution.py:313
  7.1 1.4 %shard_map.140 = (f32[3,288,256]{2,1,0:T(8,128)S(1)}, f32[3,288,256]{2,1,0:T(8,128)S(1)}, f32[3,8,128]{2,1,0:T(8,128)S(1)}, bf16[3,288,256]{2,1,0:T(8,128)(2,1)S(1)}) custom-call(bf16[4,576,128]{2,1,0:T(8,128)(2,1)S(1)} %bitcast.56, f32[2,128]{1,0:T(2,128)S(1)} %bitcast.67, f32[2,128]{1,0:T(2,128)S(1)} %bitcast.69, f32[576,128]{1,0:T(8,128)S(1)} %copy-done.5), custom_call_target="tpu_custom_call" | custom-call | bytes 6299999 | tf_op jit(solution)/shard_map/pallas_call | solution.py:313
  8.5 4.2 %collective-permute-done.1.arrived_ref = f32[576,128]{1,0:T(8,128)S(1)} collective-permute-done((f32[576,128]{1,0:T(8,128)}, f32[576,128]{1,0:T(8,128)S(1)}, u32[]{:S(2)}, u32[]{:S(2)}) %collective-permute-start.1) | collective-permute-done | bytes 294944 | tf_op jit(solution)/shard_map/ppermute | solution.py:472
  15.2 2.2 %collective-permute-start = (f32[576,128]{1,0:T(8,128)S(1)}, f32[576,128]{1,0:T(8,128)S(1)}, u32[]{:S(2)}, u32[]{:S(2)}) collective-permute-start(f32[576,128]{1,0:T(8,128)S(1)} %get-tuple-element.39.act_ref), channel_id=1, source_target_pairs={{0,8},{8,16},{16,24},{24,0},{1,9},{9,17},{17,25},{25,1},{2,10},{10... | collective-permute-start | bytes 884744 | tf_op jit(solution)/shard_map/ppermute | solution.py:475
  17.4 2.4 %collective-permute-done.3.arrived_ref = f32[576,128]{1,0:T(8,128)S(1)} collective-permute-done((f32[576,128]{1,0:T(8,128)S(1)}, f32[576,128]{1,0:T(8,128)S(1)}, u32[]{:S(2)}, u32[]{:S(2)}) %collective-permute-start.3) | collective-permute-done | bytes 294944 | tf_op jit(solution)/shard_map/ppermute | solution.py:472
  20.8 2.2 %collective-permute-done.arrived_ref = f32[576,128]{1,0:T(8,128)S(1)} collective-permute-done((f32[576,128]{1,0:T(8,128)S(1)}, f32[576,128]{1,0:T(8,128)S(1)}, u32[]{:S(2)}, u32[]{:S(2)}) %collective-permute-start) | collective-permute-done | bytes 294944 | tf_op jit(solution)/shard_map/ppermute | solution.py:475
  23.0 1.4 %shard_map.143 = (f32[576,128]{1,0:T(8,128)S(1)}, f32[4,576,128]{2,1,0:T(8,128)}, f32[4,576,128]{2,1,0:T(8,128)}) custom-call(bf16[3,576,128]{2,1,0:T(8,128)(2,1)S(1)} %copy-done.3, f32[576,128]{1,0:T(8,128)S(1)} %collective-permute-done.arrived_ref, f32[576,128]{1,0:T(8,128)S(1)} %get-tuple-element.43.grad_ref, ...), custom_call_target="tpu_custom_call", output_to_operand_aliasing={{1}: (8, {}), {2}: (9, {})} | custom-call | bytes 3900000 | tf_op jit(solution)/shard_map/pallas_call | solution.py:313
  24.6 1.8 %shard_map.146 = (f32[8,144,128]{2,1,0:T(8,128)S(1)}, f32[8,144,128]{2,1,0:T(8,128)S(1)}, f32[8,144,128]{2,1,0:T(8,128)S(1)}, f32[8,144,128]{2,1,0:T(8,128)S(1)}) custom-call(f32[576,128]{1,0:T(8,128)S(1)} %copy-done.6, f32[576,128]{1,0:T(8,128)S(1)} %get-tuple-element.53.refs_1_, f32[576,128]{1,0:T(8,128)S(1)} %get-tuple-element.54.refs_2_, ...), custom_call_target="tpu_custom_call" | custom-call | bytes 5399999 | tf_op jit(solution)/shard_map/pallas_call | solution.py:313
  27.8 2.5 %collective-permute-start.13 = (f32[4,144,128]{2,1,0:T(8,128)S(1)}, f32[4,144,128]{2,1,0:T(8,128)S(1)}, u32[]{:S(2)}, u32[]{:S(2)}) collective-permute-start(f32[4,144,128]{2,1,0:T(8,128)S(1)} %slice.75), channel_id=1, source_target_pairs={{0,2},{1,3},{2,0},{3,1},{4,6},{5,7},{6,4},{7,5},{8,10},{9,11},{10,... | collective-permute-start | bytes 884744 | tf_op jit(solution)/shard_map/ppermute | solution.py:481
  30.3 1.6 %collective-permute-start.11 = (f32[4,144,128]{2,1,0:T(8,128)S(1)}, f32[4,144,128]{2,1,0:T(8,128)S(1)}, u32[]{:S(2)}, u32[]{:S(2)}) collective-permute-start(f32[4,144,128]{2,1,0:T(8,128)S(1)} %slice.71), channel_id=1, source_target_pairs={{0,1},{1,0},{2,3},{3,2},{4,5},{5,4},{6,7},{7,6},{8,9},{9,8},{10,11... | collective-permute-start | bytes 884744 | tf_op jit(solution)/shard_map/ppermute | solution.py:481
  31.9 1.4 %shard_map.145 = (f32[576,128]{1,0:T(8,128)S(1)}, f32[4,576,128]{2,1,0:T(8,128)}, f32[4,576,128]{2,1,0:T(8,128)}) custom-call(bf16[3,576,128]{2,1,0:T(8,128)(2,1)S(1)} %copy-done.3, f32[576,128]{1,0:T(8,128)S(1)} %collective-permute-done.2.arrived_ref, f32[576,128]{1,0:T(8,128)S(1)} %get-tuple-element.47.grad_ref, ...), custom_call_target="tpu_custom_call", output_to_operand_aliasing={{1}: (8, {}), {2}: (9, {})} | custom-call | bytes 3900000 | tf_op jit(solution)/shard_map/pallas_call | solution.py:313
  34.5 1.5 %collective-permute-start.6 = (f32[4,144,128]{2,1,0:T(8,128)S(1)}, f32[4,144,128]{2,1,0:T(8,128)S(1)}, u32[]{:S(2)}, u32[]{:S(2)}) collective-permute-start(f32[4,144,128]{2,1,0:T(8,128)S(1)} %slice.61), channel_id=1, source_target_pairs={{0,1},{1,0},{2,3},{3,2},{4,5},{5,4},{6,7},{7,6},{8,9},{9,8},{10,11... | collective-permute-start | bytes 884744 | tf_op jit(solution)/shard_map/ppermute | solution.py:481
  36.0 1.8 %collective-permute-done.13 = f32[4,144,128]{2,1,0:T(8,128)S(1)} collective-permute-done((f32[4,144,128]{2,1,0:T(8,128)S(1)}, f32[4,144,128]{2,1,0:T(8,128)S(1)}, u32[]{:S(2)}, u32[]{:S(2)}) %collective-permute-start.13) | collective-permute-done | bytes 294944 | tf_op jit(solution)/shard_map/ppermute | solution.py:481
  37.9 2.3 %collective-permute-start.14 = (f32[2,144,128]{2,1,0:T(8,128)S(1)}, f32[2,144,128]{2,1,0:T(8,128)S(1)}, u32[]{:S(2)}, u32[]{:S(2)}) collective-permute-start(f32[2,144,128]{2,1,0:T(8,128)S(1)} %slice.89), channel_id=1, source_target_pairs={{0,1},{1,0},{2,3},{3,2},{4,5},{5,4},{6,7},{7,6},{8,9},{9,8},{10,11... | collective-permute-start | bytes 442376 | tf_op jit(solution)/shard_map/ppermute | solution.py:481
  40.3 1.6 %collective-permute-start.12 = (f32[2,144,128]{2,1,0:T(8,128)S(1)}, f32[2,144,128]{2,1,0:T(8,128)S(1)}, u32[]{:S(2)}, u32[]{:S(2)}) collective-permute-start(f32[2,144,128]{2,1,0:T(8,128)S(1)} %slice.87), channel_id=1, source_target_pairs={{0,2},{1,3},{2,0},{3,1},{4,6},{5,7},{6,4},{7,5},{8,10},{9,11},{10,... | collective-permute-start | bytes 442376 | tf_op jit(solution)/shard_map/ppermute | solution.py:481
  42.0 2.2 %collective-permute-done.8 = f32[4,144,128]{2,1,0:T(8,128)S(1)} collective-permute-done((f32[4,144,128]{2,1,0:T(8,128)S(1)}, f32[4,144,128]{2,1,0:T(8,128)S(1)}, u32[]{:S(2)}, u32[]{:S(2)}) %collective-permute-start.8) | collective-permute-done | bytes 294944 | tf_op jit(solution)/shard_map/ppermute | solution.py:481
  44.2 2.3 %collective-permute-start.9 = (f32[2,144,128]{2,1,0:T(8,128)S(1)}, f32[2,144,128]{2,1,0:T(8,128)S(1)}, u32[]{:S(2)}, u32[]{:S(2)}) collective-permute-start(f32[2,144,128]{2,1,0:T(8,128)S(1)} %slice.83), channel_id=1, source_target_pairs={{0,1},{1,0},{2,3},{3,2},{4,5},{5,4},{6,7},{7,6},{8,9},{9,8},{10,11... | collective-permute-start | bytes 442376 | tf_op jit(solution)/shard_map/ppermute | solution.py:481
  46.7 1.6 %collective-permute-start.7 = (f32[2,144,128]{2,1,0:T(8,128)S(1)}, f32[2,144,128]{2,1,0:T(8,128)S(1)}, u32[]{:S(2)}, u32[]{:S(2)}) collective-permute-start(f32[2,144,128]{2,1,0:T(8,128)S(1)} %slice.81), channel_id=1, source_target_pairs={{0,2},{1,3},{2,0},{3,1},{4,6},{5,7},{6,4},{7,5},{8,10},{9,11},{10,... | collective-permute-start | bytes 442376 | tf_op jit(solution)/shard_map/ppermute | solution.py:481
  48.3 1.5 %collective-permute-done.14 = f32[2,144,128]{2,1,0:T(8,128)S(1)} collective-permute-done((f32[2,144,128]{2,1,0:T(8,128)S(1)}, f32[2,144,128]{2,1,0:T(8,128)S(1)}, u32[]{:S(2)}, u32[]{:S(2)}) %collective-permute-start.14) | collective-permute-done | bytes 147488 | tf_op jit(solution)/shard_map/ppermute | solution.py:481
  49.8 2.7 %collective-permute-start.15 = (f32[1,144,256]{2,1,0:T(8,128)S(1)}, f32[1,144,256]{2,1,0:T(8,128)S(1)}, u32[]{:S(2)}, u32[]{:S(2)}) collective-permute-start(f32[1,144,256]{2,1,0:T(8,128)S(1)} %pad_maximum_fusion), channel_id=1, source_target_pairs={{0,4},{1,5},{2,6},{3,7},{4,0},{5,1},{6,2},{7,3},{8,12},{9,13},{10,... | collective-permute-start | bytes 442376 | tf_op jit(solution)/shard_map/ppermute | solution.py:481
  52.7 3.5 %collective-permute-start.10 = (f32[1,144,256]{2,1,0:T(8,128)S(1)}, f32[1,144,256]{2,1,0:T(8,128)S(1)}, u32[]{:S(2)}, u32[]{:S(2)}) collective-permute-start(f32[1,144,256]{2,1,0:T(8,128)S(1)} %pad_maximum_fusion.1), channel_id=1, source_target_pairs={{0,4},{1,5},{2,6},{3,7},{4,0},{5,1},{6,2},{7,3},{8,12},{9,13},{10,... | collective-permute-start | bytes 442376 | tf_op jit(solution)/shard_map/ppermute | solution.py:481
  57.1 2.6 %shard_map.149 = (f32[576,128]{1,0:T(8,128)}, f32[4,576,128]{2,1,0:T(8,128)}, f32[4,576,128]{2,1,0:T(8,128)}) custom-call(bf16[3,576,128]{2,1,0:T(8,128)(2,1)S(1)} %copy-done.3, f32[576,128]{1,0:T(8,128)S(1)} %collective-permute-done.4.arrived_ref, f32[576,128]{1,0:T(8,128)S(1)} %get-tuple-element.61.grad_ref, ...), custom_call_target="tpu_custom_call", output_to_operand_aliasing={{1}: (8, {}), {2}: (9, {})} | custom-call | bytes 3900000 | tf_op jit(solution)/shard_map/pallas_call | solution.py:313
  59.7 3.4 %collective-permute-done.15 = f32[1,144,256]{2,1,0:T(8,128)S(1)} collective-permute-done((f32[1,144,256]{2,1,0:T(8,128)S(1)}, f32[1,144,256]{2,1,0:T(8,128)S(1)}, u32[]{:S(2)}, u32[]{:S(2)}) %collective-permute-start.15) | collective-permute-done | bytes 147488 | tf_op jit(solution)/shard_map/ppermute | solution.py:481
  63.2 2.3 %collective-permute-done.10 = f32[1,144,256]{2,1,0:T(8,128)S(1)} collective-permute-done((f32[1,144,256]{2,1,0:T(8,128)S(1)}, f32[1,144,256]{2,1,0:T(8,128)S(1)}, u32[]{:S(2)}, u32[]{:S(2)}) %collective-permute-start.10) | collective-permute-done | bytes 147488 | tf_op jit(solution)/shard_map/ppermute | solution.py:481
  (67 shorter events, 10.0 us)
Async XLA Ops:
  0.6 5.5 %copy-start.4 = (bf16[4,1,2,12,12,256]{5,2,4,3,1,0:T(2,128)(2,1)S(1)}, bf16[4,1,2,12,12,256]{5,2,4,3,1,0:T(2,128)(2,1)}, u32[]{:S(2)}) copy-start(bf16[4,1,2,12,12,256]{5,2,4,3,1,0:T(2,128)(2,1)} %param.14) | copy-start | bytes 1769476
  0.6 5.5 %copy-start.11 = (f32[1,256]{1,0:T(1,128)S(1)}, f32[1,256]{1,0:T(1,128)}, u32[]{:S(2)}) copy-start(f32[1,256]{1,0:T(1,128)} %param.22) | copy-start | bytes 3076
  0.7 5.5 %copy-start.12 = (f32[1,256]{1,0:T(1,128)S(1)}, f32[1,256]{1,0:T(1,128)}, u32[]{:S(2)}) copy-start(f32[1,256]{1,0:T(1,128)} %param.23) | copy-start | bytes 3076
  0.7 12.0 %copy-start.1 = (bf16[1,2304,256]{2,1,0:T(8,128)(2,1)S(1)}, bf16[1,2304,256]{2,1,0:T(8,128)(2,1)}, u32[]{:S(2)}) copy-start(bf16[1,2304,256]{2,1,0:T(8,128)(2,1)} %param.21) | copy-start | bytes 3538948
  5.6 7.1 %copy-start.2 = (bf16[3,576,128]{2,1,0:T(8,128)(2,1)S(1)}, bf16[3,576,128]{2,1,0:T(8,128)(2,1)}, u32[]{:S(2)}) copy-start(bf16[3,576,128]{2,1,0:T(8,128)(2,1)} %get-tuple-element.40.grads_ref.refs_0_) | copy-start | bytes 1327108
  5.6 7.0 %collective-permute-start.1 = (f32[576,128]{1,0:T(8,128)}, f32[576,128]{1,0:T(8,128)S(1)}, u32[]{:S(2)}, u32[]{:S(2)}) collective-permute-start(f32[576,128]{1,0:T(8,128)} %get-tuple-element.37.after_ref.grad_ref), channel_id=1, source_target_pairs={{0,8},{8,16},{16,24},{24,0},{1,9},{9,17},{17,25},{25,1},{2,10},{10... | collective-permute-start | bytes 884744 | tf_op jit(solution)/shard_map/ppermute | solution.py:472
  13.6 6.2 %collective-permute-start.3 = (f32[576,128]{1,0:T(8,128)S(1)}, f32[576,128]{1,0:T(8,128)S(1)}, u32[]{:S(2)}, u32[]{:S(2)}) collective-permute-start(f32[576,128]{1,0:T(8,128)S(1)} %get-tuple-element.43.grad_ref), channel_id=1, source_target_pairs={{0,8},{8,16},{16,24},{24,0},{1,9},{9,17},{17,25},{25,1},{2,10},{10... | collective-permute-start | bytes 884744 | tf_op jit(solution)/shard_map/ppermute | solution.py:472
  15.2 7.8 %copy-start.3 = (bf16[3,576,128]{2,1,0:T(8,128)(2,1)S(1)}, bf16[3,576,128]{2,1,0:T(8,128)(2,1)}, u32[]{:S(2)}) copy-start(bf16[3,576,128]{2,1,0:T(8,128)(2,1)} %get-tuple-element.36.fresh_ref) | copy-start | bytes 1327108
  15.2 7.8 %collective-permute-start = (f32[576,128]{1,0:T(8,128)S(1)}, f32[576,128]{1,0:T(8,128)S(1)}, u32[]{:S(2)}, u32[]{:S(2)}) collective-permute-start(f32[576,128]{1,0:T(8,128)S(1)} %get-tuple-element.39.act_ref), channel_id=1, source_target_pairs={{0,8},{8,16},{16,24},{24,0},{1,9},{9,17},{17,25},{25,1},{2,10},{10... | collective-permute-start | bytes 884744 | tf_op jit(solution)/shard_map/ppermute | solution.py:475
  20.7 6.2 %collective-permute-start.5 = (f32[576,128]{1,0:T(8,128)S(1)}, f32[576,128]{1,0:T(8,128)S(1)}, u32[]{:S(2)}, u32[]{:S(2)}) collective-permute-start(f32[576,128]{1,0:T(8,128)S(1)} %get-tuple-element.47.grad_ref), channel_id=1, source_target_pairs={{0,8},{8,16},{16,24},{24,0},{1,9},{9,17},{17,25},{25,1},{2,10},{10... | collective-permute-start | bytes 884744 | tf_op jit(solution)/shard_map/ppermute | solution.py:472
  23.0 1.7 %copy-start.6 = (f32[576,128]{1,0:T(8,128)S(1)}, f32[576,128]{1,0:T(8,128)}, u32[]{:S(2)}) copy-start(f32[576,128]{1,0:T(8,128)} %get-tuple-element.52.refs_0_) | copy-start | bytes 884740
  23.0 1.7 %copy-start.8 = (bf16[288,256]{1,0:T(8,128)(2,1)S(1)}, bf16[288,256]{1,0:T(8,128)(2,1)}, u32[]{:S(2)}) copy-start(bf16[288,256]{1,0:T(8,128)(2,1)} %get-tuple-element.55.refs_3_) | copy-start | bytes 442372
  24.4 7.6 %collective-permute-start.2 = (f32[576,128]{1,0:T(8,128)S(1)}, f32[576,128]{1,0:T(8,128)S(1)}, u32[]{:S(2)}, u32[]{:S(2)}) collective-permute-start(f32[576,128]{1,0:T(8,128)S(1)} %get-tuple-element.46.act_ref), channel_id=1, source_target_pairs={{0,8},{8,16},{16,24},{24,0},{1,9},{9,17},{17,25},{25,1},{2,10},{10... | collective-permute-start | bytes 884744 | tf_op jit(solution)/shard_map/ppermute | solution.py:475
  27.8 10.0 %collective-permute-start.13 = (f32[4,144,128]{2,1,0:T(8,128)S(1)}, f32[4,144,128]{2,1,0:T(8,128)S(1)}, u32[]{:S(2)}, u32[]{:S(2)}) collective-permute-start(f32[4,144,128]{2,1,0:T(8,128)S(1)} %slice.75), channel_id=1, source_target_pairs={{0,2},{1,3},{2,0},{3,1},{4,6},{5,7},{6,4},{7,5},{8,10},{9,11},{10,... | collective-permute-start | bytes 884744 | tf_op jit(solution)/shard_map/ppermute | solution.py:481
  30.3 9.9 %collective-permute-start.11 = (f32[4,144,128]{2,1,0:T(8,128)S(1)}, f32[4,144,128]{2,1,0:T(8,128)S(1)}, u32[]{:S(2)}, u32[]{:S(2)}) collective-permute-start(f32[4,144,128]{2,1,0:T(8,128)S(1)} %slice.71), channel_id=1, source_target_pairs={{0,1},{1,0},{2,3},{3,2},{4,5},{5,4},{6,7},{7,6},{8,9},{9,8},{10,11... | collective-permute-start | bytes 884744 | tf_op jit(solution)/shard_map/ppermute | solution.py:481
  33.3 23.8 %collective-permute-start.4 = (f32[576,128]{1,0:T(8,128)S(1)}, f32[576,128]{1,0:T(8,128)S(1)}, u32[]{:S(2)}, u32[]{:S(2)}) collective-permute-start(f32[576,128]{1,0:T(8,128)S(1)} %get-tuple-element.50.act_ref), channel_id=1, source_target_pairs={{0,8},{8,16},{16,24},{24,0},{1,9},{9,17},{17,25},{25,1},{2,10},{10... | collective-permute-start | bytes 884744 | tf_op jit(solution)/shard_map/ppermute | solution.py:475
  33.8 10.4 %collective-permute-start.8 = (f32[4,144,128]{2,1,0:T(8,128)S(1)}, f32[4,144,128]{2,1,0:T(8,128)S(1)}, u32[]{:S(2)}, u32[]{:S(2)}) collective-permute-start(f32[4,144,128]{2,1,0:T(8,128)S(1)} %slice.65), channel_id=1, source_target_pairs={{0,2},{1,3},{2,0},{3,1},{4,6},{5,7},{6,4},{7,5},{8,10},{9,11},{10,... | collective-permute-start | bytes 884744 | tf_op jit(solution)/shard_map/ppermute | solution.py:481
  34.5 12.1 %collective-permute-start.6 = (f32[4,144,128]{2,1,0:T(8,128)S(1)}, f32[4,144,128]{2,1,0:T(8,128)S(1)}, u32[]{:S(2)}, u32[]{:S(2)}) collective-permute-start(f32[4,144,128]{2,1,0:T(8,128)S(1)} %slice.61), channel_id=1, source_target_pairs={{0,1},{1,0},{2,3},{3,2},{4,5},{5,4},{6,7},{7,6},{8,9},{9,8},{10,11... | collective-permute-start | bytes 884744 | tf_op jit(solution)/shard_map/ppermute | solution.py:481
  37.9 11.8 %collective-permute-start.14 = (f32[2,144,128]{2,1,0:T(8,128)S(1)}, f32[2,144,128]{2,1,0:T(8,128)S(1)}, u32[]{:S(2)}, u32[]{:S(2)}) collective-permute-start(f32[2,144,128]{2,1,0:T(8,128)S(1)} %slice.89), channel_id=1, source_target_pairs={{0,1},{1,0},{2,3},{3,2},{4,5},{5,4},{6,7},{7,6},{8,9},{9,8},{10,11... | collective-permute-start | bytes 442376 | tf_op jit(solution)/shard_map/ppermute | solution.py:481
  40.3 9.5 %collective-permute-start.12 = (f32[2,144,128]{2,1,0:T(8,128)S(1)}, f32[2,144,128]{2,1,0:T(8,128)S(1)}, u32[]{:S(2)}, u32[]{:S(2)}) collective-permute-start(f32[2,144,128]{2,1,0:T(8,128)S(1)} %slice.87), channel_id=1, source_target_pairs={{0,2},{1,3},{2,0},{3,1},{4,6},{5,7},{6,4},{7,5},{8,10},{9,11},{10,... | collective-permute-start | bytes 442376 | tf_op jit(solution)/shard_map/ppermute | solution.py:481
  44.2 8.3 %collective-permute-start.9 = (f32[2,144,128]{2,1,0:T(8,128)S(1)}, f32[2,144,128]{2,1,0:T(8,128)S(1)}, u32[]{:S(2)}, u32[]{:S(2)}) collective-permute-start(f32[2,144,128]{2,1,0:T(8,128)S(1)} %slice.83), channel_id=1, source_target_pairs={{0,1},{1,0},{2,3},{3,2},{4,5},{5,4},{6,7},{7,6},{8,9},{9,8},{10,11... | collective-permute-start | bytes 442376 | tf_op jit(solution)/shard_map/ppermute | solution.py:481
  46.7 6.0 %collective-permute-start.7 = (f32[2,144,128]{2,1,0:T(8,128)S(1)}, f32[2,144,128]{2,1,0:T(8,128)S(1)}, u32[]{:S(2)}, u32[]{:S(2)}) collective-permute-start(f32[2,144,128]{2,1,0:T(8,128)S(1)} %slice.81), channel_id=1, source_target_pairs={{0,2},{1,3},{2,0},{3,1},{4,6},{5,7},{6,4},{7,5},{8,10},{9,11},{10,... | collective-permute-start | bytes 442376 | tf_op jit(solution)/shard_map/ppermute | solution.py:481
  49.8 13.4 %collective-permute-start.15 = (f32[1,144,256]{2,1,0:T(8,128)S(1)}, f32[1,144,256]{2,1,0:T(8,128)S(1)}, u32[]{:S(2)}, u32[]{:S(2)}) collective-permute-start(f32[1,144,256]{2,1,0:T(8,128)S(1)} %pad_maximum_fusion), channel_id=1, source_target_pairs={{0,4},{1,5},{2,6},{3,7},{4,0},{5,1},{6,2},{7,3},{8,12},{9,13},{10,... | collective-permute-start | bytes 442376 | tf_op jit(solution)/shard_map/ppermute | solution.py:481
  52.7 12.8 %collective-permute-start.10 = (f32[1,144,256]{2,1,0:T(8,128)S(1)}, f32[1,144,256]{2,1,0:T(8,128)S(1)}, u32[]{:S(2)}, u32[]{:S(2)}) collective-permute-start(f32[1,144,256]{2,1,0:T(8,128)S(1)} %pad_maximum_fusion.1), channel_id=1, source_target_pairs={{0,4},{1,5},{2,6},{3,7},{4,0},{5,1},{6,2},{7,3},{8,12},{9,13},{10,... | collective-permute-start | bytes 442376 | tf_op jit(solution)/shard_map/ppermute | solution.py:481
  (5 other events, 6.0 us)

commit v4 on v3

v4 whole, which is shorter than its diff:
```python
import functools
import math

import jax
import jax.numpy as jnp
from jax import lax
from jax.experimental import pallas as pl
from jax.experimental.pallas import tpu as pltpu
from jax.sharding import PartitionSpec as P

GROUPS = 32
F32 = jnp.float32
BF16 = jnp.bfloat16
LANES = 128
VMEM_LIMIT = 24 * 1024 * 1024
WHOLE_VMEM = 60 * 1024 * 1024


class Dims:
    def __init__(self, images, rows, cols, channels):
        self.n, self.h, self.w, self.c = images, rows, cols, channels
        self.cts = channels // LANES
        self.unit = self.cts * images
        self.pix = rows * cols
        self.flat = self.pix * self.unit
        per = 8 // math.gcd(8, self.unit)
        self.pad = -(-(cols + 1) // per) * per
        self.padded = (self.pix + 2 * self.pad) * self.unit
        self.count = self.pix * (channels // GROUPS)


def interleaved(x, d):
    lead = x.shape[:-4]
    k = len(lead)
    x = x.reshape(*lead, d.n, d.pix, d.cts, LANES)
    x = x.transpose(*range(k), k + 1, k + 2, k, k + 3)
    return x.reshape(*lead, d.flat, LANES)


def standard(x, d):
    lead = x.shape[:-2]
    k = len(lead)
    x = x.reshape(*lead, d.pix, d.cts, d.n, LANES)
    x = x.transpose(*range(k), k + 2, k, k + 1, k + 3)
    return x.reshape(*lead, d.n, d.h, d.w, d.c)


def group_sum(v, width):
    lane = lax.broadcasted_iota(jnp.int32, v.shape, 1)
    k = 1
    while k < width:
        v = v + jnp.where((lane & k) == 0, pltpu.roll(v, LANES - k, 1), pltpu.roll(v, k, 1))
        k *= 2
    return v


def pattern(ref, d):
    row = lax.broadcasted_iota(jnp.int32, (8, LANES), 0)
    ct = (row // d.n) % d.cts
    out = jnp.broadcast_to(ref[0:1, :], (8, LANES))
    for i in range(1, d.cts):
        out = jnp.where(ct == i, jnp.broadcast_to(ref[i : i + 1, :], (8, LANES)), out)
    return out


def unit_sum(v, d):
    s = jnp.sum(v, axis=0)
    k = d.unit
    while k < 8:
        s = s + pltpu.roll(s, k, 0)
        k *= 2
    return group_sum(s, d.c // GROUPS)


def normalized(x, d):
    tiles = x.reshape(-1, 8, LANES)
    scale = 1.0 / d.count
    mean = unit_sum(tiles, d) * scale
    centred = tiles - mean
    var = unit_sum(centred * centred, d) * scale
    rstd = lax.rsqrt(var + 1e-05)
    return centred * rstd, rstd


def sigmoid(a):
    return 0.5 * jnp.tanh(0.5 * a) + 0.5


def spread(value, refs, d):
    zeros = jnp.zeros((d.pad * d.unit, LANES), F32)
    for ref in refs:
        ref[0 : d.pad * d.unit, :] = zeros
        ref[d.padded - d.pad * d.unit : d.padded, :] = zeros
        ref[d.pad * d.unit : d.pad * d.unit + d.flat, :] = value
    edge = jnp.zeros((d.unit, LANES), F32)
    for i in range(d.h):
        last = (d.pad + i * d.w + d.w - 1) * d.unit
        first = (d.pad + i * d.w) * d.unit
        refs[0][last : last + d.unit, :] = edge
        refs[2][first : first + d.unit, :] = edge


def plane(ref, d, shift, n):
    parts = [
        ref[pl.ds((d.pad + shift) * d.unit + ct * d.n + n, d.pix, stride=d.unit), :] for ct in range(d.cts)
    ]
    return jnp.concatenate(parts, axis=1)


def gather_patches(refs, out_ref, d):
    for kr in range(3):
        for kc in range(3):
            tap = kr * 3 + kc
            for n in range(d.n):
                block = plane(refs[kc], d, (kr - 1) * d.w + kc - 1, n)
                out_ref[n * d.pix : (n + 1) * d.pix, tap * d.c : (tap + 1) * d.c] = block.astype(BF16)


def from_interleaved(ref, d, base=0):
    rows = [
        jnp.concatenate(
            [ref[pl.ds(base + ct * d.n + n, d.pix, stride=d.unit), :] for ct in range(d.cts)], axis=1
        )
        for n in range(d.n)
    ]
    return jnp.concatenate(rows, axis=0)


def to_interleaved(ref, n, value, d):
    for ct in range(d.cts):
        ref[pl.ds(ct * d.n + n, d.pix, stride=d.unit), :] = value[:, ct * LANES : (ct + 1) * LANES]


def prepare(d, x, gain_ref, bias_ref, slope_ref, normed_ref, hidden_ref, tmp):
    normed, rstd = normalized(x, d)
    gain = pattern(gain_ref, d)
    a = normed * gain + pattern(bias_ref, d)
    s = sigmoid(a)
    for ref, value in (
        (normed_ref, normed),
        (slope_ref, s * (1.0 + a * (1.0 - s)) * gain),
        (hidden_ref, a * s),
    ):
        tmp[...] = value.reshape(d.flat, LANES)
        ref[...] = from_interleaved(tmp, d).astype(ref.dtype)
    return rstd


def prep_kernel(d, feed_ref, saved_ref, gain_ref, bias_ref, fresh_act_ref, fresh_grad_ref, *refs):
    slope_ref, normed_ref, rstd_ref, hidden_ref, acts_ref, grads_ref, tmp = refs
    for k in range(feed_ref.shape[0]):
        acts_ref[k] = fresh_act_ref[feed_ref[k]]
        grads_ref[k] = fresh_grad_ref[feed_ref[k]]
    for t in range(saved_ref.shape[0]):
        refs = [r.at[t] for r in (slope_ref, normed_ref, hidden_ref)]
        rstd_ref[t] = prepare(d, saved_ref[t].astype(F32), gain_ref, bias_ref, *refs, tmp)


def through_layer(d, cols, weight_ref, slope_ref, normed_ref, rstd, mid, out_ref):
    grad = None
    for tap in range(9):
        part = lax.dot_general(
            cols[:, tap * d.c : (tap + 1) * d.c],
            weight_ref[(8 - tap) * d.c : (9 - tap) * d.c, :],
            (((1,), (1,)), ((), ())),
            preferred_element_type=F32,
        )
        grad = part if grad is None else grad + part
    through = grad * slope_ref[...]
    weighted = through * normed_ref[...]
    rows = []
    for ct in range(d.cts):
        for n in range(d.n):
            for v in (through, weighted):
                rows.append(
                    jnp.sum(v[n * d.pix : (n + 1) * d.pix, ct * LANES : (ct + 1) * LANES], axis=0, keepdims=True)
                )
    sums = group_sum(jnp.concatenate(rows, axis=0), d.c // GROUPS) * (1.0 / d.count)
    for n in range(d.n):
        for ct in range(d.cts):
            where = ct * d.n + n
            k = where * 2
            here = (slice(n * d.pix, (n + 1) * d.pix), slice(ct * LANES, (ct + 1) * LANES))
            value = (through[here] - sums[k : k + 1] - normed_ref[here] * sums[k + 1 : k + 2]) * rstd[where : where + 1, :]
            e_here = mid[pl.ds(d.pad * d.unit + where, d.pix, stride=d.unit), :]
            out_ref[pl.ds(where, d.pix, stride=d.unit), :] = value + e_here


def first_kernel(d, saved_hbm, grad_hbm, gain_hbm, bias_hbm, weight_hbm, *refs):
    out_ref, saved, grad, gain, bias, weight, slope, normed, hidden, tmp, left, mid, right, cols, sems = refs

    @pl.when(chip() == 0)
    def _():
        pairs = [(grad_hbm.at[0], grad), (saved_hbm.at[0], saved), (gain_hbm, gain), (bias_hbm, bias), (weight_hbm, weight)]
        copies = [pltpu.make_async_copy(src, dst, sems.at[i]) for i, (src, dst) in enumerate(pairs)]
        for copy in copies:
            copy.start()
        copies[0].wait()
        spread(grad[...].astype(F32), (left, mid, right), d)
        gather_patches((left, mid, right), cols, d)
        for copy in copies[1:4]:
            copy.wait()
        rstd = prepare(d, saved[...].astype(F32), gain, bias, slope, normed, hidden, tmp)
        copies[4].wait()
        through_layer(d, cols, weight, slope, normed, rstd, mid, out_ref)

    @pl.when(chip() != 0)
    def _():
        out_ref[...] = jnp.zeros_like(out_ref)


def chip():
    return lax.axis_index("section") // 2


def enter(slot, grad0_ref, grads_ref, inner_ref, outer_ref, e_ref):
    tick = slot - chip()
    second = lax.axis_index("section") % 2 == 1

    @pl.when(tick == 0)
    def _():
        e_ref[...] = grad0_ref[0].astype(F32)

    @pl.when(jnp.logical_and(tick > 0, second))
    def _():
        e_ref[...] = inner_ref[...]

    @pl.when(jnp.logical_and(tick > 0, jnp.logical_and(jnp.logical_not(second), chip() > 0)))
    def _():
        e_ref[...] = outer_ref[...]

    @pl.when(jnp.logical_and(tick > 0, lax.axis_index("section") == 0))
    def _():
        e_ref[...] = grads_ref[jnp.minimum(jnp.maximum(tick - 1, 0), grads_ref.shape[0] - 1)].astype(F32)


def backward_kernel(
    d,
    slot,
    grad0_ref,
    grads_ref,
    inner_ref,
    outer_ref,
    slope_ref,
    normed_ref,
    rstd_ref,
    weight_ref,
    *refs,
):
    out_ref, e_ref, left, mid, right, cols = refs[-6:]
    tick = slot - chip()
    ticks = slope_ref.shape[0]
    runs = jnp.logical_and(tick >= 0, tick < ticks)

    @pl.when(runs)
    def _():
        t = jnp.minimum(jnp.maximum(tick, 0), ticks - 1)
        enter(slot, grad0_ref, grads_ref, inner_ref, outer_ref, e_ref)
        spread(e_ref[...], (left, mid, right), d)
        gather_patches((left, mid, right), cols, d)
        through_layer(d, cols, weight_ref, slope_ref.at[t], normed_ref.at[t], rstd_ref[t], mid, out_ref)

    @pl.when(jnp.logical_not(runs))
    def _():
        out_ref[...] = jnp.zeros_like(out_ref)
        e_ref[...] = jnp.zeros_like(e_ref)


def forward_kernel(d, tick, chips, grads, fresh_ref, arrived_ref, gain_ref, bias_ref, weight_ref, *refs):
    stores = []
    if grads:
        act_refs, grad_refs, refs = refs[:tick], refs[tick : tick + grads], refs[tick + grads :]
        out_ref, emitted_ref, returned_ref, left, mid, right, cols, kept, sems = refs
        for t in range(tick):
            stores.append(pltpu.make_async_copy(act_refs[t], emitted_ref.at[t], sems.at[t]))
            stores[-1].start()
        for t in range(tick + 1):
            for c in range(chips):

                @pl.when(chip() == c)
                def _():
                    pltpu.make_async_copy(grad_refs[t + c], returned_ref.at[t], sems.at[tick + 1 + t]).start()

            stores.append(pltpu.make_async_copy(grad_refs[t], returned_ref.at[t], sems.at[tick + 1 + t]))
    else:
        out_ref, left, mid, right, cols, kept = refs
    x = fresh_ref[max(tick - 1, 0)].astype(F32)
    if tick > 0:
        x = jnp.where(lax.axis_index("section") == 0, x, arrived_ref[...])
    kept[...] = x
    normed, _ = normalized(x, d)
    a = normed * pattern(gain_ref, d) + pattern(bias_ref, d)
    hidden = (a * sigmoid(a)).reshape(d.flat, LANES)
    spread(hidden, (left, mid, right), d)
    gather_patches((left, mid, right), cols, d)
    conv = jnp.dot(cols[...], weight_ref[...], preferred_element_type=F32)
    for n in range(d.n):
        for ct in range(d.cts):
            where = pl.ds(ct * d.n + n, d.pix, stride=d.unit)
            out_ref[where, :] = (
                kept[where, :] + conv[n * d.pix : (n + 1) * d.pix, ct * LANES : (ct + 1) * LANES]
            )
    if grads:
        stores.append(pltpu.make_async_copy(out_ref, emitted_ref.at[tick], sems.at[tick]))
        stores[-1].start()
    for store in stores:
        store.wait()


def weight_kernel(d, ticks, chips, n, positions, factor, grad0_ref, hidden_ref, *refs):
    me = lax.axis_index("dp")
    here = jnp.where(me % 2 == 0, me // 2, n - 1 - me // 2)
    rows = d.n * d.pix
    chunk = 9 * d.c // n
    last = hidden_ref.shape[0] - 1
    added = ticks == 0
    if added:
        grads_ref, inner_ref, outer_ref = refs[:3]
        e_refs, refs = refs[3 : 2 + chips], refs[2 + chips :]
        before, halves = refs[:2], refs[2:4]
        kept, left, mid, right, cols = refs[4:]
        h = hidden_ref[last]
        for c in range(chips - 1):

            @pl.when(chip() == c)
            def _():
                kept[...] = e_refs[c][...]

        @pl.when(chip() == chips - 1)
        def _():
            enter(last + chips - 1, grad0_ref, grads_ref, inner_ref, outer_ref, kept)

        spread(kept[...], (left, mid, right), d)
        gather_patches((left, mid, right), cols, d)
    else:
        e_refs, halves = refs[: ticks + chips - 2], refs[ticks + chips - 2 : ticks + chips]
        kept, left, mid, right, cols = refs[ticks + chips :]
        h = hidden_ref[0:ticks].reshape(ticks * rows, d.c)
        for t in range(ticks):
            if t == 0:
                kept[...] = grad0_ref[0].astype(F32)
            else:
                for c in range(chips):

                    @pl.when(chip() == c)
                    def _():
                        kept[...] = e_refs[t + c - 1][...]

            spread(kept[...], (left, mid, right), d)
            gather_patches((left, mid, right), cols.at[t * rows : (t + 1) * rows], d)
    for tap in range(9):
        block = lax.dot_general(
            h, cols[:, (8 - tap) * d.c : (9 - tap) * d.c], (((0,), (0,)), ((), ())), preferred_element_type=F32
        ) * factor
        at = tap * d.c
        while at < (tap + 1) * d.c:
            owner = at // chunk
            stop = min((owner + 1) * chunk, (tap + 1) * d.c)
            where = pl.ds(at - owner * chunk, stop - at)
            away = (positions[owner] - here + n) % n
            for i in range(2):
                piece = block[at - tap * d.c : stop - tap * d.c, i * LANES : (i + 1) * LANES]
                if added:
                    piece = piece + before[i][away, where, :]
                halves[i][away, where, :] = piece
            at = stop


def cost(us):
    return pl.CostEstimate(flops=0, bytes_accessed=int(us * 3.0e6), transcendentals=0)


VMEM = pl.BlockSpec(memory_space=pltpu.VMEM)
HBM = pl.BlockSpec(memory_space=pltpu.HBM)
SMEM = pl.BlockSpec(memory_space=pltpu.SMEM)
ANY = pl.BlockSpec(memory_space=pl.ANY)


class Chain:
    token = None

    def call(self, body, out_shape, scratch, us, *operands, in_specs=None, out_specs=None, alias=None, vmem=VMEM_LIMIT):
        def chained(*refs):
            after = refs[held + count]
            after[...] = refs[0][...] if held else jnp.zeros_like(after)
            body(*refs[held : held + count], *refs[held + count + 1 :])

        count, held = len(operands), int(self.token is not None)
        self.token, *outs = pl.pallas_call(
            chained,
            out_shape=(jax.ShapeDtypeStruct((8, LANES), F32), *out_shape),
            in_specs=[VMEM] * held + (in_specs or [VMEM] * count),
            out_specs=(VMEM, *(out_specs or [VMEM] * len(out_shape))),
            scratch_shapes=scratch,
            compiler_params=pltpu.CompilerParams(vmem_limit_bytes=vmem),
            cost_estimate=cost(us),
            input_output_aliases={i + held: o + 1 for i, o in (alias or {}).items()},
        )(*([self.token] * held), *operands)
        return outs


def add_kernel(up_offset, down_offset, first_terms, second_terms, first, second, first_out, second_out):
    first_out[...] = first_terms[up_offset] + first[...]
    second_out[...] = second_terms[down_offset] + second[...]


def final_kernel(first_terms, second_terms, first_up, first_down, second_down, second_up, out):
    out[:, :LANES] = first_terms[0] + first_up[...] + first_down[...]
    out[:, LANES:] = second_terms[0] + second_up[...] + second_down[...]


def shards(
    arriving_activations,
    fresh_images,
    saved_inputs,
    arriving_gradients,
    fresh_gradients,
    feed_order,
    forward_weight,
    forward_gain,
    forward_bias,
    backward_weight,
    backward_gain,
    backward_bias,
):
    ticks = saved_inputs.shape[0]
    d = Dims(*saved_inputs.shape[2:])
    sections = lax.axis_size("section")
    chips = sections // 2
    ring = [(i, (i + 1) % sections) for i in range(sections)]
    inside = [(i, i ^ 1) for i in range(sections)]

    act0 = interleaved(arriving_activations, d)
    grad0 = interleaved(arriving_gradients, d)
    fresh_act = interleaved(fresh_images, d)
    fresh_grad = interleaved(fresh_gradients, d)
    saved = interleaved(saved_inputs[:, 0], d)
    fgain, fbias, bgain, bbias = [
        v[0].reshape(d.cts, LANES) for v in (forward_gain, forward_bias, backward_gain, backward_bias)
    ]

    msg = jax.ShapeDtypeStruct((d.flat, LANES), F32)
    every = jax.ShapeDtypeStruct((ticks, d.flat, LANES), F32)
    rows = d.n * d.pix
    wide = jax.ShapeDtypeStruct((rows, d.c), F32)
    padded = pltpu.VMEM((d.padded, LANES), F32)
    cols = pltpu.VMEM((rows, 9 * d.c), BF16)
    flat = pltpu.VMEM((d.flat, LANES), F32)
    sem = pltpu.SemaphoreType.DMA

    whole = pltpu.VMEM((rows, d.c), F32)
    vector = pltpu.VMEM((d.cts, LANES), F32)
    narrow = jax.ShapeDtypeStruct((rows, d.c), BF16)
    raw = pltpu.VMEM((d.flat, LANES), BF16)

    last = ticks - 1

    def later(shape, dtype):
        return jax.ShapeDtypeStruct((last, *shape), dtype)

    chain = Chain()

    def first():
        return chain.call(
            functools.partial(first_kernel, d),
            (msg,),
            [raw, raw, vector, vector, pltpu.VMEM(backward_weight.shape[1:], BF16), whole, whole]
            + [pltpu.VMEM((rows, d.c), BF16), flat]
            + [padded] * 3
            + [cols, sem((5,))],
            2.5,
            saved,
            grad0,
            bgain,
            bbias,
            backward_weight[0],
            in_specs=[HBM] * 5,
            vmem=WHOLE_VMEM,
        )

    def prep():
        def all_ticks(shape, dtype, count=ticks):
            return jax.ShapeDtypeStruct((count, *shape), dtype)

        entering = all_ticks((d.flat, LANES), BF16, last)
        wide = all_ticks((rows, d.c), F32)
        return chain.call(
            functools.partial(prep_kernel, d),
            (wide, wide, all_ticks((8, LANES), F32), all_ticks((rows, d.c), BF16), entering, entering),
            [flat],
            2.0,
            feed_order,
            saved,
            bgain,
            bbias,
            fresh_act,
            fresh_grad,
            in_specs=[SMEM] + [VMEM] * 5,
        )

    def backward(slot, inner, outer):
        return chain.call(
            functools.partial(backward_kernel, d, slot),
            (msg, msg),
            [padded] * 3 + [cols],
            0.9,
            grad0,
            grads,
            inner,
            outer,
            slope,
            normed,
            rstd,
            backward_weight[0],
        )

    def forward(t, arrived, *collected):
        return chain.call(
            functools.partial(forward_kernel, d, t, chips, len(collected) - t if collected else 0),
            (msg, every, every) if collected else (msg,),
            [padded] * 3 + [cols, flat] + ([sem((2 * ticks,))] if collected else []),
            1.2,
            acts if t else act0,
            arrived,
            fgain,
            fbias,
            forward_weight[0],
            *collected,
            in_specs=[VMEM] * 5 + [ANY] * len(collected),
            out_specs=(VMEM, ANY, ANY) if collected else None,
        )

    n = lax.axis_size("dp")
    order = list(range(0, n, 2)) + list(range(n - 1 - n % 2, 0, -2))
    positions = [order.index(i) for i in range(n)]
    chunk = 9 * d.c // n
    half = jax.ShapeDtypeStruct((n, chunk, LANES), F32)

    def weight_terms(ticks, *operands):
        count = max(ticks, 1)
        return chain.call(
            functools.partial(weight_kernel, d, ticks, chips, n, positions, 1.0 / (n * d.n)),
            (half,) * 2,
            [flat] + [padded] * 3 + [pltpu.VMEM((count * rows, 9 * d.c), BF16)],
            0.6 * count,
            grad0,
            hidden,
            *operands,
            alias={} if ticks else {len(operands) + i: i for i in range(2)},
        )

    slots = ticks + chips - 1
    gradients, entered, inner, outer = first(), [None], [], []
    slope, normed, rstd, hidden, acts, grads = prep()
    arrived, outputs = jnp.zeros((8, LANES), F32), []

    def arrivals(slot):
        return inner[slot - 1], outer[max(slot - 2, 0)]

    for slot in range(slots - 1):
        if slot > 0:
            out, e = backward(slot, *arrivals(slot))
            gradients.append(out)
            entered.append(e)
        inner.append(lax.ppermute(gradients[slot], "section", inside))
        if slot < slots - 2:
            outer.append(lax.ppermute(gradients[slot], "section", ring))
        if slot == slots - 3:
            outputs += forward(0, arrived)
            arrived = lax.ppermute(outputs[0], "section", ring)
    before = weight_terms(last, *entered[1 : last + chips - 1])
    terms = weight_terms(0, grads, *arrivals(slots - 1), *entered[last : last + chips - 1], *before)

    onward = [(order[i], order[(i + 1) % n]) for i in range(n)]
    back = [(b, a) for a, b in onward]
    piece = jax.ShapeDtypeStruct((chunk, LANES), F32)
    hops = n // 2

    def swapped(first, second, ways):
        return [lax.ppermute(v, "dp", way) for v, way in zip((first, second), ways)]

    def long_hop(pair):
        return swapped(*pair, (onward, back))

    def short_hop(pair):
        return swapped(*pair, (back, onward))

    def added(pair, up, down):
        return chain.call(
            functools.partial(add_kernel, up % n, down % n), (piece,) * 2, [], 0.2, *terms, *pair
        )

    def forward_step(t, arrived):
        outputs.extend(forward(t, arrived))
        return lax.ppermute(outputs[t], "section", ring)

    long = long_hop([terms[0][hops], terms[1][n - hops]])
    short = short_hop([terms[0][n - hops + 1], terms[1][hops - 1]])
    arrived = forward_step(1, arrived)
    for hop in range(1, hops):
        long = long_hop(added(long, hops - hop, hop - hops))
        if hop < hops - 1:
            short = short_hop(added(short, hop + 1 - hops, hops - 1 - hop))
        if hop == 1:
            out, _ = backward(slots - 1, *arrivals(slots - 1))
            gradients.append(out)
        if 1 < hop < last:
            arrived = forward_step(hop, arrived)
    _, emitted, returned = forward(last, arrived, *outputs, *gradients)
    (shard_sum,) = chain.call(
        final_kernel, (jax.ShapeDtypeStruct((chunk, d.c), F32),), [], 0.4, *terms, *long[:1], *short[:1], *long[1:], *short[1:]
    )
    return standard(emitted, d)[:, None], standard(returned, d)[:, None], shard_sum[None]


def solution(mesh):
    placed = (
        P("section", "dp", None, None, None),
        P(None, "dp", None, None, None),
        P(None, "section", "dp", None, None, None),
        P("section", "dp", None, None, None),
        P(None, "dp", None, None, None),
        P(),
        P("section", None, None),
        P("section", None),
        P("section", None),
        P("section", None, None),
        P("section", None),
        P("section", None),
    )
    return jax.shard_map(
        shards,
        mesh=mesh,
        in_specs=placed,
        out_specs=(
            P(None, "section", "dp", None, None, None),
            P(None, "section", "dp", None, None, None),
            P("section", "dp", None),
        ),
        check_vma=False,
    )
```

time: 66.4 us -> 58.8 us (0.89)
  starting transfers between devices: 23.9 us -> 17.6 us
  Pallas kernels: 18.3 us -> 20 us
  waiting for transfers between devices: 20.7 us -> 19.3 us
  other arithmetic: 1.05 us -> 0 us
    ppermute x16 -> x24, starting transfers between devices: 23.9 us -> 17.6 us  [the longest x14 15.2 us: swapped(): return [lax.ppermute(v, 'dp', way) for v, way in zip((first, second), ways)]]
    pallas_call x11 -> x18, Pallas kernels: 18.3 us -> 20 us  [call(): pl.pallas_call(chained, out_shape=(jax.ShapeDtypeStruct((8, LANES), F32),...]
    ppermute x16 -> x24, waiting for transfers between devices: 20.7 us -> 19.3 us  [the longest x14 13.5 us: swapped(): return [lax.ppermute(v, 'dp', way) for v, way in zip((first, second), ways)]]
    broadcast_in_dim x1 -> x0, other arithmetic: 0.73 us -> none  [shards(): shard_sum[None]]
  transfers between devices with their start and end apart: 16 -> 24, of which waited for: 10 -> 11; matrix products, arithmetic and copies ran while one was open for 1% -> 0% of each run, Pallas kernels for 19% -> 25%
where the time goes in v4:
time: 58.8 us; the launch traced here: 58.6 us
  Pallas kernels  20 us (34%)
  waiting for transfers between devices  19.3 us (33%)
  starting transfers between devices  17.6 us (30%)
  between operations  0.96 us (2%)
  local copies, waits for them, and re-layouts  0.78 us (1%)
    pallas_call x18, Pallas kernels, call(): pl.pallas_call(chained, out_shape=(jax.ShapeDtypeStruct((8, LANES), F32),...  20 us
    ppermute x14, starting transfers between devices, swapped(): return [lax.ppermute(v, 'dp', way) for v, way in zip((first, second), ways)]  15.2 us
    ppermute x14, waiting for transfers between devices, swapped(): return [lax.ppermute(v, 'dp', way) for v, way in zip((first, second), ways)]  13.5 us
    ppermute x3, waiting for transfers between devices, shards(): outer.append(lax.ppermute(gradients[slot], 'section', ring))  4.72 us
    ppermute x3, starting transfers between devices, shards(): outer.append(lax.ppermute(gradients[slot], 'section', ring))  1.39 us
  transfers between devices with their start and end apart: 24, of which 11 were waited for; matrix products, arithmetic and copies ran while one was open for 0% of the time, Pallas kernels for 25%

profile of v4, /device:TPU:0, one launch (start us, length us, event | category | flops | bytes accessed | tf_op | source)
XLA Modules:
  0.0 58.6 jit_solution(4659471254002740342)
XLA Ops:
  0.7 3.7 %shard_map.139 = (f32[8,128]{1,0:T(8,128)}, f32[576,128]{1,0:T(8,128)}) custom-call(bf16[4,576,128]{2,1,0:T(8,128)(2,1)} %bitcast.66, bf16[1,576,128]{2,1,0:T(8,128)(2,1)} %bitcast.59, f32[2,128]{1,0:T(2,128)} %bitcast.79, f32[2,128]{1,0:T(2,128)} %bitcast.81, bf16[2304,256]{1,0:T(8,128)(2,1)} %bitcast.50), custom_call_target="tpu_custom_call" | custom-call | bytes 7500000 | tf_op jit(solution)/shard_map/pallas_call | solution.py:389
  5.7 2.2 %shard_map.140 = (f32[8,128]{1,0:T(8,128)S(1)}, f32[4,288,256]{2,1,0:T(8,128)S(1)}, f32[4,288,256]{2,1,0:T(8,128)S(1)}, f32[4,8,128]{2,1,0:T(8,128)S(1)}, bf16[4...) custom-call(f32[8,128]{1,0:T(8,128)S(1)} %copy-done.10, ...), custom_call_target="tpu_custom_call" | custom-call | bytes 6000000 | tf_op jit(solution)/shard_map/pallas_call | solution.py:389
  8.0 2.9 %collective-permute-done.1.refs_4_ = f32[576,128]{1,0:T(8,128)S(1)} collective-permute-done((f32[576,128]{1,0:T(8,128)}, f32[576,128]{1,0:T(8,128)S(1)}, u32[]{:S(2)}, u32[]{:S(2)}) %collective-permute-start.1) | collective-permute-done | bytes 294944 | tf_op jit(solution)/shard_map/ppermute | solution.py:567
  12.4 1.1 %collective-permute-done.2.refs_3_ = f32[576,128]{1,0:T(8,128)S(1)} collective-permute-done((f32[576,128]{1,0:T(8,128)S(1)}, f32[576,128]{1,0:T(8,128)S(1)}, u32[]{:S(2)}, u32[]{:S(2)}) %collective-permute-start.2) | collective-permute-done | bytes 294944 | tf_op jit(solution)/shard_map/ppermute | solution.py:565
  13.5 1.0 %shard_map.142 = (f32[8,128]{1,0:T(8,128)S(1)}, f32[576,128]{1,0:T(8,128)S(1)}, f32[576,128]{1,0:T(8,128)S(1)}) custom-call(f32[8,128]{1,0:T(8,128)S(1)} %get-tuple-element.61.refs_0_, bf16[1,576,128]{2,1,0:T(8,128)(2,1)S(1)} %bitcast.61, bf16[3,576,128]{2,1,0:T(8,128)(2,1)S(1)} %get-tuple-element.56.refs_2_.refs_3_, ...), custom_call_target="tpu_custom_call" | custom-call | bytes 2700000 | tf_op jit(solution)/shard_map/pallas_call | solution.py:389
  15.0 1.2 %shard_map.143 = (f32[8,128]{1,0:T(8,128)S(1)}, f32[576,128]{1,0:T(8,128)S(1)}) custom-call(f32[8,128]{1,0:T(8,128)S(1)} %get-tuple-element.63.refs_0_, bf16[1,576,128]{2,1,0:T(8,128)(2,1)S(1)} %bitcast.70, f32[8,128]{1,0:T(8,128)S(1)} %broadcast_in_dim.6.refs_2_, f32[2,128]{1,0:T(2,128)S(1)} %bitcast.71, f32[2,128]{1,0:T(2,128)S(1)} %bitcast.75, ...), custom_call_target="tpu_custom_call" | custom-call | bytes 3600000 | tf_op jit(solution)/shard_map/pallas_call | solution.py:389
  16.2 1.9 %collective-permute-done.4.refs_4_ = f32[576,128]{1,0:T(8,128)S(1)} collective-permute-done((f32[576,128]{1,0:T(8,128)S(1)}, f32[576,128]{1,0:T(8,128)S(1)}, u32[]{:S(2)}, u32[]{:S(2)}) %collective-permute-start.4) | collective-permute-done | bytes 294944 | tf_op jit(solution)/shard_map/ppermute | solution.py:567
  19.6 2.1 %shard_map.145 = (f32[8,128]{1,0:T(8,128)S(1)}, f32[8,288,128]{2,1,0:T(8,128)S(1)}, f32[8,288,128]{2,1,0:T(8,128)S(1)}) custom-call(f32[8,128]{1,0:T(8,128)S(1)} %get-tuple-element.66.refs_0_, bf16[1,576,128]{2,1,0:T(8,128)(2,1)S(1)} %bitcast.63, bf16[4,288,256]{2,1,0:T(8,128)(2,1)S(1)} %get-tuple-element.67.refs_2_, ...), custom_call_target="tpu_custom_call" | custom-call | bytes 5399999 | tf_op jit(solution)/shard_map/pallas_call | solution.py:389
  22.7 3.1 %collective-permute-start.8 = (f32[288,128]{1,0:T(8,128)S(1)}, f32[288,128]{1,0:T(8,128)S(1)}, u32[]{:S(2)}, u32[]{:S(2)}) collective-permute-start(f32[288,128]{1,0:T(8,128)S(1)} %get-tuple-element.108), channel_id=1, source_target_pairs={{0,2},{2,4},{4,6},{6,7},{7,5},{5,3},{3,1},{1,0},{8,10},{10,12},{12... | collective-permute-start | bytes 442376 | tf_op jit(solution)/shard_map/ppermute | solution.py:580
  25.8 2.0 %collective-permute-start.10 = (f32[288,128]{1,0:T(8,128)S(1)}, f32[288,128]{1,0:T(8,128)S(1)}, u32[]{:S(2)}, u32[]{:S(2)}) collective-permute-start(f32[288,128]{1,0:T(8,128)S(1)} %get-tuple-element.107), channel_id=1, source_target_pairs={{2,0},{4,2},{6,4},{7,6},{5,7},{3,5},{1,3},{0,1},{10,8},{12,10},{14... | collective-permute-start | bytes 442376 | tf_op jit(solution)/shard_map/ppermute | solution.py:580
  27.9 1.2 %shard_map.147 = (f32[8,128]{1,0:T(8,128)S(1)}, f32[576,128]{1,0:T(8,128)S(1)}) custom-call(f32[8,128]{1,0:T(8,128)S(1)} %get-tuple-element.75.refs_0_, bf16[3,576,128]{2,1,0:T(8,128)(2,1)S(1)} %get-tuple-element.76.refs_1_, f32[576,128]{1,0:T(8,128)S(1)} %collective-permute-done.7.refs_2_, f32[2,128]{1,0:T(2,128)S(1)} %bitcast.72, f32[2,128]{1,0:T(2,128)S(1)} %bitcast.76, ...), custom_call_target="tpu_custom_call" | custom-call | bytes 3600000 | tf_op jit(solution)/shard_map/pallas_call | solution.py:389
  30.0 2.6 %collective-permute-done.9.refs_4_ = f32[288,128]{1,0:T(8,128)S(1)} collective-permute-done((f32[288,128]{1,0:T(8,128)S(1)}, f32[288,128]{1,0:T(8,128)S(1)}, u32[]{:S(2)}, u32[]{:S(2)}) %collective-permute-start.9) | collective-permute-done | bytes 147488 | tf_op jit(solution)/shard_map/ppermute | solution.py:580
  32.6 1.6 %collective-permute-start.12 = (f32[288,128]{1,0:T(8,128)S(1)}, f32[288,128]{1,0:T(8,128)S(1)}, u32[]{:S(2)}, u32[]{:S(2)}) collective-permute-start(f32[288,128]{1,0:T(8,128)S(1)} %get-tuple-element.84), channel_id=1, source_target_pairs={{0,2},{2,4},{4,6},{6,7},{7,5},{5,3},{3,1},{1,0},{8,10},{10,12},{12... | collective-permute-start | bytes 442376 | tf_op jit(solution)/shard_map/ppermute | solution.py:580
  35.0 1.8 %collective-permute-start.15 = (f32[288,128]{1,0:T(8,128)S(1)}, f32[288,128]{1,0:T(8,128)S(1)}, u32[]{:S(2)}, u32[]{:S(2)}) collective-permute-start(f32[288,128]{1,0:T(8,128)S(1)} %get-tuple-element.88), channel_id=1, source_target_pairs={{0,2},{2,4},{4,6},{6,7},{7,5},{5,3},{3,1},{1,0},{8,10},{10,12},{12... | collective-permute-start | bytes 442376 | tf_op jit(solution)/shard_map/ppermute | solution.py:580
  37.6 1.7 %collective-permute-done.12.refs_3_ = f32[288,128]{1,0:T(8,128)S(1)} collective-permute-done((f32[288,128]{1,0:T(8,128)S(1)}, f32[288,128]{1,0:T(8,128)S(1)}, u32[]{:S(2)}, u32[]{:S(2)}) %collective-permute-start.12) | collective-permute-done | bytes 147488 | tf_op jit(solution)/shard_map/ppermute | solution.py:580
  39.4 1.6 %collective-permute-start.17 = (f32[288,128]{1,0:T(8,128)S(1)}, f32[288,128]{1,0:T(8,128)S(1)}, u32[]{:S(2)}, u32[]{:S(2)}) collective-permute-start(f32[288,128]{1,0:T(8,128)S(1)} %get-tuple-element.92), channel_id=1, source_target_pairs={{0,2},{2,4},{4,6},{6,7},{7,5},{5,3},{3,1},{1,0},{8,10},{10,12},{12... | collective-permute-start | bytes 442376 | tf_op jit(solution)/shard_map/ppermute | solution.py:580
  41.1 1.4 %collective-permute-done.15.refs_4_ = f32[288,128]{1,0:T(8,128)S(1)} collective-permute-done((f32[288,128]{1,0:T(8,128)S(1)}, f32[288,128]{1,0:T(8,128)S(1)}, u32[]{:S(2)}, u32[]{:S(2)}) %collective-permute-start.15) | collective-permute-done | bytes 147488 | tf_op jit(solution)/shard_map/ppermute | solution.py:580
  42.5 1.2 %shard_map.153 = (f32[8,128]{1,0:T(8,128)S(1)}, f32[576,128]{1,0:T(8,128)S(1)}) custom-call(f32[8,128]{1,0:T(8,128)S(1)} %get-tuple-element.89.refs_0_, bf16[3,576,128]{2,1,0:T(8,128)(2,1)S(1)} %get-tuple-element.76.refs_1_, f32[576,128]{1,0:T(8,128)S(1)} %collective-permute-done.16.refs_2_, f32[2,128]{1,0:T(2,128)S(1)} %bitcast.73, f32[2,128]{1,0:T(2,128)S(1)} %bitcast.77, ...), custom_call_target="tpu_custom_call" | custom-call | bytes 3600000 | tf_op jit(solution)/shard_map/pallas_call | solution.py:389
  43.9 2.0 %collective-permute-start.21 = (f32[288,128]{1,0:T(8,128)S(1)}, f32[288,128]{1,0:T(8,128)S(1)}, u32[]{:S(2)}, u32[]{:S(2)}) collective-permute-start(f32[288,128]{1,0:T(8,128)S(1)} %get-tuple-element.101), channel_id=1, source_target_pairs={{2,0},{4,2},{6,4},{7,6},{5,7},{3,5},{1,3},{0,1},{10,8},{12,10},{14... | collective-permute-start | bytes 442376 | tf_op jit(solution)/shard_map/ppermute | solution.py:580
  45.9 4.6 %collective-permute-done.18.refs_4_ = f32[288,128]{1,0:T(8,128)S(1)} collective-permute-done((f32[288,128]{1,0:T(8,128)S(1)}, f32[288,128]{1,0:T(8,128)S(1)}, u32[]{:S(2)}, u32[]{:S(2)}) %collective-permute-start.18) | collective-permute-done | bytes 147488 | tf_op jit(solution)/shard_map/ppermute | solution.py:580
  50.5 1.7 %collective-permute-start.20 = (f32[288,128]{1,0:T(8,128)S(1)}, f32[288,128]{1,0:T(8,128)S(1)}, u32[]{:S(2)}, u32[]{:S(2)}) collective-permute-start(f32[288,128]{1,0:T(8,128)S(1)} %get-tuple-element.100), channel_id=1, source_target_pairs={{0,2},{2,4},{4,6},{6,7},{7,5},{5,3},{3,1},{1,0},{8,10},{10,12},{12... | collective-permute-start | bytes 442376 | tf_op jit(solution)/shard_map/ppermute | solution.py:580
  52.6 2.9 %shard_map.155 = (f32[8,128]{1,0:T(8,128)S(1)}, f32[576,128]{1,0:T(8,128)}, f32[4,576,128]{2,1,0:T(8,128)}, f32[4,576,128]{2,1,0:T(8,128)}) custom-call(f32[8,128]{1,0:T(8,128)S(1)} %get-tuple-element.94.refs_0_, bf16[3,576,128]{2,1,0:T(8,128)(2,1)S(1)} %get-tuple-element.76.refs_1_, f32[576,128]{1,0:T(8,128)S(1)} %collective-permute-done.19.refs_2_, ...), custom_call_target="tpu_custom_call" | custom-call | bytes 3600000 | tf_op jit(solution)/shard_map/pallas_call | solution.py:389
  55.6 1.0 %collective-permute-done.20.refs_3_ = f32[288,128]{1,0:T(8,128)S(1)} collective-permute-done((f32[288,128]{1,0:T(8,128)S(1)}, f32[288,128]{1,0:T(8,128)S(1)}, u32[]{:S(2)}, u32[]{:S(2)}) %collective-permute-start.20) | collective-permute-done | bytes 147488 | tf_op jit(solution)/shard_map/ppermute | solution.py:580
  56.6 1.3 %collective-permute-done.22.refs_5_ = f32[288,128]{1,0:T(8,128)S(1)} collective-permute-done((f32[288,128]{1,0:T(8,128)S(1)}, f32[288,128]{1,0:T(8,128)S(1)}, u32[]{:S(2)}, u32[]{:S(2)}) %collective-permute-start.22) | collective-permute-done | bytes 147488 | tf_op jit(solution)/shard_map/ppermute | solution.py:580
  (73 shorter events, 10.1 us)
Async XLA Ops:
  4.4 6.4 %collective-permute-start.1 = (f32[576,128]{1,0:T(8,128)}, f32[576,128]{1,0:T(8,128)S(1)}, u32[]{:S(2)}, u32[]{:S(2)}) collective-permute-start(f32[576,128]{1,0:T(8,128)} %get-tuple-element.57.refs_9_), channel_id=1, source_target_pairs={{0,8},{8,16},{16,24},{24,0},{1,9},{9,17},{17,25},{25,1},{2,10},{10... | collective-permute-start | bytes 884744 | tf_op jit(solution)/shard_map/ppermute | solution.py:567
  4.9 5.9 %collective-permute-start = (f32[576,128]{1,0:T(8,128)}, f32[576,128]{1,0:T(8,128)S(1)}, u32[]{:S(2)}, u32[]{:S(2)}) collective-permute-start(f32[576,128]{1,0:T(8,128)} %get-tuple-element.57.refs_9_), channel_id=1, source_target_pairs={{0,8},{8,0},{16,24},{24,16},{1,9},{9,1},{17,25},{25,17},{2,10},{10... | collective-permute-start | bytes 884744 | tf_op jit(solution)/shard_map/ppermute | solution.py:565
  11.8 1.6 %collective-permute-start.2 = (f32[576,128]{1,0:T(8,128)S(1)}, f32[576,128]{1,0:T(8,128)S(1)}, u32[]{:S(2)}, u32[]{:S(2)}) collective-permute-start(f32[576,128]{1,0:T(8,128)S(1)} %get-tuple-element.62.refs_10_), channel_id=1, source_target_pairs={{0,8},{8,0},{16,24},{24,16},{1,9},{9,1},{17,25},{25,17},{2,10},{10... | collective-permute-start | bytes 884744 | tf_op jit(solution)/shard_map/ppermute | solution.py:565
  11.9 6.2 %collective-permute-start.4 = (f32[576,128]{1,0:T(8,128)S(1)}, f32[576,128]{1,0:T(8,128)S(1)}, u32[]{:S(2)}, u32[]{:S(2)}) collective-permute-start(f32[576,128]{1,0:T(8,128)S(1)} %get-tuple-element.62.refs_10_), channel_id=1, source_target_pairs={{0,8},{8,16},{16,24},{24,0},{1,9},{9,17},{17,25},{25,1},{2,10},{10... | collective-permute-start | bytes 884744 | tf_op jit(solution)/shard_map/ppermute | solution.py:567
  14.4 3.6 %collective-permute-start.3 = (f32[576,128]{1,0:T(8,128)S(1)}, f32[576,128]{1,0:T(8,128)S(1)}, u32[]{:S(2)}, u32[]{:S(2)}) collective-permute-start(f32[576,128]{1,0:T(8,128)S(1)} %get-tuple-element.65.refs_11_), channel_id=1, source_target_pairs={{0,8},{8,0},{16,24},{24,16},{1,9},{9,1},{17,25},{25,17},{2,10},{10... | collective-permute-start | bytes 884744 | tf_op jit(solution)/shard_map/ppermute | solution.py:565
  14.6 7.0 %collective-permute-start.6 = (f32[576,128]{1,0:T(8,128)S(1)}, f32[576,128]{1,0:T(8,128)S(1)}, u32[]{:S(2)}, u32[]{:S(2)}) collective-permute-start(f32[576,128]{1,0:T(8,128)S(1)} %get-tuple-element.65.refs_11_), channel_id=1, source_target_pairs={{0,8},{8,16},{16,24},{24,0},{1,9},{9,17},{17,25},{25,1},{2,10},{10... | collective-permute-start | bytes 884744 | tf_op jit(solution)/shard_map/ppermute | solution.py:567
  19.0 2.7 %collective-permute-start.5 = (f32[576,128]{1,0:T(8,128)S(1)}, f32[576,128]{1,0:T(8,128)S(1)}, u32[]{:S(2)}, u32[]{:S(2)}) collective-permute-start(f32[576,128]{1,0:T(8,128)S(1)} %get-tuple-element.72.refs_12_), channel_id=1, source_target_pairs={{0,8},{8,0},{16,24},{24,16},{1,9},{9,1},{17,25},{25,17},{2,10},{10... | collective-permute-start | bytes 884744 | tf_op jit(solution)/shard_map/ppermute | solution.py:565
  19.1 8.8 %collective-permute-start.7 = (f32[576,128]{1,0:T(8,128)S(1)}, f32[576,128]{1,0:T(8,128)S(1)}, u32[]{:S(2)}, u32[]{:S(2)}) collective-permute-start(f32[576,128]{1,0:T(8,128)S(1)} %get-tuple-element.77.refs_6_), channel_id=1, source_target_pairs={{0,8},{8,16},{16,24},{24,0},{1,9},{9,17},{17,25},{25,1},{2,10},{10... | collective-permute-start | bytes 884744 | tf_op jit(solution)/shard_map/ppermute | solution.py:570
  22.7 7.3 %collective-permute-start.8 = (f32[288,128]{1,0:T(8,128)S(1)}, f32[288,128]{1,0:T(8,128)S(1)}, u32[]{:S(2)}, u32[]{:S(2)}) collective-permute-start(f32[288,128]{1,0:T(8,128)S(1)} %get-tuple-element.108), channel_id=1, source_target_pairs={{0,2},{2,4},{4,6},{6,7},{7,5},{5,3},{3,1},{1,0},{8,10},{10,12},{12... | collective-permute-start | bytes 442376 | tf_op jit(solution)/shard_map/ppermute | solution.py:580
  25.8 6.8 %collective-permute-start.9 = (f32[288,128]{1,0:T(8,128)S(1)}, f32[288,128]{1,0:T(8,128)S(1)}, u32[]{:S(2)}, u32[]{:S(2)}) collective-permute-start(f32[288,128]{1,0:T(8,128)S(1)} %get-tuple-element.106), channel_id=1, source_target_pairs={{2,0},{4,2},{6,4},{7,6},{5,7},{3,5},{1,3},{0,1},{10,8},{12,10},{14... | collective-permute-start | bytes 442376 | tf_op jit(solution)/shard_map/ppermute | solution.py:580
  25.8 8.9 %collective-permute-start.10 = (f32[288,128]{1,0:T(8,128)S(1)}, f32[288,128]{1,0:T(8,128)S(1)}, u32[]{:S(2)}, u32[]{:S(2)}) collective-permute-start(f32[288,128]{1,0:T(8,128)S(1)} %get-tuple-element.107), channel_id=1, source_target_pairs={{2,0},{4,2},{6,4},{7,6},{5,7},{3,5},{1,3},{0,1},{10,8},{12,10},{14... | collective-permute-start | bytes 442376 | tf_op jit(solution)/shard_map/ppermute | solution.py:580
  27.8 6.9 %collective-permute-start.11 = (f32[288,128]{1,0:T(8,128)S(1)}, f32[288,128]{1,0:T(8,128)S(1)}, u32[]{:S(2)}, u32[]{:S(2)}) collective-permute-start(f32[288,128]{1,0:T(8,128)S(1)} %get-tuple-element.105), channel_id=1, source_target_pairs={{0,2},{2,4},{4,6},{6,7},{7,5},{5,3},{3,1},{1,0},{8,10},{10,12},{12... | collective-permute-start | bytes 442376 | tf_op jit(solution)/shard_map/ppermute | solution.py:580
  29.1 13.4 %collective-permute-start.16 = (f32[576,128]{1,0:T(8,128)S(1)}, f32[576,128]{1,0:T(8,128)S(1)}, u32[]{:S(2)}, u32[]{:S(2)}) collective-permute-start(f32[576,128]{1,0:T(8,128)S(1)} %get-tuple-element.90.refs_7_), channel_id=1, source_target_pairs={{0,8},{8,16},{16,24},{24,0},{1,9},{9,17},{17,25},{25,1},{2,10},{10... | collective-permute-start | bytes 884744 | tf_op jit(solution)/shard_map/ppermute | solution.py:595
  32.6 6.7 %collective-permute-start.12 = (f32[288,128]{1,0:T(8,128)S(1)}, f32[288,128]{1,0:T(8,128)S(1)}, u32[]{:S(2)}, u32[]{:S(2)}) collective-permute-start(f32[288,128]{1,0:T(8,128)S(1)} %get-tuple-element.84), channel_id=1, source_target_pairs={{0,2},{2,4},{4,6},{6,7},{7,5},{5,3},{3,1},{1,0},{8,10},{10,12},{12... | collective-permute-start | bytes 442376 | tf_op jit(solution)/shard_map/ppermute | solution.py:580
  34.3 5.1 %collective-permute-start.13 = (f32[288,128]{1,0:T(8,128)S(1)}, f32[288,128]{1,0:T(8,128)S(1)}, u32[]{:S(2)}, u32[]{:S(2)}) collective-permute-start(f32[288,128]{1,0:T(8,128)S(1)} %get-tuple-element.85), channel_id=1, source_target_pairs={{2,0},{4,2},{6,4},{7,6},{5,7},{3,5},{1,3},{0,1},{10,8},{12,10},{14... | collective-permute-start | bytes 442376 | tf_op jit(solution)/shard_map/ppermute | solution.py:580
  34.8 6.3 %collective-permute-start.14 = (f32[288,128]{1,0:T(8,128)S(1)}, f32[288,128]{1,0:T(8,128)S(1)}, u32[]{:S(2)}, u32[]{:S(2)}) collective-permute-start(f32[288,128]{1,0:T(8,128)S(1)} %get-tuple-element.87), channel_id=1, source_target_pairs={{2,0},{4,2},{6,4},{7,6},{5,7},{3,5},{1,3},{0,1},{10,8},{12,10},{14... | collective-permute-start | bytes 442376 | tf_op jit(solution)/shard_map/ppermute | solution.py:580
  35.0 7.4 %collective-permute-start.15 = (f32[288,128]{1,0:T(8,128)S(1)}, f32[288,128]{1,0:T(8,128)S(1)}, u32[]{:S(2)}, u32[]{:S(2)}) collective-permute-start(f32[288,128]{1,0:T(8,128)S(1)} %get-tuple-element.88), channel_id=1, source_target_pairs={{0,2},{2,4},{4,6},{6,7},{7,5},{5,3},{3,1},{1,0},{8,10},{10,12},{12... | collective-permute-start | bytes 442376 | tf_op jit(solution)/shard_map/ppermute | solution.py:580
  39.4 6.5 %collective-permute-start.17 = (f32[288,128]{1,0:T(8,128)S(1)}, f32[288,128]{1,0:T(8,128)S(1)}, u32[]{:S(2)}, u32[]{:S(2)}) collective-permute-start(f32[288,128]{1,0:T(8,128)S(1)} %get-tuple-element.92), channel_id=1, source_target_pairs={{0,2},{2,4},{4,6},{6,7},{7,5},{5,3},{3,1},{1,0},{8,10},{10,12},{12... | collective-permute-start | bytes 442376 | tf_op jit(solution)/shard_map/ppermute | solution.py:580
  43.7 8.9 %collective-permute-start.19 = (f32[576,128]{1,0:T(8,128)S(1)}, f32[576,128]{1,0:T(8,128)S(1)}, u32[]{:S(2)}, u32[]{:S(2)}) collective-permute-start(f32[576,128]{1,0:T(8,128)S(1)} %get-tuple-element.95.refs_8_), channel_id=1, source_target_pairs={{0,8},{8,16},{16,24},{24,0},{1,9},{9,17},{17,25},{25,1},{2,10},{10... | collective-permute-start | bytes 884744 | tf_op jit(solution)/shard_map/ppermute | solution.py:595
  43.8 6.7 %collective-permute-start.18 = (f32[288,128]{1,0:T(8,128)S(1)}, f32[288,128]{1,0:T(8,128)S(1)}, u32[]{:S(2)}, u32[]{:S(2)}) collective-permute-start(f32[288,128]{1,0:T(8,128)S(1)} %get-tuple-element.93), channel_id=1, source_target_pairs={{2,0},{4,2},{6,4},{7,6},{5,7},{3,5},{1,3},{0,1},{10,8},{12,10},{14... | collective-permute-start | bytes 442376 | tf_op jit(solution)/shard_map/ppermute | solution.py:580
  43.9 11.7 %collective-permute-start.21 = (f32[288,128]{1,0:T(8,128)S(1)}, f32[288,128]{1,0:T(8,128)S(1)}, u32[]{:S(2)}, u32[]{:S(2)}) collective-permute-start(f32[288,128]{1,0:T(8,128)S(1)} %get-tuple-element.101), channel_id=1, source_target_pairs={{2,0},{4,2},{6,4},{7,6},{5,7},{3,5},{1,3},{0,1},{10,8},{12,10},{14... | collective-permute-start | bytes 442376 | tf_op jit(solution)/shard_map/ppermute | solution.py:580
  45.9 9.7 %collective-permute-start.23 = (f32[288,128]{1,0:T(8,128)S(1)}, f32[288,128]{1,0:T(8,128)S(1)}, u32[]{:S(2)}, u32[]{:S(2)}) collective-permute-start(f32[288,128]{1,0:T(8,128)S(1)} %get-tuple-element.103), channel_id=1, source_target_pairs={{0,2},{2,4},{4,6},{6,7},{7,5},{5,3},{3,1},{1,0},{8,10},{10,12},{12... | collective-permute-start | bytes 442376 | tf_op jit(solution)/shard_map/ppermute | solution.py:580
  50.5 6.0 %collective-permute-start.20 = (f32[288,128]{1,0:T(8,128)S(1)}, f32[288,128]{1,0:T(8,128)S(1)}, u32[]{:S(2)}, u32[]{:S(2)}) collective-permute-start(f32[288,128]{1,0:T(8,128)S(1)} %get-tuple-element.100), channel_id=1, source_target_pairs={{0,2},{2,4},{4,6},{6,7},{7,5},{5,3},{3,1},{1,0},{8,10},{10,12},{12... | collective-permute-start | bytes 442376 | tf_op jit(solution)/shard_map/ppermute | solution.py:580
  52.2 5.7 %collective-permute-start.22 = (f32[288,128]{1,0:T(8,128)S(1)}, f32[288,128]{1,0:T(8,128)S(1)}, u32[]{:S(2)}, u32[]{:S(2)}) collective-permute-start(f32[288,128]{1,0:T(8,128)S(1)} %get-tuple-element.102), channel_id=1, source_target_pairs={{2,0},{4,2},{6,4},{7,6},{5,7},{3,5},{1,3},{0,1},{10,8},{12,10},{14... | collective-permute-start | bytes 442376 | tf_op jit(solution)/shard_map/ppermute | solution.py:580
  (14 other events, 48.1 us)

commit v5 on v4

--- a/solution.py
+++ b/solution.py
@@ -146,14 +146,17 @@
     return rstd
 
 
-def prep_kernel(d, feed_ref, saved_ref, gain_ref, bias_ref, fresh_act_ref, fresh_grad_ref, *refs):
-    slope_ref, normed_ref, rstd_ref, hidden_ref, acts_ref, grads_ref, tmp = refs
-    for k in range(feed_ref.shape[0]):
-        acts_ref[k] = fresh_act_ref[feed_ref[k]]
-        grads_ref[k] = fresh_grad_ref[feed_ref[k]]
-    for t in range(saved_ref.shape[0]):
-        refs = [r.at[t] for r in (slope_ref, normed_ref, hidden_ref)]
-        rstd_ref[t] = prepare(d, saved_ref[t].astype(F32), gain_ref, bias_ref, *refs, tmp)
+def prep_kernel(d, slot, saved_ref, gain_ref, bias_ref, slope_ref, normed_ref, rstd_ref, hidden_ref, tmp):
+    t = jnp.minimum(jnp.maximum(slot - chip(), 0), saved_ref.shape[0] - 1)
+    rstd_ref[...] = prepare(d, saved_ref[t].astype(F32), gain_ref, bias_ref, slope_ref, normed_ref, hidden_ref, tmp)
+
+
+def picked(feed_ref, tick, fresh_ref):
+    index = feed_ref[:, tick - 1 : tick]
+    out = fresh_ref[0].astype(F32)
+    for k in range(1, fresh_ref.shape[0]):
+        out = jnp.where(index == k, fresh_ref[k].astype(F32), out)
+    return out
 
 
 def through_layer(d, cols, weight_ref, slope_ref, normed_ref, rstd, mid, out_ref):
@@ -187,7 +190,7 @@
 
 
 def first_kernel(d, saved_hbm, grad_hbm, gain_hbm, bias_hbm, weight_hbm, *refs):
-    out_ref, saved, grad, gain, bias, weight, slope, normed, hidden, tmp, left, mid, right, cols, sems = refs
+    out_ref, hidden, saved, grad, gain, bias, weight, slope, normed, tmp, left, mid, right, cols, sems = refs
 
     @pl.when(chip() == 0)
     def _():
@@ -207,13 +210,14 @@
     @pl.when(chip() != 0)
     def _():
         out_ref[...] = jnp.zeros_like(out_ref)
+        hidden[...] = jnp.zeros_like(hidden)
 
 
 def chip():
     return lax.axis_index("section") // 2
 
 
-def enter(slot, grad0_ref, grads_ref, inner_ref, outer_ref, e_ref):
+def enter(slot, grad0_ref, feed_ref, fresh_ref, inner_ref, outer_ref, e_ref):
     tick = slot - chip()
     second = lax.axis_index("section") % 2 == 1
 
@@ -229,36 +233,26 @@
     def _():
         e_ref[...] = outer_ref[...]
 
-    @pl.when(jnp.logical_and(tick > 0, lax.axis_index("section") == 0))
-    def _():
-        e_ref[...] = grads_ref[jnp.minimum(jnp.maximum(tick - 1, 0), grads_ref.shape[0] - 1)].astype(F32)
+    if 0 < slot <= feed_ref.shape[1]:
+
+        @pl.when(lax.axis_index("section") == 0)
+        def _():
+            e_ref[...] = picked(feed_ref, slot, fresh_ref)
 
 
 def backward_kernel(
-    d,
-    slot,
-    grad0_ref,
-    grads_ref,
-    inner_ref,
-    outer_ref,
-    slope_ref,
-    normed_ref,
-    rstd_ref,
-    weight_ref,
-    *refs,
+    d, slot, grad0_ref, feed_ref, fresh_ref, inner_ref, outer_ref, slope_ref, normed_ref, rstd_ref, weight_ref, *refs
 ):
-    out_ref, e_ref, left, mid, right, cols = refs[-6:]
+    out_ref, e_ref, left, mid, right, cols = refs
     tick = slot - chip()
-    ticks = slope_ref.shape[0]
-    runs = jnp.logical_and(tick >= 0, tick < ticks)
+    runs = jnp.logical_and(tick >= 0, tick <= feed_ref.shape[1])
 
     @pl.when(runs)
     def _():
-        t = jnp.minimum(jnp.maximum(tick, 0), ticks - 1)
-        enter(slot, grad0_ref, grads_ref, inner_ref, outer_ref, e_ref)
+        enter(slot, grad0_ref, feed_ref, fresh_ref, inner_ref, outer_ref, e_ref)
         spread(e_ref[...], (left, mid, right), d)
         gather_patches((left, mid, right), cols, d)
-        through_layer(d, cols, weight_ref, slope_ref.at[t], normed_ref.at[t], rstd_ref[t], mid, out_ref)
+        through_layer(d, cols, weight_ref, slope_ref, normed_ref, rstd_ref[...], mid, out_ref)
 
     @pl.when(jnp.logical_not(runs))
     def _():
@@ -266,28 +260,23 @@
         e_ref[...] = jnp.zeros_like(e_ref)
 
 
-def forward_kernel(d, tick, chips, grads, fresh_ref, arrived_ref, gain_ref, bias_ref, weight_ref, *refs):
-    stores = []
-    if grads:
-        act_refs, grad_refs, refs = refs[:tick], refs[tick : tick + grads], refs[tick + grads :]
-        out_ref, emitted_ref, returned_ref, left, mid, right, cols, kept, sems = refs
-        for t in range(tick):
-            stores.append(pltpu.make_async_copy(act_refs[t], emitted_ref.at[t], sems.at[t]))
-            stores[-1].start()
-        for t in range(tick + 1):
-            for c in range(chips):
-
-                @pl.when(chip() == c)
-                def _():
-                    pltpu.make_async_copy(grad_refs[t + c], returned_ref.at[t], sems.at[tick + 1 + t]).start()
-
-            stores.append(pltpu.make_async_copy(grad_refs[t], returned_ref.at[t], sems.at[tick + 1 + t]))
+def forward_kernel(d, tick, feed_ref, fresh_ref, arrived_ref, gain_ref, bias_ref, weight_ref, *refs):
+    out_ref, left, mid, right, cols, kept = refs
+    if tick == 0:
+        x = fresh_ref[0].astype(F32)
+        kept[...] = x
     else:
-        out_ref, left, mid, right, cols, kept = refs
-    x = fresh_ref[max(tick - 1, 0)].astype(F32)
-    if tick > 0:
-        x = jnp.where(lax.axis_index("section") == 0, x, arrived_ref[...])
-    kept[...] = x
+        section = lax.axis_index("section")
+
+        @pl.when(section == 0)
+        def _():
+            kept[...] = picked(feed_ref, tick, fresh_ref)
+
+        @pl.when(section != 0)
+        def _():
+            kept[...] = arrived_ref[...]
+
+        x = kept[...]
     normed, _ = normalized(x, d)
     a = normed * pattern(gain_ref, d) + pattern(bias_ref, d)
     hidden = (a * sigmoid(a)).reshape(d.flat, LANES)
@@ -300,54 +289,36 @@
             out_ref[where, :] = (
                 kept[where, :] + conv[n * d.pix : (n + 1) * d.pix, ct * LANES : (ct + 1) * LANES]
             )
-    if grads:
-        stores.append(pltpu.make_async_copy(out_ref, emitted_ref.at[tick], sems.at[tick]))
-        stores[-1].start()
-    for store in stores:
-        store.wait()
-
-
-def weight_kernel(d, ticks, chips, n, positions, factor, grad0_ref, hidden_ref, *refs):
+
+
+def weight_kernel(d, ticks, first, chips, n, positions, factor, grad0_ref, feed_ref, fresh_ref, inner_ref, outer_ref, *refs):
     me = lax.axis_index("dp")
     here = jnp.where(me % 2 == 0, me // 2, n - 1 - me // 2)
     rows = d.n * d.pix
     chunk = 9 * d.c // n
-    last = hidden_ref.shape[0] - 1
-    added = ticks == 0
-    if added:
-        grads_ref, inner_ref, outer_ref = refs[:3]
-        e_refs, refs = refs[3 : 2 + chips], refs[2 + chips :]
-        before, halves = refs[:2], refs[2:4]
-        kept, left, mid, right, cols = refs[4:]
-        h = hidden_ref[last]
-        for c in range(chips - 1):
+    last = feed_ref.shape[1]
+    slots = last + chips
+    span = len(ticks) + chips - 1
+    hidden_refs, refs = refs[:span], refs[span:]
+    e_refs, refs = refs[:span], refs[span:]
+    before, refs = (None, refs) if first else (refs[:2], refs[2:])
+    halves, (kept, left, mid, right, cols, hid) = refs[:2], refs[2:]
+    for i, t in enumerate(ticks):
+        if t == 0:
+            kept[...] = grad0_ref[0].astype(F32)
+        for c in range(chips):
 
             @pl.when(chip() == c)
             def _():
-                kept[...] = e_refs[c][...]
-
-        @pl.when(chip() == chips - 1)
-        def _():
-            enter(last + chips - 1, grad0_ref, grads_ref, inner_ref, outer_ref, kept)
+                hid[i * rows : (i + 1) * rows, :] = hidden_refs[i + c][...]
+                if t + c == slots - 1:
+                    enter(slots - 1, grad0_ref, feed_ref, fresh_ref, inner_ref, outer_ref, kept)
+                elif t > 0:
+                    kept[...] = e_refs[i + c][...]
 
         spread(kept[...], (left, mid, right), d)
-        gather_patches((left, mid, right), cols, d)
-    else:
-        e_refs, halves = refs[: ticks + chips - 2], refs[ticks + chips - 2 : ticks + chips]
-        kept, left, mid, right, cols = refs[ticks + chips :]
-        h = hidden_ref[0:ticks].reshape(ticks * rows, d.c)
-        for t in range(ticks):
-            if t == 0:
-                kept[...] = grad0_ref[0].astype(F32)
-            else:
-                for c in range(chips):
-
-                    @pl.when(chip() == c)
-                    def _():
-                        kept[...] = e_refs[t + c - 1][...]
-
-            spread(kept[...], (left, mid, right), d)
-            gather_patches((left, mid, right), cols.at[t * rows : (t + 1) * rows], d)
+        gather_patches((left, mid, right), cols.at[i * rows : (i + 1) * rows], d)
+    h = hid[...]
     for tap in range(9):
         block = lax.dot_general(
             h, cols[:, (8 - tap) * d.c : (9 - tap) * d.c], (((0,), (0,)), ((), ())), preferred_element_type=F32
@@ -360,14 +331,14 @@
             away = (positions[owner] - here + n) % n
             for i in range(2):
                 piece = block[at - tap * d.c : stop - tap * d.c, i * LANES : (i + 1) * LANES]
-                if added:
+                if not first:
                     piece = piece + before[i][away, where, :]
                 halves[i][away, where, :] = piece
             at = stop
 
 
-def cost(us):
-    return pl.CostEstimate(flops=0, bytes_accessed=int(us * 3.0e6), transcendentals=0)
+def cost(weight):
+    return pl.CostEstimate(flops=weight * 10**9, bytes_accessed=0, transcendentals=0)
 
 
 VMEM = pl.BlockSpec(memory_space=pltpu.VMEM)
@@ -377,26 +348,105 @@
 
 
 class Chain:
-    token = None
-
-    def call(self, body, out_shape, scratch, us, *operands, in_specs=None, out_specs=None, alias=None, vmem=VMEM_LIMIT):
+    def __init__(self, chips, every):
+        self.chips, self.every = chips, every
+        self.tokens = []
+        self.kept = {}
+
+    def call(
+        self,
+        body,
+        out_shape,
+        scratch,
+        weight,
+        *operands,
+        in_specs=None,
+        alias=None,
+        vmem=VMEM_LIMIT,
+        follows=True,
+        passed=(),
+        stores=(),
+        own=None,
+    ):
+        tokens = self.tokens if follows else []
+        names = sorted({s[0] for s in stores} | ({own[0]} if own else set()))
+        sources = [v for s in stores for v in s[2]]
+        old = [self.kept[k] for k in names if k in self.kept]
+        counts = [len(tokens), len(operands), len(passed), len(sources), len(old), 1, len(out_shape), len(passed), len(names)]
+        starts = [sum(counts[:i]) for i in range(len(counts) + 1)]
+
         def chained(*refs):
-            after = refs[held + count]
-            after[...] = refs[0][...] if held else jnp.zeros_like(after)
-            body(*refs[held : held + count], *refs[held + count + 1 :])
-
-        count, held = len(operands), int(self.token is not None)
-        self.token, *outs = pl.pallas_call(
+            groups = [refs[starts[i] : starts[i + 1]] for i in range(len(counts))]
+            rest = refs[starts[-1] :]
+            outs, kept = groups[6], dict(zip(names, groups[8]))
+            waits = []
+
+            def send(source, name, tick, sem):
+                copy = pltpu.make_async_copy(source, kept[name].at[tick], sem)
+                copy.start()
+                return copy
+
+            if names:
+                *rest, sems = rest
+                from_refs = list(groups[3])
+                for i, (name, tick, per_chip) in enumerate(stores):
+                    mine, from_refs = from_refs[: len(per_chip)], from_refs[len(per_chip) :]
+                    if len(mine) == 1:
+                        waits.append(send(mine[0], name, tick, sems.at[i]))
+                        continue
+                    for c in range(len(mine)):
+
+                        @pl.when(chip() == c)
+                        def _():
+                            send(mine[c], name, tick, sems.at[i])
+
+                    waits.append(pltpu.make_async_copy(mine[0], kept[name].at[tick], sems.at[i]))
+            total = jnp.zeros((8, LANES), F32)
+            for ref in groups[0]:
+                total = total + ref[...]
+            groups[5][0][...] = total
+            body(*groups[1], *outs, *rest)
+            if own:
+                name, tick, where = own
+                if where is None:
+                    waits.append(send(outs[0], name, tick, sems.at[len(stores)]))
+                else:
+
+                    @pl.when(chip() == where)
+                    def _():
+                        send(outs[0], name, tick, sems.at[len(stores)]).wait()
+
+            for copy in waits:
+                copy.wait()
+
+        aliases = {starts[1] + i: starts[6] - starts[5] + o for i, o in (alias or {}).items()}
+        aliases |= {starts[2] + i: 1 + len(out_shape) + i for i in range(len(passed))}
+        aliases |= {
+            starts[4] + i: 1 + len(out_shape) + len(passed) + names.index(k)
+            for i, k in enumerate([k for k in names if k in self.kept])
+        }
+        token, *outs = pl.pallas_call(
             chained,
-            out_shape=(jax.ShapeDtypeStruct((8, LANES), F32), *out_shape),
-            in_specs=[VMEM] * held + (in_specs or [VMEM] * count),
-            out_specs=(VMEM, *(out_specs or [VMEM] * len(out_shape))),
-            scratch_shapes=scratch,
+            out_shape=(
+                jax.ShapeDtypeStruct((8, LANES), F32),
+                *out_shape,
+                *[jax.ShapeDtypeStruct(v.shape, v.dtype) for v in passed],
+                *[self.every] * len(names),
+            ),
+            in_specs=[VMEM] * len(tokens)
+            + (in_specs or [VMEM] * len(operands))
+            + [VMEM] * len(passed)
+            + [ANY] * (len(sources) + len(old)),
+            out_specs=[VMEM] * (1 + len(out_shape) + len(passed)) + [ANY] * len(names),
+            scratch_shapes=[*scratch] + ([pltpu.SemaphoreType.DMA((len(stores) + 1,))] if names else []),
             compiler_params=pltpu.CompilerParams(vmem_limit_bytes=vmem),
-            cost_estimate=cost(us),
-            input_output_aliases={i + held: o + 1 for i, o in (alias or {}).items()},
-        )(*([self.token] * held), *operands)
-        return outs
+            cost_estimate=cost(weight),
+            input_output_aliases=aliases,
+        )(*tokens, *operands, *passed, *sources, *old)
+        self.tokens = [token] if follows else self.tokens + [token]
+        for k, v in zip(names, outs[len(out_shape) + len(passed) :]):
+            self.kept[k] = v
+        return outs[: len(out_shape) + len(passed)]
 
 
 def add_kernel(up_offset, down_offset, first_terms, second_terms, first, second, first_out, second_out):
@@ -435,6 +485,7 @@
     fresh_act = interleaved(fresh_images, d)
     fresh_grad = interleaved(fresh_gradients, d)
     saved = interleaved(saved_inputs[:, 0], d)
+    feed = feed_order.reshape(1, -1)
     fgain, fbias, bgain, bbias = [
         v[0].reshape(d.cts, LANES) for v in (forward_gain, forward_bias, backward_gain, backward_bias)
     ]
@@ -458,17 +509,16 @@
     def later(shape, dtype):
         return jax.ShapeDtypeStruct((last, *shape), dtype)
 
-    chain = Chain()
+    chain = Chain(chips, every)
 
     def first():
         return chain.call(
             functools.partial(first_kernel, d),
-            (msg,),
-            [raw, raw, vector, vector, pltpu.VMEM(backward_weight.shape[1:], BF16), whole, whole]
-            + [pltpu.VMEM((rows, d.c), BF16), flat]
+            (msg, narrow),
+            [raw, raw, vector, vector, pltpu.VMEM(backward_weight.shape[1:], BF16), whole, whole, flat]
             + [padded] * 3
             + [cols, sem((5,))],
-            2.5,
+            0,
             saved,
             grad0,
             bgain,
@@ -478,56 +528,48 @@
             vmem=WHOLE_VMEM,
         )
 
-    def prep():
-        def all_ticks(shape, dtype, count=ticks):
-            return jax.ShapeDtypeStruct((count, *shape), dtype)
-
-        entering = all_ticks((d.flat, LANES), BF16, last)
-        wide = all_ticks((rows, d.c), F32)
+    def prep(slot):
         return chain.call(
-            functools.partial(prep_kernel, d),
-            (wide, wide, all_ticks((8, LANES), F32), all_ticks((rows, d.c), BF16), entering, entering),
+            functools.partial(prep_kernel, d, slot),
+            (wide, wide, jax.ShapeDtypeStruct((8, LANES), F32), narrow),
             [flat],
-            2.0,
-            feed_order,
+            0,
             saved,
             bgain,
             bbias,
-            fresh_act,
-            fresh_grad,
-            in_specs=[SMEM] + [VMEM] * 5,
         )
 
-    def backward(slot, inner, outer):
+    def backward(slot, inner, outer, slope, normed, rstd, **more):
         return chain.call(
             functools.partial(backward_kernel, d, slot),
             (msg, msg),
             [padded] * 3 + [cols],
-            0.9,
+            0,
             grad0,
-            grads,
+            feed,
+            fresh_grad,
             inner,
             outer,
             slope,
             normed,
             rstd,
             backward_weight[0],
+            **more,
         )
 
-    def forward(t, arrived, *collected):
+    def forward(t, arrived, **more):
         return chain.call(
-            functools.partial(forward_kernel, d, t, chips, len(collected) - t if collected else 0),
-            (msg, every, every) if collected else (msg,),
-            [padded] * 3 + [cols, flat] + ([sem((2 * ticks,))] if collected else []),
-            1.2,
-            acts if t else act0,
+            functools.partial(forward_kernel, d, t),
+            (msg,),
+            [padded] * 3 + [cols, flat],
+            0,
+            feed,
+            fresh_act if t else act0,
             arrived,
             fgain,
             fbias,
             forward_weight[0],
-            *collected,
-            in_specs=[VMEM] * 5 + [ANY] * len(collected),
-            out_specs=(VMEM, ANY, ANY) if collected else None,
+            **more,
         )
 
     n = lax.axis_size("dp")
@@ -536,40 +578,55 @@
     chunk = 9 * d.c // n
     half = jax.ShapeDtypeStruct((n, chunk, LANES), F32)
 
-    def weight_terms(ticks, *operands):
-        count = max(ticks, 1)
+    def weight_terms(ticks, inner, outer, *before, passed=()):
+        span = slice(ticks[0], ticks[-1] + chips)
+        operands = hidden[span] + [e if e is not None else grad0 for e in (entered + [None])[span]]
         return chain.call(
-            functools.partial(weight_kernel, d, ticks, chips, n, positions, 1.0 / (n * d.n)),
+            functools.partial(weight_kernel, d, ticks, not before, chips, n, positions, 1.0 / (n * d.n)),
             (half,) * 2,
-            [flat] + [padded] * 3 + [pltpu.VMEM((count * rows, 9 * d.c), BF16)],
-            0.6 * count,
+            [flat]
+            + [padded] * 3
+            + [pltpu.VMEM((len(ticks) * rows, 9 * d.c), BF16), pltpu.VMEM((len(ticks) * rows, d.c), BF16)],
+            0,
             grad0,
-            hidden,
+            feed,
+            fresh_grad,
+            inner,
+            outer,
             *operands,
-            alias={} if ticks else {len(operands) + i: i for i in range(2)},
+            *before,
+            alias={5 + len(operands) + i: i for i in range(len(before))},
+            passed=passed,
         )
 
     slots = ticks + chips - 1
-    gradients, entered, inner, outer = first(), [None], [], []
-    slope, normed, rstd, hidden, acts, grads = prep()
-    arrived, outputs = jnp.zeros((8, LANES), F32), []
+    out, h = first()
+    gradients, hidden, entered, inner, outer = [out], [h], [None], [], []
+    outputs = []
 
     def arrivals(slot):
-        return inner[slot - 1], outer[max(slot - 2, 0)]
-
+        return inner[slot - 1], outer[slot - 2] if slot > 1 else inner[0]
+
+    prepared = [None]
     for slot in range(slots - 1):
         if slot > 0:
-            out, e = backward(slot, *arrivals(slot))
+            out, e = backward(slot, *arrivals(slot), *prepared[slot])
             gradients.append(out)
             entered.append(e)
         inner.append(lax.ppermute(gradients[slot], "section", inside))
         if slot < slots - 2:
             outer.append(lax.ppermute(gradients[slot], "section", ring))
+            *ready, h = prep(slot + 1)
+            prepared.append(ready)
+            hidden.append(h)
         if slot == slots - 3:
-            outputs += forward(0, arrived)
+            outputs += forward(0, inner[0])
             arrived = lax.ppermute(outputs[0], "section", ring)
-    before = weight_terms(last, *entered[1 : last + chips - 1])
-    terms = weight_terms(0, grads, *arrivals(slots - 1), *entered[last : last + chips - 1], *before)
+            *ready, h = prep(slot + 2)
+            prepared.append(ready)
+            hidden.append(h)
+    terms = weight_terms(range(last), inner[0], inner[0])
+    terms = weight_terms([last], *arrivals(slots - 1), *terms)
 
     onward = [(order[i], order[(i + 1) % n]) for i in range(n)]
     back = [(b, a) for a, b in onward]
@@ -587,30 +644,40 @@
 
     def added(pair, up, down):
         return chain.call(
-            functools.partial(add_kernel, up % n, down % n), (piece,) * 2, [], 0.2, *terms, *pair
+            functools.partial(add_kernel, up % n, down % n), (piece,) * 2, [], 3, *terms, *pair
         )
 
-    def forward_step(t, arrived):
-        outputs.extend(forward(t, arrived))
+    def returned(t):
+        return ("returned", t, gradients[t : t + chips])
+
+    def emitted(t):
+        return ("emitted", t, outputs[t : t + 1])
+
+    def forward_step(t, arrived, **more):
+        outputs.extend(forward(t, arrived, **more))
         return lax.ppermute(outputs[t], "section", ring)
 
     long = long_hop([terms[0][hops], terms[1][n - hops]])
     short = short_hop([terms[0][n - hops + 1], terms[1][hops - 1]])
-    arrived = forward_step(1, arrived)
+    arrived = forward_step(1, arrived, stores=[emitted(0)] + [returned(t) for t in range(last - 1)])
     for hop in range(1, hops):
         long = long_hop(added(long, hops - hop, hop - hops))
         if hop < hops - 1:
             short = short_hop(added(short, hop + 1 - hops, hops - 1 - hop))
-        if hop == 1:
-            out, _ = backward(slots - 1, *arrivals(slots - 1))
+        if hop < last - 1:
+            arrived = forward_step(hop + 1, arrived, stores=[emitted(hop), returned(last - 1)] if hop == 1 else [emitted(hop)])
+        if hop == last - 1:
+            out, _ = backward(slots - 1, *arrivals(slots - 1), *prepared[slots - 1], stores=[emitted(last - 1)])
             gradients.append(out)
-        if 1 < hop < last:
-            arrived = forward_step(hop, arrived)
-    _, emitted, returned = forward(last, arrived, *outputs, *gradients)
+    forward(last, arrived, stores=[returned(last)], own=("emitted", last, None))
     (shard_sum,) = chain.call(
-        final_kernel, (jax.ShapeDtypeStruct((chunk, d.c), F32),), [], 0.4, *terms, *long[:1], *short[:1], *long[1:], *short[1:]
+        final_kernel, (jax.ShapeDtypeStruct((chunk, d.c), F32),), [], 0, *terms, *long[:1], *short[:1], *long[1:], *short[1:]
     )
-    return standard(emitted, d)[:, None], standard(returned, d)[:, None], shard_sum[None]
+    return (
+        standard(chain.kept["emitted"], d)[:, None],
+        standard(chain.kept["returned"], d)[:, None],
+        shard_sum[None],
+    )
 
 
 def solution(mesh):

time: 58.8 us -> 53.2 us (0.905)
  waiting for transfers between devices: 19.3 us -> 11 us
  Pallas kernels: 20 us -> 22.4 us
    ppermute x14, waiting for transfers between devices: 13.5 us -> 7.25 us  [swapped(): return [lax.ppermute(v, 'dp', way) for v, way in zip((first, second), ways)]]
    ppermute x3, waiting for transfers between devices: 4.72 us -> 2.23 us  [shards(): outer.append(lax.ppermute(gradients[slot], 'section', ring))]
    pallas_call x18 -> x21, Pallas kernels: 20 us -> 22.4 us  [call(): pl.pallas_call(chained, out_shape=(jax.ShapeDtypeStruct((8, LANES), F32),...]
    ppermute x2, waiting for transfers between devices: 0.01 us -> 1.46 us  [forward_step(): return lax.ppermute(outputs[t], 'section', ring)]
    ppermute x4, waiting for transfers between devices: 1.08 us -> 0.01 us  [shards(): inner.append(lax.ppermute(gradients[slot], 'section', inside))]
  transfers between devices with their start and end apart: 24 -> 24, of which waited for: 11 -> 9; matrix products, arithmetic and copies ran while one was open for 0% -> 0% of each run, Pallas kernels for 25% -> 34%
where the time goes in v5:
time: 53.2 us; the launch traced here: 53.1 us
  Pallas kernels  22.4 us (42%)
  starting transfers between devices  17.8 us (33%)
  waiting for transfers between devices  11 us (21%)
  between operations  1.06 us (2%)
  local copies, waits for them, and re-layouts  0.79 us (1%)
    pallas_call x21, Pallas kernels, call(): pl.pallas_call(chained, out_shape=(jax.ShapeDtypeStruct((8, LANES), F32),...  22.4 us
    ppermute x14, starting transfers between devices, swapped(): return [lax.ppermute(v, 'dp', way) for v, way in zip((first, second), ways)]  15.2 us
    ppermute x14, waiting for transfers between devices, swapped(): return [lax.ppermute(v, 'dp', way) for v, way in zip((first, second), ways)]  7.25 us
    ppermute x3, waiting for transfers between devices, shards(): outer.append(lax.ppermute(gradients[slot], 'section', ring))  2.23 us
    ppermute x2, waiting for transfers between devices, forward_step(): return lax.ppermute(outputs[t], 'section', ring)  1.46 us
  transfers between devices with their start and end apart: 24, of which 9 were waited for; matrix products, arithmetic and copies ran while one was open for 0% of the time, Pallas kernels for 34%

profile of v5, /device:TPU:0, one launch (start us, length us, event | category | flops | bytes accessed | tf_op | source)
XLA Modules:
  0.0 53.1 jit_solution(5618776494652641194)
XLA Ops:
  0.7 3.8 %shard_map.139 = (f32[8,128]{1,0:T(8,128)}, f32[576,128]{1,0:T(8,128)}, bf16[288,256]{1,0:T(8,128)(2,1)}) custom-call(bf16[4,576,128]{2,1,0:T(8,128)(2,1)} %bitcast.66, bf16[1,576,128]{2,1,0:T(8,128)(2,1)} %bitcast.71, f32[2,128]{1,0:T(2,128)} %bitcast.94, f32[2,128]{1,0:T(2,128)} %bitcast.99, bf16[2304,256]{1,0:T(8,128)(2,1)} %bitcast.51), custom_call_target="tpu_custom_call" | custom-call | tf_op jit(solution)/shard_map/pallas_call | solution.py:428
  6.7 1.1 %shard_map.141 = (f32[8,128]{1,0:T(8,128)S(1)}, f32[576,128]{1,0:T(8,128)S(1)}, f32[576,128]{1,0:T(8,128)S(1)}) custom-call(f32[8,128]{1,0:T(8,128)S(1)} %get-tuple-element.74.refs_0_, bf16[1,576,128]{2,1,0:T(8,128)(2,1)S(1)} %bitcast.72, s32[1,3]{1,0:T(1,128)S(1)} %bitcast.84, bf16[3,576,128]{2,1,0:T(8,128)(2,1)S(1)} %bitcast.60, ...), custom_call_target="tpu_custom_call" | custom-call | tf_op jit(solution)/shard_map/pallas_call | solution.py:428
  9.2 2.2 %collective-permute-done.2.refs_5_ = f32[576,128]{1,0:T(8,128)S(1)} collective-permute-done((f32[576,128]{1,0:T(8,128)}, f32[576,128]{1,0:T(8,128)S(1)}, u32[]{:S(2)}, u32[]{:S(2)}) %collective-permute-start.2) | collective-permute-done | bytes 294944 | tf_op jit(solution)/shard_map/ppermute | solution.py:618
  11.4 1.0 %shard_map.143 = (f32[8,128]{1,0:T(8,128)S(1)}, f32[576,128]{1,0:T(8,128)S(1)}, f32[576,128]{1,0:T(8,128)S(1)}) custom-call(f32[8,128]{1,0:T(8,128)S(1)} %get-tuple-element.80.refs_0_, bf16[1,576,128]{2,1,0:T(8,128)(2,1)S(1)} %bitcast.73, s32[1,3]{1,0:T(1,128)S(1)} %bitcast.85, bf16[3,576,128]{2,1,0:T(8,128)(2,1)S(1)} %bitcast.61, ...), custom_call_target="tpu_custom_call" | custom-call | tf_op jit(solution)/shard_map/pallas_call | solution.py:428
  13.9 1.2 %shard_map.145 = (f32[8,128]{1,0:T(8,128)S(1)}, f32[576,128]{1,0:T(8,128)S(1)}) custom-call(f32[8,128]{1,0:T(8,128)S(1)} %get-tuple-element.86.refs_0_, s32[1,3]{1,0:T(1,128)S(1)} %bitcast.86, bf16[1,576,128]{2,1,0:T(8,128)(2,1)S(1)} %bitcast.83, f32[576,128]{1,0:T(8,128)S(1)} %collective-permute-done.refs_4_.refs_5_.refs_3_, f32[2,128]{1,0:T(2,128)S(1)} %bitcast.104, ...), custom_call_target="tpu_custom_call" | custom-call | tf_op jit(solution)/shard_map/pallas_call | solution.py:428
  16.0 1.1 %shard_map.147 = (f32[8,128]{1,0:T(8,128)S(1)}, f32[576,128]{1,0:T(8,128)S(1)}, f32[576,128]{1,0:T(8,128)S(1)}) custom-call(f32[8,128]{1,0:T(8,128)S(1)} %get-tuple-element.88.refs_0_, bf16[1,576,128]{2,1,0:T(8,128)(2,1)S(1)} %bitcast.74, s32[1,3]{1,0:T(1,128)S(1)} %bitcast.87, bf16[3,576,128]{2,1,0:T(8,128)(2,1)S(1)} %bitcast.62, ...), custom_call_target="tpu_custom_call" | custom-call | tf_op jit(solution)/shard_map/pallas_call | solution.py:428
  17.7 2.1 %shard_map.148 = (f32[8,128]{1,0:T(8,128)S(1)}, f32[8,288,128]{2,1,0:T(8,128)S(1)}, f32[8,288,128]{2,1,0:T(8,128)S(1)}) custom-call(f32[8,128]{1,0:T(8,128)S(1)} %get-tuple-element.93.refs_0_, bf16[1,576,128]{2,1,0:T(8,128)(2,1)S(1)} %bitcast.75, s32[1,3]{1,0:T(1,128)S(1)} %bitcast.88, bf16[3,576,128]{2,1,0:T(8,128)(2,1)S(1)} %bitcast.63, ...), custom_call_target="tpu_custom_call" | custom-call | tf_op jit(solution)/shard_map/pallas_call | solution.py:428
  19.7 1.0 %shard_map.149 = (f32[8,128]{1,0:T(8,128)S(1)}, f32[8,288,128]{2,1,0:T(8,128)S(1)}, f32[8,288,128]{2,1,0:T(8,128)S(1)}) custom-call(f32[8,128]{1,0:T(8,128)S(1)} %get-tuple-element.101.refs_0_, bf16[1,576,128]{2,1,0:T(8,128)(2,1)S(1)} %bitcast.77, s32[1,3]{1,0:T(1,128)S(1)} %bitcast.89, ...), custom_call_target="tpu_custom_call", output_to_operand_aliasing={{1}: (10, {}), {2}: (11, {})} | custom-call | tf_op jit(solution)/shard_map/pallas_call | solution.py:428
  20.8 2.7 %collective-permute-start.8 = (f32[288,128]{1,0:T(8,128)S(1)}, f32[288,128]{1,0:T(8,128)S(1)}, u32[]{:S(2)}, u32[]{:S(2)}) collective-permute-start(f32[288,128]{1,0:T(8,128)S(1)} %get-tuple-element.146), channel_id=1, source_target_pairs={{0,2},{2,4},{4,6},{6,7},{7,5},{5,3},{3,1},{1,0},{8,10},{10,12},{12... | collective-permute-start | bytes 442376 | tf_op jit(solution)/shard_map/ppermute | solution.py:637
  23.5 2.0 %collective-permute-start.10 = (f32[288,128]{1,0:T(8,128)S(1)}, f32[288,128]{1,0:T(8,128)S(1)}, u32[]{:S(2)}, u32[]{:S(2)}) collective-permute-start(f32[288,128]{1,0:T(8,128)S(1)} %get-tuple-element.145), channel_id=1, source_target_pairs={{2,0},{4,2},{6,4},{7,6},{5,7},{3,5},{1,3},{0,1},{10,8},{12,10},{14... | collective-permute-start | bytes 442376 | tf_op jit(solution)/shard_map/ppermute | solution.py:637
  25.6 1.3 %shard_map.150 = (f32[8,128]{1,0:T(8,128)S(1)}, f32[576,128]{1,0:T(8,128)S(1)}, f32[4,576,128]{2,1,0:T(8,128)}, f32[4,576,128]{2,1,0:T(8,128)}) custom-call(f32[8,128]{1,0:T(8,128)S(1)} %get-tuple-element.106.refs_0_, s32[1,3]{1,0:T(1,128)S(1)} %bitcast.90, bf16[3,576,128]{2,1,0:T(8,128)(2,1)S(1)} %bitcast.80, ...), custom_call_target="tpu_custom_call" | custom-call | tf_op jit(solution)/shard_map/pallas_call | solution.py:428
  27.7 2.6 %collective-permute-done.9.refs_4_ = f32[288,128]{1,0:T(8,128)S(1)} collective-permute-done((f32[288,128]{1,0:T(8,128)S(1)}, f32[288,128]{1,0:T(8,128)S(1)}, u32[]{:S(2)}, u32[]{:S(2)}) %collective-permute-start.9) | collective-permute-done | bytes 147488 | tf_op jit(solution)/shard_map/ppermute | solution.py:637
  30.3 1.6 %collective-permute-start.13 = (f32[288,128]{1,0:T(8,128)S(1)}, f32[288,128]{1,0:T(8,128)S(1)}, u32[]{:S(2)}, u32[]{:S(2)}) collective-permute-start(f32[288,128]{1,0:T(8,128)S(1)} %get-tuple-element.117), channel_id=1, source_target_pairs={{0,2},{2,4},{4,6},{6,7},{7,5},{5,3},{3,1},{1,0},{8,10},{10,12},{12... | collective-permute-start | bytes 442376 | tf_op jit(solution)/shard_map/ppermute | solution.py:637
  32.4 1.0 %collective-permute-done.10.refs_3_ = f32[288,128]{1,0:T(8,128)S(1)} collective-permute-done((f32[288,128]{1,0:T(8,128)S(1)}, f32[288,128]{1,0:T(8,128)S(1)}, u32[]{:S(2)}, u32[]{:S(2)}) %collective-permute-start.10) | collective-permute-done | bytes 147488 | tf_op jit(solution)/shard_map/ppermute | solution.py:637
  33.5 2.0 %collective-permute-start.16 = (f32[288,128]{1,0:T(8,128)S(1)}, f32[288,128]{1,0:T(8,128)S(1)}, u32[]{:S(2)}, u32[]{:S(2)}) collective-permute-start(f32[288,128]{1,0:T(8,128)S(1)} %get-tuple-element.121), channel_id=1, source_target_pairs={{0,2},{2,4},{4,6},{6,7},{7,5},{5,3},{3,1},{1,0},{8,10},{10,12},{12... | collective-permute-start | bytes 442376 | tf_op jit(solution)/shard_map/ppermute | solution.py:637
  35.5 1.5 %shard_map.153 = (f32[8,128]{1,0:T(8,128)S(1)}, f32[576,128]{1,0:T(8,128)S(1)}, f32[4,576,128]{2,1,0:T(8,128)}, f32[4,576,128]{2,1,0:T(8,128)}) custom-call(f32[8,128]{1,0:T(8,128)S(1)} %get-tuple-element.112.refs_0_, s32[1,3]{1,0:T(1,128)S(1)} %bitcast.91, bf16[3,576,128]{2,1,0:T(8,128)(2,1)S(1)} %bitcast.81, ...), custom_call_target="tpu_custom_call", output_to_operand_aliasing={{2}: (10, {}), {3}: (11, {})} | custom-call | tf_op jit(solution)/shard_map/pallas_call | solution.py:428
  37.0 1.7 %collective-permute-done.14.refs_4_ = f32[288,128]{1,0:T(8,128)S(1)} collective-permute-done((f32[288,128]{1,0:T(8,128)S(1)}, f32[288,128]{1,0:T(8,128)S(1)}, u32[]{:S(2)}, u32[]{:S(2)}) %collective-permute-start.14) | collective-permute-done | bytes 147488 | tf_op jit(solution)/shard_map/ppermute | solution.py:637
  38.7 1.6 %collective-permute-start.17 = (f32[288,128]{1,0:T(8,128)S(1)}, f32[288,128]{1,0:T(8,128)S(1)}, u32[]{:S(2)}, u32[]{:S(2)}) collective-permute-start(f32[288,128]{1,0:T(8,128)S(1)} %get-tuple-element.129), channel_id=1, source_target_pairs={{0,2},{2,4},{4,6},{6,7},{7,5},{5,3},{3,1},{1,0},{8,10},{10,12},{12... | collective-permute-start | bytes 442376 | tf_op jit(solution)/shard_map/ppermute | solution.py:637
  40.8 1.5 %collective-permute-start.21 = (f32[288,128]{1,0:T(8,128)S(1)}, f32[288,128]{1,0:T(8,128)S(1)}, u32[]{:S(2)}, u32[]{:S(2)}) collective-permute-start(f32[288,128]{1,0:T(8,128)S(1)} %get-tuple-element.139), channel_id=1, source_target_pairs={{2,0},{4,2},{6,4},{7,6},{5,7},{3,5},{1,3},{0,1},{10,8},{12,10},{14... | collective-permute-start | bytes 442376 | tf_op jit(solution)/shard_map/ppermute | solution.py:637
  42.9 1.4 %shard_map.156 = (f32[8,128]{1,0:T(8,128)S(1)}, f32[576,128]{1,0:T(8,128)S(1)}, f32[576,128]{1,0:T(8,128)}, f32[4,576,128]{2,1,0:T(8,128)}) custom-call(f32[8,128]{1,0:T(8,128)S(1)} %get-tuple-element.122.refs_0_, bf16[1,576,128]{2,1,0:T(8,128)(2,1)S(1)} %bitcast.79, s32[1,3]{1,0:T(1,128)S(1)} %bitcast.92, ...), custom_call_target="tpu_custom_call", output_to_operand_aliasing={{3}: (11, {})} | custom-call | tf_op jit(solution)/shard_map/pallas_call | solution.py:428
  44.4 1.0 %collective-permute-done.17.refs_3_ = f32[288,128]{1,0:T(8,128)S(1)} collective-permute-done((f32[288,128]{1,0:T(8,128)S(1)}, f32[288,128]{1,0:T(8,128)S(1)}, u32[]{:S(2)}, u32[]{:S(2)}) %collective-permute-start.17) | collective-permute-done | bytes 147488 | tf_op jit(solution)/shard_map/ppermute | solution.py:637
  45.5 1.6 %collective-permute-start.20 = (f32[288,128]{1,0:T(8,128)S(1)}, f32[288,128]{1,0:T(8,128)S(1)}, u32[]{:S(2)}, u32[]{:S(2)}) collective-permute-start(f32[288,128]{1,0:T(8,128)S(1)} %get-tuple-element.138), channel_id=1, source_target_pairs={{0,2},{2,4},{4,6},{6,7},{7,5},{5,3},{3,1},{1,0},{8,10},{10,12},{12... | collective-permute-start | bytes 442376 | tf_op jit(solution)/shard_map/ppermute | solution.py:637
  47.6 1.5 %collective-permute-done.19.refs_3_ = f32[576,128]{1,0:T(8,128)S(1)} collective-permute-done((f32[576,128]{1,0:T(8,128)S(1)}, f32[576,128]{1,0:T(8,128)S(1)}, u32[]{:S(2)}, u32[]{:S(2)}) %collective-permute-start.19) | collective-permute-done | bytes 294944 | tf_op jit(solution)/shard_map/ppermute | solution.py:658
  49.1 2.7 %shard_map.158 = (f32[8,128]{1,0:T(8,128)S(1)}, f32[576,128]{1,0:T(8,128)}, f32[4,576,128]{2,1,0:T(8,128)}, f32[4,576,128]{2,1,0:T(8,128)}) custom-call(f32[8,128]{1,0:T(8,128)S(1)} %get-tuple-element.131.refs_0_, s32[1,3]{1,0:T(1,128)S(1)} %bitcast.93, bf16[3,576,128]{2,1,0:T(8,128)(2,1)S(1)} %bitcast.82, ...), custom_call_target="tpu_custom_call", output_to_operand_aliasing={{2}: (9, {}), {3}: (10, {})} | custom-call | tf_op jit(solution)/shard_map/pallas_call | solution.py:428
  (77 shorter events, 10.9 us)
Async XLA Ops:
  4.5 2.1 %collective-permute-start = (f32[576,128]{1,0:T(8,128)}, f32[576,128]{1,0:T(8,128)S(1)}, u32[]{:S(2)}, u32[]{:S(2)}) collective-permute-start(f32[576,128]{1,0:T(8,128)} %get-tuple-element.75.refs_8_), channel_id=1, source_target_pairs={{0,8},{8,0},{16,24},{24,16},{1,9},{9,1},{17,25},{25,17},{2,10},{10... | collective-permute-start | bytes 884744 | tf_op jit(solution)/shard_map/ppermute | solution.py:616
  5.0 6.4 %collective-permute-start.2 = (f32[576,128]{1,0:T(8,128)}, f32[576,128]{1,0:T(8,128)S(1)}, u32[]{:S(2)}, u32[]{:S(2)}) collective-permute-start(f32[576,128]{1,0:T(8,128)} %get-tuple-element.75.refs_8_), channel_id=1, source_target_pairs={{0,8},{8,16},{16,24},{24,0},{1,9},{9,17},{17,25},{25,1},{2,10},{10... | collective-permute-start | bytes 884744 | tf_op jit(solution)/shard_map/ppermute | solution.py:618
  7.8 3.6 %collective-permute-start.1 = (f32[576,128]{1,0:T(8,128)S(1)}, f32[576,128]{1,0:T(8,128)S(1)}, u32[]{:S(2)}, u32[]{:S(2)}) collective-permute-start(f32[576,128]{1,0:T(8,128)S(1)} %get-tuple-element.81.refs_9_.refs_10_), channel_id=1, source_target_pairs={{0,8},{8,0},{16,24},{24,16},{1,9},{9,1},{17,25},{25,17},{2,10},{10... | collective-permute-start | bytes 884744 | tf_op jit(solution)/shard_map/ppermute | solution.py:616
  7.9 8.1 %collective-permute-start.4 = (f32[576,128]{1,0:T(8,128)S(1)}, f32[576,128]{1,0:T(8,128)S(1)}, u32[]{:S(2)}, u32[]{:S(2)}) collective-permute-start(f32[576,128]{1,0:T(8,128)S(1)} %get-tuple-element.81.refs_9_.refs_10_), channel_id=1, source_target_pairs={{0,8},{8,16},{16,24},{24,0},{1,9},{9,17},{17,25},{25,1},{2,10},{10... | collective-permute-start | bytes 884744 | tf_op jit(solution)/shard_map/ppermute | solution.py:618
  12.5 3.5 %collective-permute-start.3 = (f32[576,128]{1,0:T(8,128)S(1)}, f32[576,128]{1,0:T(8,128)S(1)}, u32[]{:S(2)}, u32[]{:S(2)}) collective-permute-start(f32[576,128]{1,0:T(8,128)S(1)} %get-tuple-element.89.refs_11_.refs_8_), channel_id=1, source_target_pairs={{0,8},{8,0},{16,24},{24,16},{1,9},{9,1},{17,25},{25,17},{2,10},{10... | collective-permute-start | bytes 884744 | tf_op jit(solution)/shard_map/ppermute | solution.py:616
  12.6 7.2 %collective-permute-start.6 = (f32[576,128]{1,0:T(8,128)S(1)}, f32[576,128]{1,0:T(8,128)S(1)}, u32[]{:S(2)}, u32[]{:S(2)}) collective-permute-start(f32[576,128]{1,0:T(8,128)S(1)} %get-tuple-element.89.refs_11_.refs_8_), channel_id=1, source_target_pairs={{0,8},{8,16},{16,24},{24,0},{1,9},{9,17},{17,25},{25,1},{2,10},{10... | collective-permute-start | bytes 884744 | tf_op jit(solution)/shard_map/ppermute | solution.py:618
  17.1 2.7 %collective-permute-start.5 = (f32[576,128]{1,0:T(8,128)S(1)}, f32[576,128]{1,0:T(8,128)S(1)}, u32[]{:S(2)}, u32[]{:S(2)}) collective-permute-start(f32[576,128]{1,0:T(8,128)S(1)} %get-tuple-element.102.refs_9_.refs_7_), channel_id=1, source_target_pairs={{0,8},{8,0},{16,24},{24,16},{1,9},{9,1},{17,25},{25,17},{2,10},{10... | collective-permute-start | bytes 884744 | tf_op jit(solution)/shard_map/ppermute | solution.py:616
  17.2 8.5 %collective-permute-start.7 = (f32[576,128]{1,0:T(8,128)S(1)}, f32[576,128]{1,0:T(8,128)S(1)}, u32[]{:S(2)}, u32[]{:S(2)}) collective-permute-start(f32[576,128]{1,0:T(8,128)S(1)} %get-tuple-element.107.refs_7_), channel_id=1, source_target_pairs={{0,8},{8,16},{16,24},{24,0},{1,9},{9,17},{17,25},{25,1},{2,10},{10... | collective-permute-start | bytes 884744 | tf_op jit(solution)/shard_map/ppermute | solution.py:624
  20.8 6.9 %collective-permute-start.8 = (f32[288,128]{1,0:T(8,128)S(1)}, f32[288,128]{1,0:T(8,128)S(1)}, u32[]{:S(2)}, u32[]{:S(2)}) collective-permute-start(f32[288,128]{1,0:T(8,128)S(1)} %get-tuple-element.146), channel_id=1, source_target_pairs={{0,2},{2,4},{4,6},{6,7},{7,5},{5,3},{3,1},{1,0},{8,10},{10,12},{12... | collective-permute-start | bytes 442376 | tf_op jit(solution)/shard_map/ppermute | solution.py:637
  23.5 6.8 %collective-permute-start.9 = (f32[288,128]{1,0:T(8,128)S(1)}, f32[288,128]{1,0:T(8,128)S(1)}, u32[]{:S(2)}, u32[]{:S(2)}) collective-permute-start(f32[288,128]{1,0:T(8,128)S(1)} %get-tuple-element.144), channel_id=1, source_target_pairs={{2,0},{4,2},{6,4},{7,6},{5,7},{3,5},{1,3},{0,1},{10,8},{12,10},{14... | collective-permute-start | bytes 442376 | tf_op jit(solution)/shard_map/ppermute | solution.py:637
  23.5 9.8 %collective-permute-start.10 = (f32[288,128]{1,0:T(8,128)S(1)}, f32[288,128]{1,0:T(8,128)S(1)}, u32[]{:S(2)}, u32[]{:S(2)}) collective-permute-start(f32[288,128]{1,0:T(8,128)S(1)} %get-tuple-element.145), channel_id=1, source_target_pairs={{2,0},{4,2},{6,4},{7,6},{5,7},{3,5},{1,3},{0,1},{10,8},{12,10},{14... | collective-permute-start | bytes 442376 | tf_op jit(solution)/shard_map/ppermute | solution.py:637
  25.5 7.9 %collective-permute-start.11 = (f32[288,128]{1,0:T(8,128)S(1)}, f32[288,128]{1,0:T(8,128)S(1)}, u32[]{:S(2)}, u32[]{:S(2)}) collective-permute-start(f32[288,128]{1,0:T(8,128)S(1)} %get-tuple-element.143), channel_id=1, source_target_pairs={{0,2},{2,4},{4,6},{6,7},{7,5},{5,3},{3,1},{1,0},{8,10},{10,12},{12... | collective-permute-start | bytes 442376 | tf_op jit(solution)/shard_map/ppermute | solution.py:637
  27.0 8.5 %collective-permute-start.12 = (f32[576,128]{1,0:T(8,128)S(1)}, f32[576,128]{1,0:T(8,128)S(1)}, u32[]{:S(2)}, u32[]{:S(2)}) collective-permute-start(f32[576,128]{1,0:T(8,128)S(1)} %get-tuple-element.113.refs_7_), channel_id=1, source_target_pairs={{0,8},{8,16},{16,24},{24,0},{1,9},{9,17},{17,25},{25,1},{2,10},{10... | collective-permute-start | bytes 884744 | tf_op jit(solution)/shard_map/ppermute | solution.py:658
  30.3 6.7 %collective-permute-start.13 = (f32[288,128]{1,0:T(8,128)S(1)}, f32[288,128]{1,0:T(8,128)S(1)}, u32[]{:S(2)}, u32[]{:S(2)}) collective-permute-start(f32[288,128]{1,0:T(8,128)S(1)} %get-tuple-element.117), channel_id=1, source_target_pairs={{0,2},{2,4},{4,6},{6,7},{7,5},{5,3},{3,1},{1,0},{8,10},{10,12},{12... | collective-permute-start | bytes 442376 | tf_op jit(solution)/shard_map/ppermute | solution.py:637
  31.9 6.7 %collective-permute-start.14 = (f32[288,128]{1,0:T(8,128)S(1)}, f32[288,128]{1,0:T(8,128)S(1)}, u32[]{:S(2)}, u32[]{:S(2)}) collective-permute-start(f32[288,128]{1,0:T(8,128)S(1)} %get-tuple-element.118), channel_id=1, source_target_pairs={{2,0},{4,2},{6,4},{7,6},{5,7},{3,5},{1,3},{0,1},{10,8},{12,10},{14... | collective-permute-start | bytes 442376 | tf_op jit(solution)/shard_map/ppermute | solution.py:637
  33.4 7.4 %collective-permute-start.15 = (f32[288,128]{1,0:T(8,128)S(1)}, f32[288,128]{1,0:T(8,128)S(1)}, u32[]{:S(2)}, u32[]{:S(2)}) collective-permute-start(f32[288,128]{1,0:T(8,128)S(1)} %get-tuple-element.120), channel_id=1, source_target_pairs={{2,0},{4,2},{6,4},{7,6},{5,7},{3,5},{1,3},{0,1},{10,8},{12,10},{14... | collective-permute-start | bytes 442376 | tf_op jit(solution)/shard_map/ppermute | solution.py:637
  33.5 7.3 %collective-permute-start.16 = (f32[288,128]{1,0:T(8,128)S(1)}, f32[288,128]{1,0:T(8,128)S(1)}, u32[]{:S(2)}, u32[]{:S(2)}) collective-permute-start(f32[288,128]{1,0:T(8,128)S(1)} %get-tuple-element.121), channel_id=1, source_target_pairs={{0,2},{2,4},{4,6},{6,7},{7,5},{5,3},{3,1},{1,0},{8,10},{10,12},{12... | collective-permute-start | bytes 442376 | tf_op jit(solution)/shard_map/ppermute | solution.py:637
  38.7 6.7 %collective-permute-start.17 = (f32[288,128]{1,0:T(8,128)S(1)}, f32[288,128]{1,0:T(8,128)S(1)}, u32[]{:S(2)}, u32[]{:S(2)}) collective-permute-start(f32[288,128]{1,0:T(8,128)S(1)} %get-tuple-element.129), channel_id=1, source_target_pairs={{0,2},{2,4},{4,6},{6,7},{7,5},{5,3},{3,1},{1,0},{8,10},{10,12},{12... | collective-permute-start | bytes 442376 | tf_op jit(solution)/shard_map/ppermute | solution.py:637
  40.3 5.1 %collective-permute-start.18 = (f32[288,128]{1,0:T(8,128)S(1)}, f32[288,128]{1,0:T(8,128)S(1)}, u32[]{:S(2)}, u32[]{:S(2)}) collective-permute-start(f32[288,128]{1,0:T(8,128)S(1)} %get-tuple-element.130), channel_id=1, source_target_pairs={{2,0},{4,2},{6,4},{7,6},{5,7},{3,5},{1,3},{0,1},{10,8},{12,10},{14... | collective-permute-start | bytes 442376 | tf_op jit(solution)/shard_map/ppermute | solution.py:637
  40.8 10.9 %collective-permute-start.21 = (f32[288,128]{1,0:T(8,128)S(1)}, f32[288,128]{1,0:T(8,128)S(1)}, u32[]{:S(2)}, u32[]{:S(2)}) collective-permute-start(f32[288,128]{1,0:T(8,128)S(1)} %get-tuple-element.139), channel_id=1, source_target_pairs={{2,0},{4,2},{6,4},{7,6},{5,7},{3,5},{1,3},{0,1},{10,8},{12,10},{14... | collective-permute-start | bytes 442376 | tf_op jit(solution)/shard_map/ppermute | solution.py:637
  42.3 9.5 %collective-permute-start.23 = (f32[288,128]{1,0:T(8,128)S(1)}, f32[288,128]{1,0:T(8,128)S(1)}, u32[]{:S(2)}, u32[]{:S(2)}) collective-permute-start(f32[288,128]{1,0:T(8,128)S(1)} %get-tuple-element.141), channel_id=1, source_target_pairs={{0,2},{2,4},{4,6},{6,7},{7,5},{5,3},{3,1},{1,0},{8,10},{10,12},{12... | collective-permute-start | bytes 442376 | tf_op jit(solution)/shard_map/ppermute | solution.py:637
  42.9 6.1 %collective-permute-start.19 = (f32[576,128]{1,0:T(8,128)S(1)}, f32[576,128]{1,0:T(8,128)S(1)}, u32[]{:S(2)}, u32[]{:S(2)}) collective-permute-start(f32[576,128]{1,0:T(8,128)S(1)} %get-tuple-element.126.refs_10_), channel_id=1, source_target_pairs={{0,8},{8,16},{16,24},{24,0},{1,9},{9,17},{17,25},{25,1},{2,10},{10... | collective-permute-start | bytes 884744 | tf_op jit(solution)/shard_map/ppermute | solution.py:658
  45.5 6.3 %collective-permute-start.20 = (f32[288,128]{1,0:T(8,128)S(1)}, f32[288,128]{1,0:T(8,128)S(1)}, u32[]{:S(2)}, u32[]{:S(2)}) collective-permute-start(f32[288,128]{1,0:T(8,128)S(1)} %get-tuple-element.138), channel_id=1, source_target_pairs={{0,2},{2,4},{4,6},{6,7},{7,5},{5,3},{3,1},{1,0},{8,10},{10,12},{12... | collective-permute-start | bytes 442376 | tf_op jit(solution)/shard_map/ppermute | solution.py:637
  47.1 5.1 %collective-permute-start.22 = (f32[288,128]{1,0:T(8,128)S(1)}, f32[288,128]{1,0:T(8,128)S(1)}, u32[]{:S(2)}, u32[]{:S(2)}) collective-permute-start(f32[288,128]{1,0:T(8,128)S(1)} %get-tuple-element.140), channel_id=1, source_target_pairs={{2,0},{4,2},{6,4},{7,6},{5,7},{3,5},{1,3},{0,1},{10,8},{12,10},{14... | collective-permute-start | bytes 442376 | tf_op jit(solution)/shard_map/ppermute | solution.py:637
  (15 other events, 59.5 us)

commit v6 on v5

--- a/solution.py
+++ b/solution.py
@@ -147,8 +147,13 @@
 
 
 def prep_kernel(d, slot, saved_ref, gain_ref, bias_ref, slope_ref, normed_ref, rstd_ref, hidden_ref, tmp):
-    t = jnp.minimum(jnp.maximum(slot - chip(), 0), saved_ref.shape[0] - 1)
-    rstd_ref[...] = prepare(d, saved_ref[t].astype(F32), gain_ref, bias_ref, slope_ref, normed_ref, hidden_ref, tmp)
+    tick = slot - chip()
+    last = saved_ref.shape[0] - 1
+
+    @pl.when(jnp.logical_and(tick >= 1, tick <= last))
+    def _():
+        x = saved_ref[jnp.minimum(jnp.maximum(tick, 1), last)].astype(F32)
+        rstd_ref[...] = prepare(d, x, gain_ref, bias_ref, slope_ref, normed_ref, hidden_ref, tmp)
 
 
 def picked(feed_ref, tick, fresh_ref):
@@ -191,65 +196,56 @@
 
 def first_kernel(d, saved_hbm, grad_hbm, gain_hbm, bias_hbm, weight_hbm, *refs):
     out_ref, hidden, saved, grad, gain, bias, weight, slope, normed, tmp, left, mid, right, cols, sems = refs
-
-    @pl.when(chip() == 0)
-    def _():
-        pairs = [(grad_hbm.at[0], grad), (saved_hbm.at[0], saved), (gain_hbm, gain), (bias_hbm, bias), (weight_hbm, weight)]
-        copies = [pltpu.make_async_copy(src, dst, sems.at[i]) for i, (src, dst) in enumerate(pairs)]
-        for copy in copies:
-            copy.start()
-        copies[0].wait()
-        spread(grad[...].astype(F32), (left, mid, right), d)
-        gather_patches((left, mid, right), cols, d)
-        for copy in copies[1:4]:
-            copy.wait()
-        rstd = prepare(d, saved[...].astype(F32), gain, bias, slope, normed, hidden, tmp)
-        copies[4].wait()
-        through_layer(d, cols, weight, slope, normed, rstd, mid, out_ref)
-
-    @pl.when(chip() != 0)
-    def _():
-        out_ref[...] = jnp.zeros_like(out_ref)
-        hidden[...] = jnp.zeros_like(hidden)
+    pairs = [(grad_hbm.at[0], grad), (saved_hbm.at[0], saved), (gain_hbm, gain), (bias_hbm, bias), (weight_hbm, weight)]
+    copies = [pltpu.make_async_copy(src, dst, sems.at[i]) for i, (src, dst) in enumerate(pairs)]
+    for copy in copies:
+        copy.start()
+    copies[0].wait()
+    spread(grad[...].astype(F32), (left, mid, right), d)
+    gather_patches((left, mid, right), cols, d)
+    for copy in copies[1:4]:
+        copy.wait()
+    rstd = prepare(d, saved[...].astype(F32), gain, bias, slope, normed, hidden, tmp)
+    copies[4].wait()
+    through_layer(d, cols, weight, slope, normed, rstd, mid, out_ref)
 
 
 def chip():
     return lax.axis_index("section") // 2
 
 
-def enter(slot, grad0_ref, feed_ref, fresh_ref, inner_ref, outer_ref, e_ref):
+def enter(slot, feed_ref, fresh_ref, inner0_ref, inner_ref, outer0_ref, outer_ref, e_ref):
     tick = slot - chip()
     second = lax.axis_index("section") % 2 == 1
-
-    @pl.when(tick == 0)
-    def _():
-        e_ref[...] = grad0_ref[0].astype(F32)
-
-    @pl.when(jnp.logical_and(tick > 0, second))
-    def _():
-        e_ref[...] = inner_ref[...]
-
-    @pl.when(jnp.logical_and(tick > 0, jnp.logical_and(jnp.logical_not(second), chip() > 0)))
-    def _():
-        e_ref[...] = outer_ref[...]
-
-    if 0 < slot <= feed_ref.shape[1]:
+    beyond = jnp.logical_and(jnp.logical_not(second), chip() > 0)
+
+    for condition, ref in (
+        (jnp.logical_and(second, tick == 1), inner0_ref),
+        (jnp.logical_and(second, tick > 1), inner_ref),
+        (jnp.logical_and(beyond, tick == 1), outer0_ref),
+        (jnp.logical_and(beyond, tick > 1), outer_ref),
+    ):
+
+        @pl.when(condition)
+        def _():
+            e_ref[...] = ref[...]
+
+    if slot <= feed_ref.shape[1]:
 
         @pl.when(lax.axis_index("section") == 0)
         def _():
             e_ref[...] = picked(feed_ref, slot, fresh_ref)
 
 
-def backward_kernel(
-    d, slot, grad0_ref, feed_ref, fresh_ref, inner_ref, outer_ref, slope_ref, normed_ref, rstd_ref, weight_ref, *refs
-):
+def backward_kernel(d, slot, feed_ref, fresh_ref, *refs):
+    arrived, (slope_ref, normed_ref, rstd_ref, weight_ref), refs = refs[:4], refs[4:8], refs[8:]
     out_ref, e_ref, left, mid, right, cols = refs
     tick = slot - chip()
-    runs = jnp.logical_and(tick >= 0, tick <= feed_ref.shape[1])
+    runs = jnp.logical_and(tick >= 1, tick <= feed_ref.shape[1])
 
     @pl.when(runs)
     def _():
-        enter(slot, grad0_ref, feed_ref, fresh_ref, inner_ref, outer_ref, e_ref)
+        enter(slot, feed_ref, fresh_ref, *arrived, e_ref)
         spread(e_ref[...], (left, mid, right), d)
         gather_patches((left, mid, right), cols, d)
         through_layer(d, cols, weight_ref, slope_ref, normed_ref, rstd_ref[...], mid, out_ref)
@@ -291,30 +287,30 @@
             )
 
 
-def weight_kernel(d, ticks, first, chips, n, positions, factor, grad0_ref, feed_ref, fresh_ref, inner_ref, outer_ref, *refs):
+def weight_kernel(d, ticks, first, chips, n, positions, factor, slots, grad0_ref, feed_ref, fresh_ref, *refs):
     me = lax.axis_index("dp")
     here = jnp.where(me % 2 == 0, me // 2, n - 1 - me // 2)
     rows = d.n * d.pix
     chunk = 9 * d.c // n
     last = feed_ref.shape[1]
-    slots = last + chips
-    span = len(ticks) + chips - 1
-    hidden_refs, refs = refs[:span], refs[span:]
-    e_refs, refs = refs[:span], refs[span:]
+    arrived, refs = refs[:4], refs[4:]
+    hidden_refs, refs = dict(zip(slots, refs)), refs[len(slots) :]
+    e_refs, refs = dict(zip(slots, refs)), refs[len(slots) :]
     before, refs = (None, refs) if first else (refs[:2], refs[2:])
-    halves, (kept, left, mid, right, cols, hid) = refs[:2], refs[2:]
+    halves, first_short, (kept, left, mid, right, cols, hid) = refs[:2], refs[2:-6], refs[-6:]
     for i, t in enumerate(ticks):
         if t == 0:
             kept[...] = grad0_ref[0].astype(F32)
-        for c in range(chips):
+            hid[i * rows : (i + 1) * rows, :] = hidden_refs[0][...]
+        for c in range(chips if t else 0):
 
             @pl.when(chip() == c)
             def _():
-                hid[i * rows : (i + 1) * rows, :] = hidden_refs[i + c][...]
-                if t + c == slots - 1:
-                    enter(slots - 1, grad0_ref, feed_ref, fresh_ref, inner_ref, outer_ref, kept)
-                elif t > 0:
-                    kept[...] = e_refs[i + c][...]
+                hid[i * rows : (i + 1) * rows, :] = hidden_refs[t + c][...]
+                if t + c == last + chips - 1:
+                    enter(t + c, feed_ref, fresh_ref, *arrived, kept)
+                else:
+                    kept[...] = e_refs[t + c][...]
 
         spread(kept[...], (left, mid, right), d)
         gather_patches((left, mid, right), cols.at[i * rows : (i + 1) * rows], d)
@@ -335,6 +331,8 @@
                     piece = piece + before[i][away, where, :]
                 halves[i][away, where, :] = piece
             at = stop
+    for i, ref in enumerate(first_short):
+        ref[...] = halves[i][(n // 2 + 1, n // 2 - 1)[i]]
 
 
 def cost(weight):
@@ -409,7 +407,7 @@
             if own:
                 name, tick, where = own
                 if where is None:
-                    waits.append(send(outs[0], name, tick, sems.at[len(stores)]))
+                    waits.append(send((outs or rest)[0], name, tick, sems.at[len(stores)]))
                 else:
 
                     @pl.when(chip() == where)
@@ -539,17 +537,15 @@
             bbias,
         )
 
-    def backward(slot, inner, outer, slope, normed, rstd, **more):
+    def backward(slot, slope, normed, rstd, **more):
         return chain.call(
             functools.partial(backward_kernel, d, slot),
             (msg, msg),
             [padded] * 3 + [cols],
             0,
-            grad0,
             feed,
             fresh_grad,
-            inner,
-            outer,
+            *arrivals(slot),
             slope,
             normed,
             rstd,
@@ -560,8 +556,8 @@
     def forward(t, arrived, **more):
         return chain.call(
             functools.partial(forward_kernel, d, t),
-            (msg,),
-            [padded] * 3 + [cols, flat],
+            (msg,) if t < last else (),
+            [flat] * (t == last) + [padded] * 3 + [cols, flat],
             0,
             feed,
             fresh_act if t else act0,
@@ -577,13 +573,15 @@
     positions = [order.index(i) for i in range(n)]
     chunk = 9 * d.c // n
     half = jax.ShapeDtypeStruct((n, chunk, LANES), F32)
-
-    def weight_terms(ticks, inner, outer, *before, passed=()):
-        span = slice(ticks[0], ticks[-1] + chips)
-        operands = hidden[span] + [e if e is not None else grad0 for e in (entered + [None])[span]]
+    piece = jax.ShapeDtypeStruct((chunk, LANES), F32)
+
+    def weight_terms(ticks, arrived, *before):
+        used = sorted({t + c if t else 0 for t in ticks for c in range(chips)})
+        operands = [hidden[k] for k in used]
+        operands += [entered[k] if 0 < k < len(entered) else grad0 for k in used]
         return chain.call(
-            functools.partial(weight_kernel, d, ticks, not before, chips, n, positions, 1.0 / (n * d.n)),
-            (half,) * 2,
+            functools.partial(weight_kernel, d, ticks, not before, chips, n, positions, 1.0 / (n * d.n), used),
+            (half,) * 2 + ((piece,) * 2 if before else ()),
             [flat]
             + [padded] * 3
             + [pltpu.VMEM((len(ticks) * rows, 9 * d.c), BF16), pltpu.VMEM((len(ticks) * rows, d.c), BF16)],
@@ -591,46 +589,40 @@
             grad0,
             feed,
             fresh_grad,
-            inner,
-            outer,
+            *arrived,
             *operands,
             *before,
-            alias={5 + len(operands) + i: i for i in range(len(before))},
-            passed=passed,
+            alias={7 + len(operands) + i: i for i in range(len(before))},
         )
 
     slots = ticks + chips - 1
     out, h = first()
-    gradients, hidden, entered, inner, outer = [out], [h], [None], [], []
-    outputs = []
+    chain.tokens = []
+    gradients, hidden, entered, inner, outer, outputs = [out], [h], [None], [], [], []
 
     def arrivals(slot):
-        return inner[slot - 1], outer[slot - 2] if slot > 1 else inner[0]
+        within = inner[0], inner[slot - 1]
+        between = (outer[0], outer[max(slot - 2, 0)]) if slot > 1 else (inner[0], inner[0])
+        return *within, *between
 
     prepared = [None]
     for slot in range(slots - 1):
         if slot > 0:
-            out, e = backward(slot, *arrivals(slot), *prepared[slot])
+            out, e = backward(slot, *prepared[slot])
             gradients.append(out)
             entered.append(e)
         inner.append(lax.ppermute(gradients[slot], "section", inside))
         if slot < slots - 2:
             outer.append(lax.ppermute(gradients[slot], "section", ring))
-            *ready, h = prep(slot + 1)
-            prepared.append(ready)
-            hidden.append(h)
-        if slot == slots - 3:
-            outputs += forward(0, inner[0])
-            arrived = lax.ppermute(outputs[0], "section", ring)
-            *ready, h = prep(slot + 2)
-            prepared.append(ready)
-            hidden.append(h)
-    terms = weight_terms(range(last), inner[0], inner[0])
-    terms = weight_terms([last], *arrivals(slots - 1), *terms)
+            for later in [slot + 1] if slot < slots - 3 else [slot + 1, slot + 2]:
+                *ready, h = prep(later)
+                prepared.append(ready)
+                hidden.append(h)
+    terms = weight_terms(range(last), (inner[0],) * 4)
+    *terms, short0, short1 = weight_terms([last], arrivals(slots - 1), *terms)
 
     onward = [(order[i], order[(i + 1) % n]) for i in range(n)]
     back = [(b, a) for a, b in onward]
-    piece = jax.ShapeDtypeStruct((chunk, LANES), F32)
     hops = n // 2
 
     def swapped(first, second, ways):
@@ -642,34 +634,37 @@
     def short_hop(pair):
         return swapped(*pair, (back, onward))
 
-    def added(pair, up, down):
+    def added(pair, up, down, weight):
         return chain.call(
-            functools.partial(add_kernel, up % n, down % n), (piece,) * 2, [], 3, *terms, *pair
+            functools.partial(add_kernel, up % n, down % n), (piece,) * 2, [], weight, *terms, *pair
         )
 
     def returned(t):
-        return ("returned", t, gradients[t : t + chips])
+        return ("returned", t, gradients[t : t + chips] if t else gradients[:1])
 
     def emitted(t):
         return ("emitted", t, outputs[t : t + 1])
 
     def forward_step(t, arrived, **more):
-        outputs.extend(forward(t, arrived, **more))
-        return lax.ppermute(outputs[t], "section", ring)
+        out, *passed = forward(t, arrived, **more)
+        outputs.append(out)
+        return lax.ppermute(out, "section", ring), passed
 
     long = long_hop([terms[0][hops], terms[1][n - hops]])
-    short = short_hop([terms[0][n - hops + 1], terms[1][hops - 1]])
-    arrived = forward_step(1, arrived, stores=[emitted(0)] + [returned(t) for t in range(last - 1)])
+    arrived, short = forward_step(0, inner[0], stores=[returned(0)], passed=[short0, short1])
+    short = short_hop(short)
     for hop in range(1, hops):
-        long = long_hop(added(long, hops - hop, hop - hops))
+        long = long_hop(added(long, hops - hop, hop - hops, 3))
+        if hop < last and hop in ():
+            arrived, _ = forward_step(hop, arrived, stores=[emitted(hop - 1), returned(hop)])
+        if hop == 1:
+            out, _ = backward(slots - 1, *prepared[slots - 1])
+            gradients.append(out)
         if hop < hops - 1:
-            short = short_hop(added(short, hop + 1 - hops, hops - 1 - hop))
-        if hop < last - 1:
-            arrived = forward_step(hop + 1, arrived, stores=[emitted(hop), returned(last - 1)] if hop == 1 else [emitted(hop)])
-        if hop == last - 1:
-            out, _ = backward(slots - 1, *arrivals(slots - 1), *prepared[slots - 1], stores=[emitted(last - 1)])
-            gradients.append(out)
-    forward(last, arrived, stores=[returned(last)], own=("emitted", last, None))
+            short = short_hop(added(short, hop + 1 - hops, hops - 1 - hop, 3))
+        if hop < last:
+            arrived, _ = forward_step(hop, arrived, stores=[emitted(hop - 1), returned(hop)])
+    forward(last, arrived, stores=[returned(last), emitted(last - 1)], own=("emitted", last, None))
     (shard_sum,) = chain.call(
         final_kernel, (jax.ShapeDtypeStruct((chunk, d.c), F32),), [], 0, *terms, *long[:1], *short[:1], *long[1:], *short[1:]
     )

time: 53.2 us -> 51.6 us (0.970)
  Pallas kernels: 22.4 us -> 20.1 us
  waiting for transfers between devices: 11 us -> 12 us
  local copies, waits for them, and re-layouts: 0.79 us -> 0.08 us
  starting transfers between devices: 17.8 us -> 18.4 us
    ppermute x14, waiting for transfers between devices: 7.25 us -> 4.49 us  [swapped(): return [lax.ppermute(v, 'dp', way) for v, way in zip((first, second), ways)]]
    pallas_call x21, Pallas kernels: 22.4 us -> 20.1 us  [call(): pl.pallas_call(chained, out_shape=(jax.ShapeDtypeStruct((8, LANES), F32),...]
    ppermute x3, waiting for transfers between devices: 1.47 us -> 3.79 us  [forward_step(): return (lax.ppermute(out, 'section', ring), passed)]
    ppermute x4, starting transfers between devices: 0.78 us -> 2.92 us  [shards(): inner.append(lax.ppermute(gradients[slot], 'section', inside))]
    ppermute x3, waiting for transfers between devices: 2.23 us -> 3.18 us  [shards(): outer.append(lax.ppermute(gradients[slot], 'section', ring))]
    unnamed x30 -> x28, local copies, waits for them, and re-layouts: 0.75 us -> 0.06 us
    ppermute x14, starting transfers between devices: 15.2 us -> 14.5 us  [swapped(): return [lax.ppermute(v, 'dp', way) for v, way in zip((first, second), ways)]]
  transfers between devices with their start and end apart: 24 -> 24, of which waited for: 9 -> 13; matrix products, arithmetic and copies ran while one was open for 0% -> 0% of each run, Pallas kernels for 34% -> 28%
where the time goes in v6:
time: 51.6 us; the launch traced here: 51.5 us
  Pallas kernels  20.1 us (39%)
  starting transfers between devices  18.4 us (36%)
  waiting for transfers between devices  12 us (23%)
  between operations  0.95 us (2%)
    pallas_call x21, Pallas kernels, call(): pl.pallas_call(chained, out_shape=(jax.ShapeDtypeStruct((8, LANES), F32),...  20.1 us
    ppermute x14, starting transfers between devices, swapped(): return [lax.ppermute(v, 'dp', way) for v, way in zip((first, second), ways)]  14.5 us
    ppermute x14, waiting for transfers between devices, swapped(): return [lax.ppermute(v, 'dp', way) for v, way in zip((first, second), ways)]  4.49 us
    ppermute x3, waiting for transfers between devices, forward_step(): return (lax.ppermute(out, 'section', ring), passed)  3.79 us
    ppermute x3, waiting for transfers between devices, shards(): outer.append(lax.ppermute(gradients[slot], 'section', ring))  3.18 us
    ppermute x4, starting transfers between devices, shards(): inner.append(lax.ppermute(gradients[slot], 'section', inside))  2.92 us
  transfers between devices with their start and end apart: 24, of which 13 were waited for; matrix products, arithmetic and copies ran while one was open for 0% of the time, Pallas kernels for 28%

profile of v6, /device:TPU:0, one launch (start us, length us, event | category | flops | bytes accessed | tf_op | source)
XLA Modules:
  0.0 51.5 jit_solution(17569337477063768310)
XLA Ops:
  0.7 3.8 %shard_map.140 = (f32[8,128]{1,0:T(8,128)}, f32[576,128]{1,0:T(8,128)}, bf16[288,256]{1,0:T(8,128)(2,1)}) custom-call(bf16[4,576,128]{2,1,0:T(8,128)(2,1)} %bitcast.62, bf16[1,576,128]{2,1,0:T(8,128)(2,1)} %bitcast.70, f32[2,128]{1,0:T(2,128)} %bitcast.86, f32[2,128]{1,0:T(2,128)} %bitcast.91, bf16[2304,256]{1,0:T(8,128)(2,1)} %bitcast.47), custom_call_target="tpu_custom_call" | custom-call | tf_op jit(solution)/shard_map/pallas_call | solution.py:426
  5.1 0.9 %shard_map.139 = (f32[8,128]{1,0:T(8,128)S(1)}, f32[288,256]{1,0:T(8,128)S(1)}, f32[288,256]{1,0:T(8,128)S(1)}, f32[8,128]{1,0:T(8,128)S(1)}, bf16[288,256]{1,0:T(8,128)(2,1)S(1)}) custom-call(bf16[4,576,128]{2,1,0:T(8,128)(2,1)S(1)} %bitcast.63, f32[2,128]{1,0:T(2,128)S(1)} %bitcast.87, f32[2,128]{1,0:T(2,128)S(1)} %bitcast.92), custom_call_target="tpu_custom_call" | custom-call | tf_op jit(solution)/shard_map/pallas_call | solution.py:426
  6.4 1.0 %shard_map.141 = (f32[8,128]{1,0:T(8,128)S(1)}, f32[576,128]{1,0:T(8,128)S(1)}, f32[576,128]{1,0:T(8,128)S(1)}) custom-call(f32[8,128]{1,0:T(8,128)S(1)} %get-tuple-element.76.refs_0_, s32[1,3]{1,0:T(1,128)S(1)} %bitcast.76, bf16[3,576,128]{2,1,0:T(8,128)(2,1)S(1)} %bitcast.56, f32[576,128]{1,0:T(8,128)S(1)} %collective-permute-done.refs_3_.refs_4_.refs_5_.refs_6_.refs_7_, ...), custom_call_target="tpu_custom_call" | custom-call | tf_op jit(solution)/shard_map/pallas_call | solution.py:426
  7.5 2.1 %collective-permute-start.1 = (f32[576,128]{1,0:T(8,128)S(1)}, f32[576,128]{1,0:T(8,128)S(1)}, u32[]{:S(2)}, u32[]{:S(2)}) collective-permute-start(f32[576,128]{1,0:T(8,128)S(1)} %get-tuple-element.83.refs_8_), channel_id=1, source_target_pairs={{0,8},{8,0},{16,24},{24,16},{1,9},{9,1},{17,25},{25,17},{2,10},{10... | collective-permute-start | bytes 884744 | tf_op jit(solution)/shard_map/ppermute | solution.py:614
  10.5 1.7 %collective-permute-done.2.refs_5_.refs_6_ = f32[576,128]{1,0:T(8,128)S(1)} collective-permute-done((f32[576,128]{1,0:T(8,128)}, f32[576,128]{1,0:T(8,128)S(1)}, u32[]{:S(2)}, u32[]{:S(2)}) %collective-permute-start.2) | collective-permute-done | bytes 294944 | tf_op jit(solution)/shard_map/ppermute | solution.py:616
  12.2 1.0 %shard_map.143 = (f32[8,128]{1,0:T(8,128)S(1)}, f32[576,128]{1,0:T(8,128)S(1)}, f32[576,128]{1,0:T(8,128)S(1)}) custom-call(f32[8,128]{1,0:T(8,128)S(1)} %get-tuple-element.82.refs_0_, s32[1,3]{1,0:T(1,128)S(1)} %bitcast.77, bf16[3,576,128]{2,1,0:T(8,128)(2,1)S(1)} %bitcast.57, f32[576,128]{1,0:T(8,128)S(1)} %collective-permute-done.refs_3_.refs_4_.refs_5_.refs_6_.refs_7_, ...), custom_call_target="tpu_custom_call" | custom-call | tf_op jit(solution)/shard_map/pallas_call | solution.py:426
  14.7 1.0 %collective-permute-done.4.refs_6_ = f32[576,128]{1,0:T(8,128)S(1)} collective-permute-done((f32[576,128]{1,0:T(8,128)S(1)}, f32[576,128]{1,0:T(8,128)S(1)}, u32[]{:S(2)}, u32[]{:S(2)}) %collective-permute-start.4) | collective-permute-done | bytes 294944 | tf_op jit(solution)/shard_map/ppermute | solution.py:616
  15.8 1.1 %shard_map.146 = (f32[8,128]{1,0:T(8,128)S(1)}, f32[576,128]{1,0:T(8,128)S(1)}, f32[576,128]{1,0:T(8,128)S(1)}) custom-call(f32[8,128]{1,0:T(8,128)S(1)} %get-tuple-element.89.refs_0_, s32[1,3]{1,0:T(1,128)S(1)} %bitcast.78, bf16[3,576,128]{2,1,0:T(8,128)(2,1)S(1)} %bitcast.58, f32[576,128]{1,0:T(8,128)S(1)} %collective-permute-done.refs_3_.refs_4_.refs_5_.refs_6_.refs_7_, ...), custom_call_target="tpu_custom_call" | custom-call | tf_op jit(solution)/shard_map/pallas_call | solution.py:426
  17.1 2.1 %shard_map.147 = (f32[8,128]{1,0:T(8,128)S(1)}, f32[8,288,128]{2,1,0:T(8,128)S(1)}, f32[8,288,128]{2,1,0:T(8,128)S(1)}) custom-call(f32[8,128]{1,0:T(8,128)S(1)} %get-tuple-element.94.refs_0_, bf16[1,576,128]{2,1,0:T(8,128)(2,1)S(1)} %bitcast.71, s32[1,3]{1,0:T(1,128)S(1)} %bitcast.79, bf16[3,576,128]{2,1,0:T(8,128)(2,1)S(1)} %bitcast.59, ...), custom_call_target="tpu_custom_call" | custom-call | tf_op jit(solution)/shard_map/pallas_call | solution.py:426
  19.6 1.0 %shard_map.148 = (f32[8,128]{1,0:T(8,128)S(1)}, f32[8,288,128]{2,1,0:T(8,128)S(1)}, f32[8,288,128]{2,1,0:T(8,128)S(1)}, f32[288,128]{1,0:T(8,128)S(1)}, f32[288,128]{1,0:T(8,128)S(1)}) custom-call(f32[8,128]{1,0:T(8,128)S(1)} %get-tuple-element.102.refs_0_, bf16[1,576,128]{2,1,0:T(8,128)(2,1)S(1)} %bitcast.73, ...), custom_call_target="tpu_custom_call", output_to_operand_aliasing={{1}: (12, {}), {2}: (13, {})} | custom-call | tf_op jit(solution)/shard_map/pallas_call | solution.py:426
  20.6 1.8 %collective-permute-start.8 = (f32[288,128]{1,0:T(8,128)S(1)}, f32[288,128]{1,0:T(8,128)S(1)}, u32[]{:S(2)}, u32[]{:S(2)}) collective-permute-start(f32[288,128]{1,0:T(8,128)S(1)} %slice_bitcast_fusion), channel_id=1, source_target_pairs={{2,0},{4,2},{6,4},{7,6},{5,7},{3,5},{1,3},{0,1},{10,8},{12,10},{14... | collective-permute-start | bytes 442376 | tf_op jit(solution)/shard_map/ppermute | solution.py:629
  22.7 1.3 %shard_map.149 = (f32[8,128]{1,0:T(8,128)S(1)}, f32[576,128]{1,0:T(8,128)S(1)}, f32[288,128]{1,0:T(8,128)S(1)}, f32[288,128]{1,0:T(8,128)S(1)}, f32[4,576,128]{2,1,0:T(8,128)}) custom-call(f32[8,128]{1,0:T(8,128)S(1)} %get-tuple-element.107.refs_0_, s32[1,3]{1,0:T(1,128)S(1)} %bitcast.81, ...), custom_call_target="tpu_custom_call", output_to_operand_aliasing={{2}: (7, {}), {3}: (8, {})} | custom-call | tf_op jit(solution)/shard_map/pallas_call | solution.py:426
  24.0 1.8 %collective-permute-start.9 = (f32[288,128]{1,0:T(8,128)S(1)}, f32[288,128]{1,0:T(8,128)S(1)}, u32[]{:S(2)}, u32[]{:S(2)}) collective-permute-start(f32[288,128]{1,0:T(8,128)S(1)} %get-tuple-element.118), channel_id=1, source_target_pairs={{2,0},{4,2},{6,4},{7,6},{5,7},{3,5},{1,3},{0,1},{10,8},{12,10},{14... | collective-permute-start | bytes 442376 | tf_op jit(solution)/shard_map/ppermute | solution.py:629
  26.7 1.3 %collective-permute-done.7.refs_3_ = f32[288,128]{1,0:T(8,128)S(1)} collective-permute-done((f32[288,128]{1,0:T(8,128)S(1)}, f32[288,128]{1,0:T(8,128)S(1)}, u32[]{:S(2)}, u32[]{:S(2)}) %collective-permute-start.7) | collective-permute-done | bytes 147488 | tf_op jit(solution)/shard_map/ppermute | solution.py:629
  28.5 1.5 %collective-permute-start.13 = (f32[288,128]{1,0:T(8,128)S(1)}, f32[288,128]{1,0:T(8,128)S(1)}, u32[]{:S(2)}, u32[]{:S(2)}) collective-permute-start(f32[288,128]{1,0:T(8,128)S(1)} %get-tuple-element.125), channel_id=1, source_target_pairs={{2,0},{4,2},{6,4},{7,6},{5,7},{3,5},{1,3},{0,1},{10,8},{12,10},{14... | collective-permute-start | bytes 442376 | tf_op jit(solution)/shard_map/ppermute | solution.py:629
  31.3 1.7 %collective-permute-start.14 = (f32[288,128]{1,0:T(8,128)S(1)}, f32[288,128]{1,0:T(8,128)S(1)}, u32[]{:S(2)}, u32[]{:S(2)}) collective-permute-start(f32[288,128]{1,0:T(8,128)S(1)} %get-tuple-element.127), channel_id=1, source_target_pairs={{2,0},{4,2},{6,4},{7,6},{5,7},{3,5},{1,3},{0,1},{10,8},{12,10},{14... | collective-permute-start | bytes 442376 | tf_op jit(solution)/shard_map/ppermute | solution.py:629
  33.4 1.3 %shard_map.153 = (f32[8,128]{1,0:T(8,128)S(1)}, f32[576,128]{1,0:T(8,128)S(1)}, f32[4,576,128]{2,1,0:T(8,128)}, f32[4,576,128]{2,1,0:T(8,128)}) custom-call(f32[8,128]{1,0:T(8,128)S(1)} %get-tuple-element.120.refs_0_, s32[1,3]{1,0:T(1,128)S(1)} %bitcast.83, bf16[3,576,128]{2,1,0:T(8,128)(2,1)S(1)} %bitcast.67, ...), custom_call_target="tpu_custom_call", output_to_operand_aliasing={{3}: (10, {})} | custom-call | tf_op jit(solution)/shard_map/pallas_call | solution.py:426
  35.3 1.7 %collective-permute-start.17 = (f32[288,128]{1,0:T(8,128)S(1)}, f32[288,128]{1,0:T(8,128)S(1)}, u32[]{:S(2)}, u32[]{:S(2)}) collective-permute-start(f32[288,128]{1,0:T(8,128)S(1)} %get-tuple-element.134), channel_id=1, source_target_pairs={{0,2},{2,4},{4,6},{6,7},{7,5},{5,3},{3,1},{1,0},{8,10},{10,12},{12... | collective-permute-start | bytes 442376 | tf_op jit(solution)/shard_map/ppermute | solution.py:629
  38.2 1.7 %collective-permute-start.21 = (f32[288,128]{1,0:T(8,128)S(1)}, f32[288,128]{1,0:T(8,128)S(1)}, u32[]{:S(2)}, u32[]{:S(2)}) collective-permute-start(f32[288,128]{1,0:T(8,128)S(1)} %get-tuple-element.145), channel_id=1, source_target_pairs={{2,0},{4,2},{6,4},{7,6},{5,7},{3,5},{1,3},{0,1},{10,8},{12,10},{14... | collective-permute-start | bytes 442376 | tf_op jit(solution)/shard_map/ppermute | solution.py:629
  41.1 1.3 %shard_map.156 = (f32[8,128]{1,0:T(8,128)S(1)}, f32[576,128]{1,0:T(8,128)S(1)}, f32[4,576,128]{2,1,0:T(8,128)}, f32[4,576,128]{2,1,0:T(8,128)}) custom-call(f32[8,128]{1,0:T(8,128)S(1)} %get-tuple-element.129.refs_0_, s32[1,3]{1,0:T(1,128)S(1)} %bitcast.84, bf16[3,576,128]{2,1,0:T(8,128)(2,1)S(1)} %bitcast.68, ...), custom_call_target="tpu_custom_call", output_to_operand_aliasing={{2}: (10, {}), {3}: (11, {})} | custom-call | tf_op jit(solution)/shard_map/pallas_call | solution.py:426
  42.5 1.1 %collective-permute-done.18.refs_4_ = f32[288,128]{1,0:T(8,128)S(1)} collective-permute-done((f32[288,128]{1,0:T(8,128)S(1)}, f32[288,128]{1,0:T(8,128)S(1)}, u32[]{:S(2)}, u32[]{:S(2)}) %collective-permute-start.18) | collective-permute-done | bytes 147488 | tf_op jit(solution)/shard_map/ppermute | solution.py:629
  43.6 1.7 %collective-permute-start.20 = (f32[288,128]{1,0:T(8,128)S(1)}, f32[288,128]{1,0:T(8,128)S(1)}, u32[]{:S(2)}, u32[]{:S(2)}) collective-permute-start(f32[288,128]{1,0:T(8,128)S(1)} %get-tuple-element.144), channel_id=1, source_target_pairs={{0,2},{2,4},{4,6},{6,7},{7,5},{5,3},{3,1},{1,0},{8,10},{10,12},{12... | collective-permute-start | bytes 442376 | tf_op jit(solution)/shard_map/ppermute | solution.py:629
  45.7 3.0 %collective-permute-done.19.refs_3_ = f32[576,128]{1,0:T(8,128)S(1)} collective-permute-done((f32[576,128]{1,0:T(8,128)S(1)}, f32[576,128]{1,0:T(8,128)S(1)}, u32[]{:S(2)}, u32[]{:S(2)}) %collective-permute-start.19) | collective-permute-done | bytes 294944 | tf_op jit(solution)/shard_map/ppermute | solution.py:651
  48.6 2.0 %shard_map.158 = (f32[8,128]{1,0:T(8,128)S(1)}, f32[4,576,128]{2,1,0:T(8,128)}, f32[4,576,128]{2,1,0:T(8,128)}) custom-call(f32[8,128]{1,0:T(8,128)S(1)} %get-tuple-element.136.refs_0_, s32[1,3]{1,0:T(1,128)S(1)} %bitcast.85, bf16[3,576,128]{2,1,0:T(8,128)(2,1)S(1)} %bitcast.69, ...), custom_call_target="tpu_custom_call", output_to_operand_aliasing={{1}: (10, {}), {2}: (11, {})} | custom-call | tf_op jit(solution)/shard_map/pallas_call | solution.py:426
  (75 shorter events, 11.9 us)
Async XLA Ops:
  4.5 1.9 %collective-permute-start = (f32[576,128]{1,0:T(8,128)}, f32[576,128]{1,0:T(8,128)S(1)}, u32[]{:S(2)}, u32[]{:S(2)}) collective-permute-start(f32[576,128]{1,0:T(8,128)} %get-tuple-element.77.refs_9_), channel_id=1, source_target_pairs={{0,8},{8,0},{16,24},{24,16},{1,9},{9,1},{17,25},{25,17},{2,10},{10... | collective-permute-start | bytes 884744 | tf_op jit(solution)/shard_map/ppermute | solution.py:614
  5.0 7.2 %collective-permute-start.2 = (f32[576,128]{1,0:T(8,128)}, f32[576,128]{1,0:T(8,128)S(1)}, u32[]{:S(2)}, u32[]{:S(2)}) collective-permute-start(f32[576,128]{1,0:T(8,128)} %get-tuple-element.77.refs_9_), channel_id=1, source_target_pairs={{0,8},{8,16},{16,24},{24,0},{1,9},{9,17},{17,25},{25,1},{2,10},{10... | collective-permute-start | bytes 884744 | tf_op jit(solution)/shard_map/ppermute | solution.py:616
  7.5 4.7 %collective-permute-start.1 = (f32[576,128]{1,0:T(8,128)S(1)}, f32[576,128]{1,0:T(8,128)S(1)}, u32[]{:S(2)}, u32[]{:S(2)}) collective-permute-start(f32[576,128]{1,0:T(8,128)S(1)} %get-tuple-element.83.refs_8_), channel_id=1, source_target_pairs={{0,8},{8,0},{16,24},{24,16},{1,9},{9,1},{17,25},{25,17},{2,10},{10... | collective-permute-start | bytes 884744 | tf_op jit(solution)/shard_map/ppermute | solution.py:614
  9.6 6.1 %collective-permute-start.4 = (f32[576,128]{1,0:T(8,128)S(1)}, f32[576,128]{1,0:T(8,128)S(1)}, u32[]{:S(2)}, u32[]{:S(2)}) collective-permute-start(f32[576,128]{1,0:T(8,128)S(1)} %get-tuple-element.83.refs_8_), channel_id=1, source_target_pairs={{0,8},{8,16},{16,24},{24,0},{1,9},{9,17},{17,25},{25,1},{2,10},{10... | collective-permute-start | bytes 884744 | tf_op jit(solution)/shard_map/ppermute | solution.py:616
  13.3 2.5 %collective-permute-start.3 = (f32[576,128]{1,0:T(8,128)S(1)}, f32[576,128]{1,0:T(8,128)S(1)}, u32[]{:S(2)}, u32[]{:S(2)}) collective-permute-start(f32[576,128]{1,0:T(8,128)S(1)} %get-tuple-element.90.refs_9_.refs_8_), channel_id=1, source_target_pairs={{0,8},{8,0},{16,24},{24,16},{1,9},{9,1},{17,25},{25,17},{2,10},{10... | collective-permute-start | bytes 884744 | tf_op jit(solution)/shard_map/ppermute | solution.py:614
  13.3 6.2 %collective-permute-start.6 = (f32[576,128]{1,0:T(8,128)S(1)}, f32[576,128]{1,0:T(8,128)S(1)}, u32[]{:S(2)}, u32[]{:S(2)}) collective-permute-start(f32[576,128]{1,0:T(8,128)S(1)} %get-tuple-element.90.refs_9_.refs_8_), channel_id=1, source_target_pairs={{0,8},{8,16},{16,24},{24,0},{1,9},{9,17},{17,25},{25,1},{2,10},{10... | collective-permute-start | bytes 884744 | tf_op jit(solution)/shard_map/ppermute | solution.py:616
  16.8 2.7 %collective-permute-start.5 = (f32[576,128]{1,0:T(8,128)S(1)}, f32[576,128]{1,0:T(8,128)S(1)}, u32[]{:S(2)}, u32[]{:S(2)}) collective-permute-start(f32[576,128]{1,0:T(8,128)S(1)} %get-tuple-element.103.refs_9_.refs_7_), channel_id=1, source_target_pairs={{0,8},{8,0},{16,24},{24,16},{1,9},{9,1},{17,25},{25,17},{2,10},{10... | collective-permute-start | bytes 884744 | tf_op jit(solution)/shard_map/ppermute | solution.py:614
  20.6 6.1 %collective-permute-start.8 = (f32[288,128]{1,0:T(8,128)S(1)}, f32[288,128]{1,0:T(8,128)S(1)}, u32[]{:S(2)}, u32[]{:S(2)}) collective-permute-start(f32[288,128]{1,0:T(8,128)S(1)} %slice_bitcast_fusion), channel_id=1, source_target_pairs={{2,0},{4,2},{6,4},{7,6},{5,7},{3,5},{1,3},{0,1},{10,8},{12,10},{14... | collective-permute-start | bytes 442376 | tf_op jit(solution)/shard_map/ppermute | solution.py:629
  22.4 5.6 %collective-permute-start.7 = (f32[288,128]{1,0:T(8,128)S(1)}, f32[288,128]{1,0:T(8,128)S(1)}, u32[]{:S(2)}, u32[]{:S(2)}) collective-permute-start(f32[288,128]{1,0:T(8,128)S(1)} %slice_bitcast_fusion.1), channel_id=1, source_target_pairs={{0,2},{2,4},{4,6},{6,7},{7,5},{5,3},{3,1},{1,0},{8,10},{10,12},{12... | collective-permute-start | bytes 442376 | tf_op jit(solution)/shard_map/ppermute | solution.py:629
  24.0 6.8 %collective-permute-start.9 = (f32[288,128]{1,0:T(8,128)S(1)}, f32[288,128]{1,0:T(8,128)S(1)}, u32[]{:S(2)}, u32[]{:S(2)}) collective-permute-start(f32[288,128]{1,0:T(8,128)S(1)} %get-tuple-element.118), channel_id=1, source_target_pairs={{2,0},{4,2},{6,4},{7,6},{5,7},{3,5},{1,3},{0,1},{10,8},{12,10},{14... | collective-permute-start | bytes 442376 | tf_op jit(solution)/shard_map/ppermute | solution.py:629
  25.8 5.5 %collective-permute-start.10 = (f32[288,128]{1,0:T(8,128)S(1)}, f32[288,128]{1,0:T(8,128)S(1)}, u32[]{:S(2)}, u32[]{:S(2)}) collective-permute-start(f32[288,128]{1,0:T(8,128)S(1)} %get-tuple-element.119), channel_id=1, source_target_pairs={{0,2},{2,4},{4,6},{6,7},{7,5},{5,3},{3,1},{1,0},{8,10},{10,12},{12... | collective-permute-start | bytes 442376 | tf_op jit(solution)/shard_map/ppermute | solution.py:629
  26.1 7.4 %collective-permute-start.11 = (f32[576,128]{1,0:T(8,128)S(1)}, f32[576,128]{1,0:T(8,128)S(1)}, u32[]{:S(2)}, u32[]{:S(2)}) collective-permute-start(f32[576,128]{1,0:T(8,128)S(1)} %get-tuple-element.121.refs_7_), channel_id=1, source_target_pairs={{0,8},{8,16},{16,24},{24,0},{1,9},{9,17},{17,25},{25,1},{2,10},{10... | collective-permute-start | bytes 884744 | tf_op jit(solution)/shard_map/ppermute | solution.py:651
  28.0 7.0 %collective-permute-start.12 = (f32[288,128]{1,0:T(8,128)S(1)}, f32[288,128]{1,0:T(8,128)S(1)}, u32[]{:S(2)}, u32[]{:S(2)}) collective-permute-start(f32[288,128]{1,0:T(8,128)S(1)} %get-tuple-element.124), channel_id=1, source_target_pairs={{0,2},{2,4},{4,6},{6,7},{7,5},{5,3},{3,1},{1,0},{8,10},{10,12},{12... | collective-permute-start | bytes 442376 | tf_op jit(solution)/shard_map/ppermute | solution.py:629
  28.5 6.7 %collective-permute-start.13 = (f32[288,128]{1,0:T(8,128)S(1)}, f32[288,128]{1,0:T(8,128)S(1)}, u32[]{:S(2)}, u32[]{:S(2)}) collective-permute-start(f32[288,128]{1,0:T(8,128)S(1)} %get-tuple-element.125), channel_id=1, source_target_pairs={{2,0},{4,2},{6,4},{7,6},{5,7},{3,5},{1,3},{0,1},{10,8},{12,10},{14... | collective-permute-start | bytes 442376 | tf_op jit(solution)/shard_map/ppermute | solution.py:629
  31.3 6.8 %collective-permute-start.14 = (f32[288,128]{1,0:T(8,128)S(1)}, f32[288,128]{1,0:T(8,128)S(1)}, u32[]{:S(2)}, u32[]{:S(2)}) collective-permute-start(f32[288,128]{1,0:T(8,128)S(1)} %get-tuple-element.127), channel_id=1, source_target_pairs={{2,0},{4,2},{6,4},{7,6},{5,7},{3,5},{1,3},{0,1},{10,8},{12,10},{14... | collective-permute-start | bytes 442376 | tf_op jit(solution)/shard_map/ppermute | solution.py:629
  33.0 5.1 %collective-permute-start.15 = (f32[288,128]{1,0:T(8,128)S(1)}, f32[288,128]{1,0:T(8,128)S(1)}, u32[]{:S(2)}, u32[]{:S(2)}) collective-permute-start(f32[288,128]{1,0:T(8,128)S(1)} %get-tuple-element.128), channel_id=1, source_target_pairs={{0,2},{2,4},{4,6},{6,7},{7,5},{5,3},{3,1},{1,0},{8,10},{10,12},{12... | collective-permute-start | bytes 442376 | tf_op jit(solution)/shard_map/ppermute | solution.py:629
  34.7 6.4 %collective-permute-start.16 = (f32[576,128]{1,0:T(8,128)S(1)}, f32[576,128]{1,0:T(8,128)S(1)}, u32[]{:S(2)}, u32[]{:S(2)}) collective-permute-start(f32[576,128]{1,0:T(8,128)S(1)} %get-tuple-element.130.refs_7_), channel_id=1, source_target_pairs={{0,8},{8,16},{16,24},{24,0},{1,9},{9,17},{17,25},{25,1},{2,10},{10... | collective-permute-start | bytes 884744 | tf_op jit(solution)/shard_map/ppermute | solution.py:651
  35.3 7.2 %collective-permute-start.17 = (f32[288,128]{1,0:T(8,128)S(1)}, f32[288,128]{1,0:T(8,128)S(1)}, u32[]{:S(2)}, u32[]{:S(2)}) collective-permute-start(f32[288,128]{1,0:T(8,128)S(1)} %get-tuple-element.134), channel_id=1, source_target_pairs={{0,2},{2,4},{4,6},{6,7},{7,5},{5,3},{3,1},{1,0},{8,10},{10,12},{12... | collective-permute-start | bytes 442376 | tf_op jit(solution)/shard_map/ppermute | solution.py:629
  36.9 6.6 %collective-permute-start.18 = (f32[288,128]{1,0:T(8,128)S(1)}, f32[288,128]{1,0:T(8,128)S(1)}, u32[]{:S(2)}, u32[]{:S(2)}) collective-permute-start(f32[288,128]{1,0:T(8,128)S(1)} %get-tuple-element.135), channel_id=1, source_target_pairs={{2,0},{4,2},{6,4},{7,6},{5,7},{3,5},{1,3},{0,1},{10,8},{12,10},{14... | collective-permute-start | bytes 442376 | tf_op jit(solution)/shard_map/ppermute | solution.py:629
  38.2 12.4 %collective-permute-start.21 = (f32[288,128]{1,0:T(8,128)S(1)}, f32[288,128]{1,0:T(8,128)S(1)}, u32[]{:S(2)}, u32[]{:S(2)}) collective-permute-start(f32[288,128]{1,0:T(8,128)S(1)} %get-tuple-element.145), channel_id=1, source_target_pairs={{2,0},{4,2},{6,4},{7,6},{5,7},{3,5},{1,3},{0,1},{10,8},{12,10},{14... | collective-permute-start | bytes 442376 | tf_op jit(solution)/shard_map/ppermute | solution.py:629
  39.9 10.8 %collective-permute-start.23 = (f32[288,128]{1,0:T(8,128)S(1)}, f32[288,128]{1,0:T(8,128)S(1)}, u32[]{:S(2)}, u32[]{:S(2)}) collective-permute-start(f32[288,128]{1,0:T(8,128)S(1)} %get-tuple-element.147), channel_id=1, source_target_pairs={{0,2},{2,4},{4,6},{6,7},{7,5},{5,3},{3,1},{1,0},{8,10},{10,12},{12... | collective-permute-start | bytes 442376 | tf_op jit(solution)/shard_map/ppermute | solution.py:629
  42.4 6.2 %collective-permute-start.19 = (f32[576,128]{1,0:T(8,128)S(1)}, f32[576,128]{1,0:T(8,128)S(1)}, u32[]{:S(2)}, u32[]{:S(2)}) collective-permute-start(f32[576,128]{1,0:T(8,128)S(1)} %get-tuple-element.137.refs_9_), channel_id=1, source_target_pairs={{0,8},{8,16},{16,24},{24,0},{1,9},{9,17},{17,25},{25,1},{2,10},{10... | collective-permute-start | bytes 884744 | tf_op jit(solution)/shard_map/ppermute | solution.py:651
  43.6 7.1 %collective-permute-start.20 = (f32[288,128]{1,0:T(8,128)S(1)}, f32[288,128]{1,0:T(8,128)S(1)}, u32[]{:S(2)}, u32[]{:S(2)}) collective-permute-start(f32[288,128]{1,0:T(8,128)S(1)} %get-tuple-element.144), channel_id=1, source_target_pairs={{0,2},{2,4},{4,6},{6,7},{7,5},{5,3},{3,1},{1,0},{8,10},{10,12},{12... | collective-permute-start | bytes 442376 | tf_op jit(solution)/shard_map/ppermute | solution.py:629
  45.3 5.4 %collective-permute-start.22 = (f32[288,128]{1,0:T(8,128)S(1)}, f32[288,128]{1,0:T(8,128)S(1)}, u32[]{:S(2)}, u32[]{:S(2)}) collective-permute-start(f32[288,128]{1,0:T(8,128)S(1)} %get-tuple-element.146), channel_id=1, source_target_pairs={{2,0},{4,2},{6,4},{7,6},{5,7},{3,5},{1,3},{0,1},{10,8},{12,10},{14... | collective-permute-start | bytes 442376 | tf_op jit(solution)/shard_map/ppermute | solution.py:629
  (14 other events, 51.0 us)

commit v7 on v6

--- a/solution.py
+++ b/solution.py
@@ -581,7 +581,7 @@
         operands += [entered[k] if 0 < k < len(entered) else grad0 for k in used]
         return chain.call(
             functools.partial(weight_kernel, d, ticks, not before, chips, n, positions, 1.0 / (n * d.n), used),
-            (half,) * 2 + ((piece,) * 2 if before else ()),
+            (half,) * 2 + ((piece,) * 2 if last in ticks else ()),
             [flat]
             + [padded] * 3
             + [pltpu.VMEM((len(ticks) * rows, 9 * d.c), BF16), pltpu.VMEM((len(ticks) * rows, d.c), BF16)],
@@ -618,7 +618,9 @@
                 *ready, h = prep(later)
                 prepared.append(ready)
                 hidden.append(h)
-    terms = weight_terms(range(last), (inner[0],) * 4)
+        if slot == slots - 4:
+            terms = weight_terms([0], (inner[0],) * 4)
+    terms = weight_terms(range(1, last), (inner[0],) * 4, *terms)
     *terms, short0, short1 = weight_terms([last], arrivals(slots - 1), *terms)
 
     onward = [(order[i], order[(i + 1) % n]) for i in range(n)]
@@ -655,8 +657,6 @@
     short = short_hop(short)
     for hop in range(1, hops):
         long = long_hop(added(long, hops - hop, hop - hops, 3))
-        if hop < last and hop in ():
-            arrived, _ = forward_step(hop, arrived, stores=[emitted(hop - 1), returned(hop)])
         if hop == 1:
             out, _ = backward(slots - 1, *prepared[slots - 1])
             gradients.append(out)

time: 51.6 us -> 51.7 us (level)
    ppermute x14, waiting for transfers between devices: 4.49 us -> 5.08 us  [swapped(): return [lax.ppermute(v, 'dp', way) for v, way in zip((first, second), ways)]]
    pallas_call x21 -> x22, Pallas kernels: 20.1 us -> 20.5 us  [call(): pl.pallas_call(chained, out_shape=(jax.ShapeDtypeStruct((8, LANES), F32),...]
  transfers between devices with their start and end apart: 24 -> 24, of which waited for: 13 -> 14; matrix products, arithmetic and copies ran while one was open for 0% -> 0% of each run, Pallas kernels for 28% -> 29%
where the time goes in v7:
time: 51.7 us; the launch traced here: 51.5 us
  Pallas kernels  20.5 us (40%)
  starting transfers between devices  18.2 us (35%)
  waiting for transfers between devices  11.8 us (23%)
  between operations  0.98 us (2%)
    pallas_call x22, Pallas kernels, call(): pl.pallas_call(chained, out_shape=(jax.ShapeDtypeStruct((8, LANES), F32),...  20.5 us
    ppermute x14, starting transfers between devices, swapped(): return [lax.ppermute(v, 'dp', way) for v, way in zip((first, second), ways)]  14.5 us
    ppermute x14, waiting for transfers between devices, swapped(): return [lax.ppermute(v, 'dp', way) for v, way in zip((first, second), ways)]  5.08 us
    ppermute x3, waiting for transfers between devices, forward_step(): return (lax.ppermute(out, 'section', ring), passed)  3.32 us
    ppermute x3, waiting for transfers between devices, shards(): outer.append(lax.ppermute(gradients[slot], 'section', ring))  2.89 us
    ppermute x4, starting transfers between devices, shards(): inner.append(lax.ppermute(gradients[slot], 'section', inside))  2.89 us
  transfers between devices with their start and end apart: 24, of which 14 were waited for; matrix products, arithmetic and copies ran while one was open for 0% of the time, Pallas kernels for 29%

profile of v7, /device:TPU:0, one launch (start us, length us, event | category | flops | bytes accessed | tf_op | source)
XLA Modules:
  0.0 51.5 jit_solution(5197328031803847160)
XLA Ops:
  0.7 3.8 %shard_map.140 = (f32[8,128]{1,0:T(8,128)}, f32[576,128]{1,0:T(8,128)}, bf16[288,256]{1,0:T(8,128)(2,1)}) custom-call(bf16[4,576,128]{2,1,0:T(8,128)(2,1)} %bitcast.63, bf16[1,576,128]{2,1,0:T(8,128)(2,1)} %bitcast.68, f32[2,128]{1,0:T(2,128)} %bitcast.89, f32[2,128]{1,0:T(2,128)} %bitcast.94, bf16[2304,256]{1,0:T(8,128)(2,1)} %bitcast.47), custom_call_target="tpu_custom_call" | custom-call | tf_op jit(solution)/shard_map/pallas_call | solution.py:426
  6.5 1.1 %shard_map.141 = (f32[8,128]{1,0:T(8,128)S(1)}, f32[576,128]{1,0:T(8,128)S(1)}, f32[576,128]{1,0:T(8,128)S(1)}) custom-call(f32[8,128]{1,0:T(8,128)S(1)} %get-tuple-element.79.refs_0_, s32[1,3]{1,0:T(1,128)S(1)} %bitcast.78, bf16[3,576,128]{2,1,0:T(8,128)(2,1)S(1)} %bitcast.52, f32[576,128]{1,0:T(8,128)S(1)} %collective-permute-done.refs_3_.refs_4_.refs_5_.refs_6_.refs_7_, ...), custom_call_target="tpu_custom_call" | custom-call | tf_op jit(solution)/shard_map/pallas_call | solution.py:426
  7.5 2.1 %collective-permute-start.1 = (f32[576,128]{1,0:T(8,128)S(1)}, f32[576,128]{1,0:T(8,128)S(1)}, u32[]{:S(2)}, u32[]{:S(2)}) collective-permute-start(f32[576,128]{1,0:T(8,128)S(1)} %get-tuple-element.88.refs_8_), channel_id=1, source_target_pairs={{0,8},{8,0},{16,24},{24,16},{1,9},{9,1},{17,25},{25,17},{2,10},{10... | collective-permute-start | bytes 884744 | tf_op jit(solution)/shard_map/ppermute | solution.py:614
  10.6 0.9 %shard_map.143 = (f32[8,128]{1,0:T(8,128)S(1)}, f32[8,288,128]{2,1,0:T(8,128)S(1)}, f32[8,288,128]{2,1,0:T(8,128)S(1)}) custom-call(f32[8,128]{1,0:T(8,128)S(1)} %get-tuple-element.85.refs_0_, bf16[1,576,128]{2,1,0:T(8,128)(2,1)S(1)} %bitcast.69, s32[1,3]{1,0:T(1,128)S(1)} %bitcast.79, bf16[3,576,128]{2,1,0:T(8,128)(2,1)S(1)} %bitcast.53, ...), custom_call_target="tpu_custom_call" | custom-call | tf_op jit(solution)/shard_map/pallas_call | solution.py:426
  12.2 1.0 %shard_map.144 = (f32[8,128]{1,0:T(8,128)S(1)}, f32[576,128]{1,0:T(8,128)S(1)}, f32[576,128]{1,0:T(8,128)S(1)}) custom-call(f32[8,128]{1,0:T(8,128)S(1)} %get-tuple-element.87.refs_0_, s32[1,3]{1,0:T(1,128)S(1)} %bitcast.80, bf16[3,576,128]{2,1,0:T(8,128)(2,1)S(1)} %bitcast.54, f32[576,128]{1,0:T(8,128)S(1)} %collective-permute-done.refs_3_.refs_4_.refs_5_.refs_6_.refs_7_, ...), custom_call_target="tpu_custom_call" | custom-call | tf_op jit(solution)/shard_map/pallas_call | solution.py:426
  14.7 1.1 %collective-permute-done.4.refs_6_ = f32[576,128]{1,0:T(8,128)S(1)} collective-permute-done((f32[576,128]{1,0:T(8,128)S(1)}, f32[576,128]{1,0:T(8,128)S(1)}, u32[]{:S(2)}, u32[]{:S(2)}) %collective-permute-start.4) | collective-permute-done | bytes 294944 | tf_op jit(solution)/shard_map/ppermute | solution.py:616
  15.8 1.0 %shard_map.147 = (f32[8,128]{1,0:T(8,128)S(1)}, f32[576,128]{1,0:T(8,128)S(1)}, f32[576,128]{1,0:T(8,128)S(1)}) custom-call(f32[8,128]{1,0:T(8,128)S(1)} %get-tuple-element.94.refs_0_, s32[1,3]{1,0:T(1,128)S(1)} %bitcast.81, bf16[3,576,128]{2,1,0:T(8,128)(2,1)S(1)} %bitcast.55, f32[576,128]{1,0:T(8,128)S(1)} %collective-permute-done.refs_3_.refs_4_.refs_5_.refs_6_.refs_7_, ...), custom_call_target="tpu_custom_call" | custom-call | tf_op jit(solution)/shard_map/pallas_call | solution.py:426
  17.0 1.5 %shard_map.148 = (f32[8,128]{1,0:T(8,128)S(1)}, f32[8,288,128]{2,1,0:T(8,128)S(1)}, f32[8,288,128]{2,1,0:T(8,128)S(1)}) custom-call(f32[8,128]{1,0:T(8,128)S(1)} %get-tuple-element.99.refs_0_, bf16[1,576,128]{2,1,0:T(8,128)(2,1)S(1)} %bitcast.71, s32[1,3]{1,0:T(1,128)S(1)} %bitcast.82, ...), custom_call_target="tpu_custom_call", output_to_operand_aliasing={{1}: (14, {}), {2}: (15, {})} | custom-call | tf_op jit(solution)/shard_map/pallas_call | solution.py:426
  18.5 1.0 %collective-permute-done.6.refs_7_.refs_6_ = f32[576,128]{1,0:T(8,128)S(1)} collective-permute-done((f32[576,128]{1,0:T(8,128)S(1)}, f32[576,128]{1,0:T(8,128)S(1)}, u32[]{:S(2)}, u32[]{:S(2)}) %collective-permute-start.6) | collective-permute-done | bytes 294944 | tf_op jit(solution)/shard_map/ppermute | solution.py:616
  19.6 1.0 %shard_map.149 = (f32[8,128]{1,0:T(8,128)S(1)}, f32[8,288,128]{2,1,0:T(8,128)S(1)}, f32[8,288,128]{2,1,0:T(8,128)S(1)}, f32[288,128]{1,0:T(8,128)S(1)}, f32[288,128]{1,0:T(8,128)S(1)}) custom-call(f32[8,128]{1,0:T(8,128)S(1)} %get-tuple-element.108.refs_0_, bf16[1,576,128]{2,1,0:T(8,128)(2,1)S(1)} %bitcast.72, ...), custom_call_target="tpu_custom_call", output_to_operand_aliasing={{1}: (12, {}), {2}: (13, {})} | custom-call | tf_op jit(solution)/shard_map/pallas_call | solution.py:426
  20.6 1.8 %collective-permute-start.8 = (f32[288,128]{1,0:T(8,128)S(1)}, f32[288,128]{1,0:T(8,128)S(1)}, u32[]{:S(2)}, u32[]{:S(2)}) collective-permute-start(f32[288,128]{1,0:T(8,128)S(1)} %slice_bitcast_fusion), channel_id=1, source_target_pairs={{2,0},{4,2},{6,4},{7,6},{5,7},{3,5},{1,3},{0,1},{10,8},{12,10},{14... | collective-permute-start | bytes 442376 | tf_op jit(solution)/shard_map/ppermute | solution.py:631
  22.7 1.3 %shard_map.150 = (f32[8,128]{1,0:T(8,128)S(1)}, f32[576,128]{1,0:T(8,128)S(1)}, f32[288,128]{1,0:T(8,128)S(1)}, f32[288,128]{1,0:T(8,128)S(1)}, f32[4,576,128]{2,1,0:T(8,128)}) custom-call(f32[8,128]{1,0:T(8,128)S(1)} %get-tuple-element.113.refs_0_, s32[1,3]{1,0:T(1,128)S(1)} %bitcast.84, ...), custom_call_target="tpu_custom_call", output_to_operand_aliasing={{2}: (7, {}), {3}: (8, {})} | custom-call | tf_op jit(solution)/shard_map/pallas_call | solution.py:426
  24.0 1.8 %collective-permute-start.9 = (f32[288,128]{1,0:T(8,128)S(1)}, f32[288,128]{1,0:T(8,128)S(1)}, u32[]{:S(2)}, u32[]{:S(2)}) collective-permute-start(f32[288,128]{1,0:T(8,128)S(1)} %get-tuple-element.124), channel_id=1, source_target_pairs={{2,0},{4,2},{6,4},{7,6},{5,7},{3,5},{1,3},{0,1},{10,8},{12,10},{14... | collective-permute-start | bytes 442376 | tf_op jit(solution)/shard_map/ppermute | solution.py:631
  26.1 2.2 %collective-permute-done.7.refs_3_ = f32[288,128]{1,0:T(8,128)S(1)} collective-permute-done((f32[288,128]{1,0:T(8,128)S(1)}, f32[288,128]{1,0:T(8,128)S(1)}, u32[]{:S(2)}, u32[]{:S(2)}) %collective-permute-start.7) | collective-permute-done | bytes 147488 | tf_op jit(solution)/shard_map/ppermute | solution.py:631
  28.5 1.9 %collective-permute-start.13 = (f32[288,128]{1,0:T(8,128)S(1)}, f32[288,128]{1,0:T(8,128)S(1)}, u32[]{:S(2)}, u32[]{:S(2)}) collective-permute-start(f32[288,128]{1,0:T(8,128)S(1)} %get-tuple-element.131), channel_id=1, source_target_pairs={{2,0},{4,2},{6,4},{7,6},{5,7},{3,5},{1,3},{0,1},{10,8},{12,10},{14... | collective-permute-start | bytes 442376 | tf_op jit(solution)/shard_map/ppermute | solution.py:631
  31.3 1.7 %collective-permute-start.14 = (f32[288,128]{1,0:T(8,128)S(1)}, f32[288,128]{1,0:T(8,128)S(1)}, u32[]{:S(2)}, u32[]{:S(2)}) collective-permute-start(f32[288,128]{1,0:T(8,128)S(1)} %get-tuple-element.133), channel_id=1, source_target_pairs={{2,0},{4,2},{6,4},{7,6},{5,7},{3,5},{1,3},{0,1},{10,8},{12,10},{14... | collective-permute-start | bytes 442376 | tf_op jit(solution)/shard_map/ppermute | solution.py:631
  33.4 1.5 %shard_map.154 = (f32[8,128]{1,0:T(8,128)S(1)}, f32[576,128]{1,0:T(8,128)S(1)}, f32[4,576,128]{2,1,0:T(8,128)}, f32[4,576,128]{2,1,0:T(8,128)}) custom-call(f32[8,128]{1,0:T(8,128)S(1)} %get-tuple-element.126.refs_0_, s32[1,3]{1,0:T(1,128)S(1)} %bitcast.86, bf16[3,576,128]{2,1,0:T(8,128)(2,1)S(1)} %bitcast.74, ...), custom_call_target="tpu_custom_call", output_to_operand_aliasing={{3}: (10, {})} | custom-call | tf_op jit(solution)/shard_map/pallas_call | solution.py:426
  35.3 2.0 %collective-permute-start.17 = (f32[288,128]{1,0:T(8,128)S(1)}, f32[288,128]{1,0:T(8,128)S(1)}, u32[]{:S(2)}, u32[]{:S(2)}) collective-permute-start(f32[288,128]{1,0:T(8,128)S(1)} %get-tuple-element.140), channel_id=1, source_target_pairs={{0,2},{2,4},{4,6},{6,7},{7,5},{5,3},{3,1},{1,0},{8,10},{10,12},{12... | collective-permute-start | bytes 442376 | tf_op jit(solution)/shard_map/ppermute | solution.py:631
  38.2 1.6 %collective-permute-start.21 = (f32[288,128]{1,0:T(8,128)S(1)}, f32[288,128]{1,0:T(8,128)S(1)}, u32[]{:S(2)}, u32[]{:S(2)}) collective-permute-start(f32[288,128]{1,0:T(8,128)S(1)} %get-tuple-element.151), channel_id=1, source_target_pairs={{2,0},{4,2},{6,4},{7,6},{5,7},{3,5},{1,3},{0,1},{10,8},{12,10},{14... | collective-permute-start | bytes 442376 | tf_op jit(solution)/shard_map/ppermute | solution.py:631
  41.1 1.3 %shard_map.157 = (f32[8,128]{1,0:T(8,128)S(1)}, f32[576,128]{1,0:T(8,128)S(1)}, f32[4,576,128]{2,1,0:T(8,128)}, f32[4,576,128]{2,1,0:T(8,128)}) custom-call(f32[8,128]{1,0:T(8,128)S(1)} %get-tuple-element.135.refs_0_, s32[1,3]{1,0:T(1,128)S(1)} %bitcast.87, bf16[3,576,128]{2,1,0:T(8,128)(2,1)S(1)} %bitcast.75, ...), custom_call_target="tpu_custom_call", output_to_operand_aliasing={{2}: (10, {}), {3}: (11, {})} | custom-call | tf_op jit(solution)/shard_map/pallas_call | solution.py:426
  42.5 1.5 %collective-permute-done.18.refs_4_ = f32[288,128]{1,0:T(8,128)S(1)} collective-permute-done((f32[288,128]{1,0:T(8,128)S(1)}, f32[288,128]{1,0:T(8,128)S(1)}, u32[]{:S(2)}, u32[]{:S(2)}) %collective-permute-start.18) | collective-permute-done | bytes 147488 | tf_op jit(solution)/shard_map/ppermute | solution.py:631
  44.0 1.6 %collective-permute-start.20 = (f32[288,128]{1,0:T(8,128)S(1)}, f32[288,128]{1,0:T(8,128)S(1)}, u32[]{:S(2)}, u32[]{:S(2)}) collective-permute-start(f32[288,128]{1,0:T(8,128)S(1)} %get-tuple-element.150), channel_id=1, source_target_pairs={{0,2},{2,4},{4,6},{6,7},{7,5},{5,3},{3,1},{1,0},{8,10},{10,12},{12... | collective-permute-start | bytes 442376 | tf_op jit(solution)/shard_map/ppermute | solution.py:631
  46.1 2.5 %collective-permute-done.19.refs_3_ = f32[576,128]{1,0:T(8,128)S(1)} collective-permute-done((f32[576,128]{1,0:T(8,128)S(1)}, f32[576,128]{1,0:T(8,128)S(1)}, u32[]{:S(2)}, u32[]{:S(2)}) %collective-permute-start.19) | collective-permute-done | bytes 294944 | tf_op jit(solution)/shard_map/ppermute | solution.py:653
  48.6 2.0 %shard_map.159 = (f32[8,128]{1,0:T(8,128)S(1)}, f32[4,576,128]{2,1,0:T(8,128)}, f32[4,576,128]{2,1,0:T(8,128)}) custom-call(f32[8,128]{1,0:T(8,128)S(1)} %get-tuple-element.142.refs_0_, s32[1,3]{1,0:T(1,128)S(1)} %bitcast.88, bf16[3,576,128]{2,1,0:T(8,128)(2,1)S(1)} %bitcast.76, ...), custom_call_target="tpu_custom_call", output_to_operand_aliasing={{1}: (10, {}), {2}: (11, {})} | custom-call | tf_op jit(solution)/shard_map/pallas_call | solution.py:426
  (76 shorter events, 11.3 us)
Async XLA Ops:
  4.5 1.9 %collective-permute-start = (f32[576,128]{1,0:T(8,128)}, f32[576,128]{1,0:T(8,128)S(1)}, u32[]{:S(2)}, u32[]{:S(2)}) collective-permute-start(f32[576,128]{1,0:T(8,128)} %get-tuple-element.80.refs_9_), channel_id=1, source_target_pairs={{0,8},{8,0},{16,24},{24,16},{1,9},{9,1},{17,25},{25,17},{2,10},{10... | collective-permute-start | bytes 884744 | tf_op jit(solution)/shard_map/ppermute | solution.py:614
  5.0 7.2 %collective-permute-start.2 = (f32[576,128]{1,0:T(8,128)}, f32[576,128]{1,0:T(8,128)S(1)}, u32[]{:S(2)}, u32[]{:S(2)}) collective-permute-start(f32[576,128]{1,0:T(8,128)} %get-tuple-element.80.refs_9_), channel_id=1, source_target_pairs={{0,8},{8,16},{16,24},{24,0},{1,9},{9,17},{17,25},{25,1},{2,10},{10... | collective-permute-start | bytes 884744 | tf_op jit(solution)/shard_map/ppermute | solution.py:616
  7.5 4.7 %collective-permute-start.1 = (f32[576,128]{1,0:T(8,128)S(1)}, f32[576,128]{1,0:T(8,128)S(1)}, u32[]{:S(2)}, u32[]{:S(2)}) collective-permute-start(f32[576,128]{1,0:T(8,128)S(1)} %get-tuple-element.88.refs_8_), channel_id=1, source_target_pairs={{0,8},{8,0},{16,24},{24,16},{1,9},{9,1},{17,25},{25,17},{2,10},{10... | collective-permute-start | bytes 884744 | tf_op jit(solution)/shard_map/ppermute | solution.py:614
  9.6 6.1 %collective-permute-start.4 = (f32[576,128]{1,0:T(8,128)S(1)}, f32[576,128]{1,0:T(8,128)S(1)}, u32[]{:S(2)}, u32[]{:S(2)}) collective-permute-start(f32[576,128]{1,0:T(8,128)S(1)} %get-tuple-element.88.refs_8_), channel_id=1, source_target_pairs={{0,8},{8,16},{16,24},{24,0},{1,9},{9,17},{17,25},{25,1},{2,10},{10... | collective-permute-start | bytes 884744 | tf_op jit(solution)/shard_map/ppermute | solution.py:616
  13.2 2.5 %collective-permute-start.3 = (f32[576,128]{1,0:T(8,128)S(1)}, f32[576,128]{1,0:T(8,128)S(1)}, u32[]{:S(2)}, u32[]{:S(2)}) collective-permute-start(f32[576,128]{1,0:T(8,128)S(1)} %get-tuple-element.95.refs_9_.refs_8_), channel_id=1, source_target_pairs={{0,8},{8,0},{16,24},{24,16},{1,9},{9,1},{17,25},{25,17},{2,10},{10... | collective-permute-start | bytes 884744 | tf_op jit(solution)/shard_map/ppermute | solution.py:614
  13.3 6.2 %collective-permute-start.6 = (f32[576,128]{1,0:T(8,128)S(1)}, f32[576,128]{1,0:T(8,128)S(1)}, u32[]{:S(2)}, u32[]{:S(2)}) collective-permute-start(f32[576,128]{1,0:T(8,128)S(1)} %get-tuple-element.95.refs_9_.refs_8_), channel_id=1, source_target_pairs={{0,8},{8,16},{16,24},{24,0},{1,9},{9,17},{17,25},{25,1},{2,10},{10... | collective-permute-start | bytes 884744 | tf_op jit(solution)/shard_map/ppermute | solution.py:616
  16.8 2.7 %collective-permute-start.5 = (f32[576,128]{1,0:T(8,128)S(1)}, f32[576,128]{1,0:T(8,128)S(1)}, u32[]{:S(2)}, u32[]{:S(2)}) collective-permute-start(f32[576,128]{1,0:T(8,128)S(1)} %get-tuple-element.109.refs_9_.refs_7_), channel_id=1, source_target_pairs={{0,8},{8,0},{16,24},{24,16},{1,9},{9,1},{17,25},{25,17},{2,10},{10... | collective-permute-start | bytes 884744 | tf_op jit(solution)/shard_map/ppermute | solution.py:614
  20.6 5.5 %collective-permute-start.8 = (f32[288,128]{1,0:T(8,128)S(1)}, f32[288,128]{1,0:T(8,128)S(1)}, u32[]{:S(2)}, u32[]{:S(2)}) collective-permute-start(f32[288,128]{1,0:T(8,128)S(1)} %slice_bitcast_fusion), channel_id=1, source_target_pairs={{2,0},{4,2},{6,4},{7,6},{5,7},{3,5},{1,3},{0,1},{10,8},{12,10},{14... | collective-permute-start | bytes 442376 | tf_op jit(solution)/shard_map/ppermute | solution.py:631
  22.4 6.0 %collective-permute-start.7 = (f32[288,128]{1,0:T(8,128)S(1)}, f32[288,128]{1,0:T(8,128)S(1)}, u32[]{:S(2)}, u32[]{:S(2)}) collective-permute-start(f32[288,128]{1,0:T(8,128)S(1)} %slice_bitcast_fusion.1), channel_id=1, source_target_pairs={{0,2},{2,4},{4,6},{6,7},{7,5},{5,3},{3,1},{1,0},{8,10},{10,12},{12... | collective-permute-start | bytes 442376 | tf_op jit(solution)/shard_map/ppermute | solution.py:631
  24.0 7.2 %collective-permute-start.9 = (f32[288,128]{1,0:T(8,128)S(1)}, f32[288,128]{1,0:T(8,128)S(1)}, u32[]{:S(2)}, u32[]{:S(2)}) collective-permute-start(f32[288,128]{1,0:T(8,128)S(1)} %get-tuple-element.124), channel_id=1, source_target_pairs={{2,0},{4,2},{6,4},{7,6},{5,7},{3,5},{1,3},{0,1},{10,8},{12,10},{14... | collective-permute-start | bytes 442376 | tf_op jit(solution)/shard_map/ppermute | solution.py:631
  25.7 5.5 %collective-permute-start.10 = (f32[288,128]{1,0:T(8,128)S(1)}, f32[288,128]{1,0:T(8,128)S(1)}, u32[]{:S(2)}, u32[]{:S(2)}) collective-permute-start(f32[288,128]{1,0:T(8,128)S(1)} %get-tuple-element.125), channel_id=1, source_target_pairs={{0,2},{2,4},{4,6},{6,7},{7,5},{5,3},{3,1},{1,0},{8,10},{10,12},{12... | collective-permute-start | bytes 442376 | tf_op jit(solution)/shard_map/ppermute | solution.py:631
  26.1 7.4 %collective-permute-start.11 = (f32[576,128]{1,0:T(8,128)S(1)}, f32[576,128]{1,0:T(8,128)S(1)}, u32[]{:S(2)}, u32[]{:S(2)}) collective-permute-start(f32[576,128]{1,0:T(8,128)S(1)} %get-tuple-element.127.refs_7_), channel_id=1, source_target_pairs={{0,8},{8,16},{16,24},{24,0},{1,9},{9,17},{17,25},{25,1},{2,10},{10... | collective-permute-start | bytes 884744 | tf_op jit(solution)/shard_map/ppermute | solution.py:653
  28.4 6.6 %collective-permute-start.12 = (f32[288,128]{1,0:T(8,128)S(1)}, f32[288,128]{1,0:T(8,128)S(1)}, u32[]{:S(2)}, u32[]{:S(2)}) collective-permute-start(f32[288,128]{1,0:T(8,128)S(1)} %get-tuple-element.130), channel_id=1, source_target_pairs={{0,2},{2,4},{4,6},{6,7},{7,5},{5,3},{3,1},{1,0},{8,10},{10,12},{12... | collective-permute-start | bytes 442376 | tf_op jit(solution)/shard_map/ppermute | solution.py:631
  28.5 6.7 %collective-permute-start.13 = (f32[288,128]{1,0:T(8,128)S(1)}, f32[288,128]{1,0:T(8,128)S(1)}, u32[]{:S(2)}, u32[]{:S(2)}) collective-permute-start(f32[288,128]{1,0:T(8,128)S(1)} %get-tuple-element.131), channel_id=1, source_target_pairs={{2,0},{4,2},{6,4},{7,6},{5,7},{3,5},{1,3},{0,1},{10,8},{12,10},{14... | collective-permute-start | bytes 442376 | tf_op jit(solution)/shard_map/ppermute | solution.py:631
  31.3 6.7 %collective-permute-start.14 = (f32[288,128]{1,0:T(8,128)S(1)}, f32[288,128]{1,0:T(8,128)S(1)}, u32[]{:S(2)}, u32[]{:S(2)}) collective-permute-start(f32[288,128]{1,0:T(8,128)S(1)} %get-tuple-element.133), channel_id=1, source_target_pairs={{2,0},{4,2},{6,4},{7,6},{5,7},{3,5},{1,3},{0,1},{10,8},{12,10},{14... | collective-permute-start | bytes 442376 | tf_op jit(solution)/shard_map/ppermute | solution.py:631
  33.0 5.1 %collective-permute-start.15 = (f32[288,128]{1,0:T(8,128)S(1)}, f32[288,128]{1,0:T(8,128)S(1)}, u32[]{:S(2)}, u32[]{:S(2)}) collective-permute-start(f32[288,128]{1,0:T(8,128)S(1)} %get-tuple-element.134), channel_id=1, source_target_pairs={{0,2},{2,4},{4,6},{6,7},{7,5},{5,3},{3,1},{1,0},{8,10},{10,12},{12... | collective-permute-start | bytes 442376 | tf_op jit(solution)/shard_map/ppermute | solution.py:631
  34.9 6.2 %collective-permute-start.16 = (f32[576,128]{1,0:T(8,128)S(1)}, f32[576,128]{1,0:T(8,128)S(1)}, u32[]{:S(2)}, u32[]{:S(2)}) collective-permute-start(f32[576,128]{1,0:T(8,128)S(1)} %get-tuple-element.136.refs_7_), channel_id=1, source_target_pairs={{0,8},{8,16},{16,24},{24,0},{1,9},{9,17},{17,25},{25,1},{2,10},{10... | collective-permute-start | bytes 884744 | tf_op jit(solution)/shard_map/ppermute | solution.py:653
  35.3 7.2 %collective-permute-start.17 = (f32[288,128]{1,0:T(8,128)S(1)}, f32[288,128]{1,0:T(8,128)S(1)}, u32[]{:S(2)}, u32[]{:S(2)}) collective-permute-start(f32[288,128]{1,0:T(8,128)S(1)} %get-tuple-element.140), channel_id=1, source_target_pairs={{0,2},{2,4},{4,6},{6,7},{7,5},{5,3},{3,1},{1,0},{8,10},{10,12},{12... | collective-permute-start | bytes 442376 | tf_op jit(solution)/shard_map/ppermute | solution.py:631
  37.3 6.7 %collective-permute-start.18 = (f32[288,128]{1,0:T(8,128)S(1)}, f32[288,128]{1,0:T(8,128)S(1)}, u32[]{:S(2)}, u32[]{:S(2)}) collective-permute-start(f32[288,128]{1,0:T(8,128)S(1)} %get-tuple-element.141), channel_id=1, source_target_pairs={{2,0},{4,2},{6,4},{7,6},{5,7},{3,5},{1,3},{0,1},{10,8},{12,10},{14... | collective-permute-start | bytes 442376 | tf_op jit(solution)/shard_map/ppermute | solution.py:631
  38.2 12.4 %collective-permute-start.21 = (f32[288,128]{1,0:T(8,128)S(1)}, f32[288,128]{1,0:T(8,128)S(1)}, u32[]{:S(2)}, u32[]{:S(2)}) collective-permute-start(f32[288,128]{1,0:T(8,128)S(1)} %get-tuple-element.151), channel_id=1, source_target_pairs={{2,0},{4,2},{6,4},{7,6},{5,7},{3,5},{1,3},{0,1},{10,8},{12,10},{14... | collective-permute-start | bytes 442376 | tf_op jit(solution)/shard_map/ppermute | solution.py:631
  39.8 10.8 %collective-permute-start.23 = (f32[288,128]{1,0:T(8,128)S(1)}, f32[288,128]{1,0:T(8,128)S(1)}, u32[]{:S(2)}, u32[]{:S(2)}) collective-permute-start(f32[288,128]{1,0:T(8,128)S(1)} %get-tuple-element.153), channel_id=1, source_target_pairs={{0,2},{2,4},{4,6},{6,7},{7,5},{5,3},{3,1},{1,0},{8,10},{10,12},{12... | collective-permute-start | bytes 442376 | tf_op jit(solution)/shard_map/ppermute | solution.py:631
  42.4 6.2 %collective-permute-start.19 = (f32[576,128]{1,0:T(8,128)S(1)}, f32[576,128]{1,0:T(8,128)S(1)}, u32[]{:S(2)}, u32[]{:S(2)}) collective-permute-start(f32[576,128]{1,0:T(8,128)S(1)} %get-tuple-element.143.refs_9_), channel_id=1, source_target_pairs={{0,8},{8,16},{16,24},{24,0},{1,9},{9,17},{17,25},{25,1},{2,10},{10... | collective-permute-start | bytes 884744 | tf_op jit(solution)/shard_map/ppermute | solution.py:653
  44.0 6.6 %collective-permute-start.20 = (f32[288,128]{1,0:T(8,128)S(1)}, f32[288,128]{1,0:T(8,128)S(1)}, u32[]{:S(2)}, u32[]{:S(2)}) collective-permute-start(f32[288,128]{1,0:T(8,128)S(1)} %get-tuple-element.150), channel_id=1, source_target_pairs={{0,2},{2,4},{4,6},{6,7},{7,5},{5,3},{3,1},{1,0},{8,10},{10,12},{12... | collective-permute-start | bytes 442376 | tf_op jit(solution)/shard_map/ppermute | solution.py:631
  45.6 5.1 %collective-permute-start.22 = (f32[288,128]{1,0:T(8,128)S(1)}, f32[288,128]{1,0:T(8,128)S(1)}, u32[]{:S(2)}, u32[]{:S(2)}) collective-permute-start(f32[288,128]{1,0:T(8,128)S(1)} %get-tuple-element.152), channel_id=1, source_target_pairs={{2,0},{4,2},{6,4},{7,6},{5,7},{3,5},{1,3},{0,1},{10,8},{12,10},{14... | collective-permute-start | bytes 442376 | tf_op jit(solution)/shard_map/ppermute | solution.py:631
  (14 other events, 56.7 us)
